TPU v7x, 32 devices: a whole 2x2x4 slice. The times are simulated.
32 devices in a mesh: member: 2 (over core), comp: 2 (over y), tile: 8 (over z, x).
Axes of the slice: x: 2, y: 2, z: 4, core: 2. Of those that a mesh axis runs over, the one named last changes fastest.
Arguments:
- member_state: float32 [4, 2, 4, 4, 384, 768], P('member', 'comp', None, None, 'tile'), may hold values from -6 to 6
- layer_blend_operator: float32 [2, 4, 4], P('comp'), may hold values from -3 to 3
- coefficient: float32 [2, 4], P('comp'), may hold values from 0.05 to 0.24
- interpolation_donor_meridians: int32 [2, 384, 768], P('comp', 'tile'), may hold values from 0 to 767, as said below
- land_sea: int32 [384, 768], P('tile'), may hold values 0 or 1
- ancestry: int32 [4], replicated, may hold values from 0 to 3, as said below
Outputs:
- cloned: float32 [4, 2, 4, 4, 384, 768], P('member', 'comp', None, None, 'tile')
- region_score: float32 [4, 2], P('member', 'comp')
Inputs may be any that keep to these rules, and one draw needn't show every extreme that they name: interpolation_donor_meridians[c, j, x] is a longitude from one cell west to four cells east of x, cyclically. `ancestry`: slot 0 has a parent among slots 2 and above, slot 2 one below 2.
All inputs are finite; a program needn't handle non-finite values. No bound on the sum of `land_sea` on one device may be relied on, other than what follows from the above.
Results may differ from a plain program's by a relative error of at most 0.00014.
Values sent between devices are 32-bit elements; how exact they have to be, the bound alone decides.
A program may use at most 128 MiB of HBM per device.

v0:
```python
import functools
import math

import jax
import jax.numpy as jnp
import numpy as np
from jax import lax
from jax.experimental import pallas as pl
from jax.experimental.pallas import tpu as pltpu
from jax.sharding import PartitionSpec as P

LAT = 384
MODES = 256
STEPS = 2
MESH = pl.DeviceIdType.MESH


coupling_rate = 0.5
forcing_rate = 0.5
precise = lax.Precision.HIGH


def partner_2(value, axis, distance):
    mask = 2**distance
    pairs = [(source, source ^ mask) for source in range(lax.axis_size(axis))]
    return lax.ppermute(value, axis, pairs)


def padded_2(block, sides, width):
    for axis, dim in sides:
        count = lax.axis_size(axis)
        forward = [(i, i + 1) for i in range(count - 1)]
        backward = [(target, source) for source, target in forward]
        low = lax.ppermute(
            lax.slice_in_dim(block, block.shape[dim] - width, None, axis=dim), axis, forward
        )
        high = lax.ppermute(lax.slice_in_dim(block, 0, width, axis=dim), axis, backward)
        block = jnp.concatenate([low, block, high], axis=dim)
    return block


def kept_lon_basis(lon_count):
    wave = np.arange(2 * MODES)
    is_cosine = wave < MODES
    number = np.where(is_cosine, wave, wave - MODES + 1).astype(np.float32)
    cells = np.arange(lon_count).astype(np.float32)
    angle = np.float32(2.0 * math.pi) * number[:, None] * cells[None, :] / np.float32(lon_count)
    scale = np.where(number == 0.0, math.sqrt(1.0 / lon_count), math.sqrt(2.0 / lon_count)).astype(
        np.float32
    )
    table = np.where(is_cosine[:, None], np.cos(angle), np.sin(angle)) * scale[:, None]
    return table.astype(np.float32), number


def lat_table():
    order = np.arange(MODES).astype(np.float32)
    cells = np.arange(LAT).astype(np.float32)
    scale = np.where(order == 0.0, math.sqrt(1.0 / LAT), math.sqrt(2.0 / LAT)).astype(np.float32)
    angle = np.float32(math.pi) * (cells[None, :] + np.float32(0.5)) * order[:, None]
    return (np.cos(angle / np.float32(LAT)) * scale[:, None]).astype(np.float32)


def row_weights():
    rows = np.arange(LAT).astype(np.float32)
    return np.cos(
        np.float32(math.pi) * ((rows + np.float32(0.5)) / np.float32(LAT) - np.float32(0.5))
    ).astype(np.float32)


def donor_lookup(partner, donors):
    lon_count = partner.shape[-1]
    cells = jnp.arange(lon_count, dtype=jnp.int32)[None, :]
    offsets = jnp.mod(donors - cells, lon_count)
    result = jnp.zeros_like(partner)
    for shift_by in (-1, 0, 1, 2, 3, 4):
        moved = jnp.roll(partner, -shift_by, axis=-1)
        result = result + jnp.where(offsets == shift_by % lon_count, moved, 0.0)
    return result


def remote(src, dst, send_sem, recv_sem, device):
    return pltpu.make_async_remote_copy(
        src_ref=src,
        dst_ref=dst,
        send_sem=send_sem,
        recv_sem=recv_sem,
        device_id=device,
        device_id_type=MESH,
    )


def here():
    return lax.axis_index("member"), lax.axis_index("comp"), lax.axis_index("tile")


def greet(targets, count):
    barrier = pltpu.get_barrier_semaphore()
    for condition, device in targets:

        @pl.when(condition)
        def _():
            pl.semaphore_signal(barrier, inc=1, device_id=device, device_id_type=MESH)

    @pl.when(count > 0)
    def _():
        pl.semaphore_wait(barrier, count)


def differs(a, b):
    return jnp.logical_or(a[0] != b[0], jnp.logical_or(a[1] != b[1], a[2] != b[2]))


def spread_kernel(
    sizes, c_ref, r_ref, u_ref, ru_ref, h_ref, send, hsend, hrecv, rsend, recv, rrecv, loc
):
    members, comps, fields, tiles, rows = sizes
    me = m, y, t = here()
    per = c_ref.shape[2] // members
    unit_m, unit_f = t // fields, t % fields
    has_surface = jnp.logical_and(m == 0, unit_f == 0)
    targets = [(y == 1, (m, 0, t))]
    for j in range(tiles):
        source = (unit_m, y, j)
        targets.append((differs(source, me), source))
    for j in range(tiles):
        source = (unit_m, 1, j)
        targets.append((jnp.logical_and(has_surface, differs(source, me)), source))
    self_unit = (unit_m == m).astype(jnp.int32)
    self_surface = jnp.logical_and(has_surface, unit_m == m).astype(jnp.int32)
    count = members * fields - self_unit + jnp.where(y == 0, 1, comps - self_surface)
    greet(targets, count)

    def rows_of(j):
        return pl.ds(pl.multiple_of(j * rows, 8), rows)

    pieces = [(f, c) for f in range(fields) for c in range(members)]

    def place(k):
        f, c = pieces[k]
        return lax.rem(f + t, fields), c

    def piece(k, ref):
        f, c = place(k)
        device = (c, y, m * fields + f)
        src = ref.at[f, pl.ds(c * per, per)]
        dst = u_ref.at[:, rows_of(t), :]
        copy = remote(src, dst, send.at[k], recv.at[t], device)
        return differs(device, me), copy, pltpu.make_async_copy(src, dst, loc.at[0])

    def hop(k):
        f, c = place(k)
        part = (f, pl.ds(c * per, per))
        return remote(
            c_ref.at[(1,) + part], h_ref.at[part], hsend.at[k], hrecv.at[k], (m, 1 - y, t)
        )

    def surface(s):
        device = (0, s, m * fields)
        dst = ru_ref.at[rows_of(t), :]
        copy = remote(r_ref.at[s], dst, rsend.at[s], rrecv.at[t], device)
        return differs(device, me), copy, pltpu.make_async_copy(r_ref.at[s], dst, loc.at[1])

    def begin(parts):
        away, copy, local = parts
        pl.when(away)(copy.start)
        pl.when(jnp.logical_not(away))(local.start)

    def end(parts):
        away, copy, local = parts
        pl.when(away)(copy.wait_send)
        pl.when(jnp.logical_not(away))(local.wait)

    @pl.when(y == 0)
    def _():
        for k in range(len(pieces)):
            hop(k).start()
            begin(piece(k, c_ref.at[0]))

    @pl.when(y == 1)
    def _():
        for s in range(comps):
            begin(surface(s))
        for k in range(len(pieces)):
            hop(k).wait_recv()
            begin(piece(k, h_ref))

    for j in range(tiles):
        away = differs((unit_m, y, j), me)
        part = u_ref.at[:, rows_of(j), :]
        arrival = remote(part, part, send.at[0], recv.at[j], me)
        pl.when(away)(arrival.wait_recv)
        late = remote(
            ru_ref.at[rows_of(j), :], ru_ref.at[rows_of(j), :], rsend.at[0], rrecv.at[j], me
        )
        away = jnp.logical_and(has_surface, differs((unit_m, 1, j), me))
        pl.when(away)(late.wait_recv)

    @pl.when(y == 0)
    def _():
        for k in range(len(pieces)):
            hop(k).wait_send()
            end(piece(k, c_ref.at[0]))

    @pl.when(y == 1)
    def _():
        for s in range(comps):
            end(surface(s))
        for k in range(len(pieces)):
            end(piece(k, h_ref))


def swap_kernel(sizes, x_ref, xo_ref, sa_ref, send, recv, ssend, srecv, loc):
    members, comps, fields, tiles, rows = sizes
    me = m, y, t = here()
    unit_m, unit_f = t // fields, t % fields
    has_surface = jnp.logical_and(m == 0, unit_f == 0)
    other = (1 - m, y, t)
    targets = [(m >= 0, other)]
    for s in range(comps):
        source = (0, s, m * fields)
        targets.append((jnp.logical_and(y == 1, differs(source, me)), source))
    own_surface = jnp.logical_and(has_surface, jnp.logical_and(y == 1, unit_m == m))
    count = 1 + jnp.where(has_surface, tiles - own_surface.astype(jnp.int32), 0)
    greet(targets, count)

    def surface(j):
        device = (unit_m, 1, j)
        part = x_ref.at[0, pl.ds(j * rows, rows), :]
        copy = remote(part, sa_ref.at[y], ssend.at[j], srecv.at[y], device)
        return device, copy, pltpu.make_async_copy(part, sa_ref.at[y], loc.at[0])

    @pl.when(has_surface)
    def _():
        for j in range(tiles):
            device, copy, local = surface(j)
            away = differs(device, me)
            pl.when(away)(copy.start)
            pl.when(jnp.logical_not(away))(local.start)

    across = remote(x_ref, xo_ref, send.at[0], recv.at[0], other)
    across.start()
    across.wait()

    @pl.when(has_surface)
    def _():
        for j in range(tiles):
            device, copy, local = surface(j)
            away = differs(device, me)
            pl.when(away)(copy.wait_send)
            pl.when(jnp.logical_not(away))(local.wait)

    for s in range(comps):
        away = jnp.logical_and(y == 1, differs((0, s, m * fields), me))
        arrival = remote(sa_ref.at[s], sa_ref.at[s], ssend.at[0], srecv.at[s], me)
        pl.when(away)(arrival.wait_recv)


def return_kernel(
    sizes, f_ref, p_ref, own_ref, far_ref, score_ref, send, recv, fsend, frecv, psend, precv, loc
):
    members, comps, fields, tiles, rows = sizes
    me = m, y, t = here()
    per = f_ref.shape[0]
    unit_m, unit_f = t // fields, t % fields
    has_surface = jnp.logical_and(m == 0, unit_f == 0)
    other = (1 - m, y, t)
    pieces = [(s, f, c) for s in range(comps) for f in range(fields) for c in range(members)]
    targets = [(y == 0, other)]
    for s, f, c in pieces:
        source = (c, s, m * fields + f)
        targets.append((jnp.logical_and(y == 0, differs(source, me)), source))
    own_unit = jnp.logical_and(y == 0, unit_m == m).astype(jnp.int32)
    greet(targets, tiles - own_unit + jnp.where(y == 0, 1, 0))

    def band(j):
        device = (unit_m, 0, j)
        src = f_ref.at[:, pl.ds(j * rows, rows), :]
        dst = own_ref.at[y, unit_f, pl.ds(m * per, per)]
        slot = (y * fields + unit_f) * members + m
        return (
            device,
            remote(src, dst, send.at[j], recv.at[slot], device),
            pltpu.make_async_copy(src, dst, loc.at[0]),
            remote(p_ref, score_ref.at[y], psend.at[j], precv.at[y], device),
            pltpu.make_async_copy(p_ref, score_ref.at[y], loc.at[1]),
        )

    for j in range(tiles):
        device, copy, local, point, local_point = band(j)
        away = differs(device, me)
        pl.when(away)(copy.start)
        pl.when(jnp.logical_not(away))(local.start)
        pl.when(jnp.logical_and(has_surface, away))(point.start)
        pl.when(jnp.logical_and(has_surface, jnp.logical_not(away)))(local_point.start)

    def forward(k):
        s, f, c = pieces[k]
        part = (s, f, pl.ds(c * per, per))
        return remote(own_ref.at[part], far_ref.at[part], fsend.at[k], frecv.at[k], other)

    @pl.when(y == 0)
    def _():
        for k, (s, f, c) in enumerate(pieces):
            part = own_ref.at[s, f, pl.ds(c * per, per)]
            away = differs((c, s, m * fields + f), me)
            arrival = remote(part, part, send.at[0], recv.at[k], me)
            pl.when(away)(arrival.wait_recv)
            own = pltpu.make_async_copy(part, part, loc.at[0])
            pl.when(jnp.logical_not(away))(own.wait)
            forward(k).start()
        for s in range(comps):
            away = differs((0, s, m * fields), me)
            arrival = remote(score_ref.at[s], score_ref.at[s], psend.at[0], precv.at[s], me)
            pl.when(away)(arrival.wait_recv)
            own = pltpu.make_async_copy(p_ref, score_ref.at[s], loc.at[1])
            pl.when(jnp.logical_not(away))(own.wait)
        for k in range(len(pieces)):
            forward(k).wait()

    for j in range(tiles):
        device, copy, local, point, local_point = band(j)
        away = differs(device, me)
        pl.when(away)(copy.wait_send)
        pl.when(jnp.logical_and(has_surface, away))(point.wait_send)


def ocean_kernel(sizes, o_ref, p_ref, far_ref, score_ref, send, recv, psend, precv, loc):
    members, comps, fields, tiles, rows = sizes
    me = m, y, t = here()
    other = (1 - m, y, t)
    targets = [(y == 1, other)]
    for j in range(tiles):
        targets.append((jnp.logical_and(y == 1, j != t), (m, y, j)))
    greet(targets, jnp.where(y == 1, tiles, 0))

    @pl.when(y == 1)
    def _():
        across = remote(o_ref, far_ref, send.at[0], recv.at[0], other)
        across.start()
        local = pltpu.make_async_copy(p_ref, score_ref.at[t], loc.at[0])
        local.start()

        def point(j):
            return remote(p_ref, score_ref.at[t], psend.at[j], precv.at[t], (m, y, j))

        for j in range(tiles):
            pl.when(j != t)(point(j).start)
        for j in range(tiles):
            arrival = remote(score_ref.at[j], score_ref.at[j], psend.at[0], precv.at[j], me)
            pl.when(j != t)(arrival.wait_recv)
            pl.when(j != t)(point(j).wait_send)
        local.wait()
        across.wait()


def call(kernel, collective_id, outs, sems, *args):
    return pl.pallas_call(
        kernel,
        out_shape=[jax.ShapeDtypeStruct(shape, jnp.float32) for shape in outs],
        in_specs=[pl.BlockSpec(memory_space=pl.ANY)] * len(args),
        out_specs=[pl.BlockSpec(memory_space=pl.ANY)] * len(outs),
        scratch_shapes=[pltpu.SemaphoreType.DMA((n,)) for n in sems],
        compiler_params=pltpu.CompilerParams(collective_id=collective_id, has_side_effects=True),
    )(*args)


def matmul(a, b):
    return jnp.dot(a, b, precision=precise, preferred_element_type=jnp.float32)


def split(value):
    high = value.astype(jnp.bfloat16)
    return high, (value - high.astype(jnp.float32)).astype(jnp.bfloat16)


def split_table(table):
    high = table.astype(jnp.bfloat16)
    low = (table - high.astype(np.float32)).astype(jnp.bfloat16)
    return jnp.asarray(high), jnp.asarray(low)


def dot3(value, high_ref, low_ref):
    high, low = split(value)
    total = jnp.dot(high, low_ref[...], preferred_element_type=jnp.float32)
    total = total + jnp.dot(low, high_ref[...], preferred_element_type=jnp.float32)
    return total + jnp.dot(high, high_ref[...], preferred_element_type=jnp.float32)


def lookup(surface, donors):
    lon_count = surface.shape[-1]
    offset = donors - lax.broadcasted_iota(jnp.int32, donors.shape, 1)
    offset = jnp.where(offset > lon_count // 2, offset - lon_count, offset)
    offset = jnp.where(offset < -(lon_count // 2), offset + lon_count, offset)
    result = surface
    for shift in (-1, 1, 2, 3, 4):
        moved = pltpu.roll(surface, (-shift) % lon_count, 1)
        result = jnp.where(offset == shift, moved, result)
    return result


def mixed_level(blend_ref, field_ref, u):
    levels = field_ref.shape[2]
    total = blend_ref[u, 0] * field_ref[0, 0, 0]
    for v in range(1, levels):
        total = total + blend_ref[u, v] * field_ref[0, 0, v]
    return forcing_rate * jnp.tanh(total)


def air_kernel(field_ref, partner_ref, donors_ref, blend_ref, high_ref, low_ref, out_ref, forced):
    levels, rows = field_ref.shape[2:4]
    for u in range(levels):
        forced[u * rows : (u + 1) * rows] = field_ref[0, 0, u] + mixed_level(blend_ref, field_ref, u)

    @pl.when(pl.program_id(1) == 0)
    def _():
        received = lookup(partner_ref[0], donors_ref[...])
        forced[:rows] += coupling_rate * (received - field_ref[0, 0, 0])

    out_ref[0, 0] = dot3(forced[...], high_ref, low_ref).reshape(out_ref.shape[2:])


def sea_kernel(
    field_ref,
    low_ref,
    high_ref,
    partner_ref,
    donors_ref,
    next_ref,
    land_ref,
    blend_ref,
    rate_ref,
    out_ref,
    look_ref,
):
    levels, rows, lon_count = field_ref.shape[2:]
    rate = rate_ref[pl.program_id(1)]
    sea = land_ref[...] == 1
    first = pl.program_id(1) == 0
    row = lax.broadcasted_iota(jnp.int32, (rows, lon_count), 0)
    for u in range(levels):
        value = field_ref[0, 0, u]
        forced = value + mixed_level(blend_ref, field_ref, u)
        north = jnp.where(row == 0, low_ref[0, 0, u], pltpu.roll(value, 1, 0))
        south = jnp.where(row == rows - 1, high_ref[0, 0, u], pltpu.roll(value, rows - 1, 0))
        laplacian = (
            south
            + north
            + pltpu.roll(value, 1, 1)
            + pltpu.roll(value, lon_count - 1, 1)
            - 4.0 * value
        )
        if u == 0:
            received = lookup(partner_ref[0], donors_ref[...])
            extra = coupling_rate * (received - value)
            forced = forced + jnp.where(first, extra, 0.0)
        out_ref[0, 0, u] = jnp.where(sea, forced + rate * laplacian, value)

    @pl.when(first)
    def _():
        look_ref[0] = lookup(out_ref[0, 0, 0], next_ref[...])


def whole_spec(array):
    zeros = (0,) * array.ndim
    return pl.BlockSpec(array.shape, lambda *_: zeros)


def scalar_spec():
    return pl.BlockSpec(memory_space=pltpu.SMEM)


def state_spec(shape):
    return pl.BlockSpec((1, 1) + tuple(shape[2:]), lambda s, f, *_: (s, f, 0, 0, 0))


def surface_spec(shape):
    return pl.BlockSpec((1,) + tuple(shape[1:]), lambda s, f, *_: (s, 0, 0))


large = pltpu.CompilerParams(vmem_limit_bytes=40 * 1024 * 1024)


def air_forward(field, partner, donors, blend, table):
    slots, fields, levels, rows, lon_count = field.shape
    high, low = split_table(table)
    shape = field.shape[:-1] + (table.shape[1],)
    return pl.pallas_call(
        air_kernel,
        grid=(slots, fields),
        out_shape=jax.ShapeDtypeStruct(shape, jnp.float32),
        in_specs=[
            state_spec(field.shape),
            surface_spec(partner.shape),
            whole_spec(donors),
            scalar_spec(),
            whole_spec(high),
            whole_spec(low),
        ],
        out_specs=state_spec(shape),
        scratch_shapes=[pltpu.VMEM((levels * rows, lon_count), jnp.float32)],
        compiler_params=large,
    )(field, partner, donors, blend, high, low)


def sea_step(field, low, high, partner, donors, following, land_sea, blend, rate):
    return pl.pallas_call(
        sea_kernel,
        grid=field.shape[:2],
        out_shape=[
            jax.ShapeDtypeStruct(field.shape, jnp.float32),
            jax.ShapeDtypeStruct(partner.shape, jnp.float32),
        ],
        in_specs=[
            state_spec(field.shape),
            state_spec(low.shape),
            state_spec(high.shape),
            surface_spec(partner.shape),
            whole_spec(donors),
            whole_spec(following),
            whole_spec(land_sea),
            scalar_spec(),
            scalar_spec(),
        ],
        out_specs=[state_spec(field.shape), surface_spec(partner.shape)],
        compiler_params=large,
    )(field, low, high, partner, donors, following, land_sea, blend, rate)


def air_last_kernel(inside_ref, near_ref, own_ref, far_ref, high_ref, low_ref, out_ref):
    near = near_ref[pl.program_id(0)] == 1
    levels, rows, waves = own_ref.shape[2:]
    coefs = jnp.where(near, own_ref[0, 0], far_ref[0, 0]).reshape(levels * rows, waves)
    out_ref[0, 0] = dot3(coefs, high_ref, low_ref).reshape(out_ref.shape[2:])


def sea_last_kernel(inside_ref, near_ref, own_ref, far_ref, out_ref):
    near = near_ref[pl.program_id(0)] == 1
    out_ref[0, 0] = jnp.where(near, own_ref[0, 0], far_ref[0, 0])


def resampled(kernel, inside, near, own, far, tables, lon_count):
    shape = own.shape[:-1] + (lon_count,)

    def parent(s, f, inside_ref, near_ref):
        return (inside_ref[s], f, 0, 0, 0)

    parent_spec = pl.BlockSpec((1, 1) + own.shape[2:], parent)
    return pl.pallas_call(
        kernel,
        grid_spec=pltpu.PrefetchScalarGridSpec(
            num_scalar_prefetch=2,
            grid=own.shape[:2],
            in_specs=[parent_spec, parent_spec] + [whole_spec(table) for table in tables],
            out_specs=state_spec(shape),
        ),
        out_shape=jax.ShapeDtypeStruct(shape, jnp.float32),
        compiler_params=large,
    )(inside, near, own, far, *tables)


def edges(field):
    count = lax.axis_size("tile")
    forward = [(i, i + 1) for i in range(count - 1)]
    backward = [(target, source) for source, target in forward]
    low = lax.ppermute(field[:, :, :, -1:], "tile", forward)
    high = lax.ppermute(field[:, :, :, :1], "tile", backward)
    return low, high


def by_units(
    member_state,
    layer_blend_operator,
    coefficient,
    interpolation_donor_meridians,
    land_sea,
    ancestry,
):
    member, component, tile = here()
    members, comps, tiles = (lax.axis_size(name) for name in ("member", "comp", "tile"))
    field = member_state[:, 0]
    slots, fields, levels, rows, lon_count = field.shape
    per = levels // members
    sizes = (members, comps, fields, tiles, rows)
    lon_basis, number = kept_lon_basis(lon_count)
    waves = lon_basis.shape[0]
    lon_forward = jnp.asarray(np.ascontiguousarray(lon_basis.T))
    lon_inverse = jnp.asarray(lon_basis)
    lat_basis = lat_table()
    lat_forward = jnp.asarray(lat_basis)
    lat_inverse = jnp.asarray(np.ascontiguousarray(lat_basis.T))
    weights = row_weights()
    weight_total = float(weights.sum())
    order = np.arange(MODES).astype(np.float32)
    squares = jnp.asarray(order[:, None] ** 2 + number[None, :] ** 2)

    is_air = component == 0
    small = jnp.concatenate([layer_blend_operator[0].reshape(-1), coefficient[0]])
    other_small = partner_2(small, "comp", 0)
    air_small = jnp.where(is_air, small, other_small)
    air_blend = air_small[: levels * levels].reshape(levels, levels)
    air_coefficient = air_small[levels * levels :]
    donors = interpolation_donor_meridians[0]
    other_donors = partner_2(donors, "comp", 0)
    partner = partner_2(field[:, 0, 0], "comp", 0)
    low, high = edges(field)

    blend = layer_blend_operator[0]
    rate = coefficient[0]

    def air_first(_):
        fourier = air_forward(field, partner, donors, blend, np.ascontiguousarray(lon_basis.T))
        return fourier, jnp.zeros((slots, rows, lon_count), jnp.float32), field

    def sea_first(_):
        new, looked = sea_step(
            field, low, high, partner, donors, other_donors, land_sea, blend, rate
        )
        return jnp.zeros((slots, fields, levels, rows, waves), jnp.float32), looked, new

    fourier, looked, ocean = lax.cond(is_air, air_first, sea_first, 0)
    low, high = edges(ocean)
    gathered, sst, _ = call(
        functools.partial(spread_kernel, sizes),
        0,
        [(per, LAT, waves), (LAT, lon_count), (fields, levels, rows, waves)],
        (members * fields,) * 3 + (comps, tiles, tiles, 2),
        fourier,
        looked,
    )
    unit_field = tile % fields
    unit_rate = lax.dynamic_index_in_dim(air_coefficient, unit_field, keepdims=False)
    gain = 1.0 / (1.0 + unit_rate * squares / (MODES * MODES))

    def filtered(level):
        return matmul(lat_inverse, matmul(lat_forward, level) * gain)

    coefs = jnp.concatenate([filtered(gathered[v]) for v in range(per)])
    state = matmul(coefs, lon_inverse).reshape(per, LAT, lon_count)
    other_state, flux = call(
        functools.partial(swap_kernel, sizes),
        1,
        [(per, LAT, lon_count), (slots, rows, lon_count)],
        (1, 1, tiles, comps, 1),
        state,
    )
    mine = lax.dynamic_slice_in_dim(air_blend, member * per, per)
    mine_own = lax.dynamic_slice_in_dim(mine, member * per, per, axis=1)
    mine_other = lax.dynamic_slice_in_dim(mine, (1 - member) * per, per, axis=1)
    has_surface = jnp.logical_and(member == 0, unit_field == 0)
    forced = []
    for u in range(per):
        mixing = mine_own[u, 0] * state[0] + mine_other[u, 0] * other_state[0]
        for v in range(1, per):
            mixing = mixing + mine_own[u, v] * state[v] + mine_other[u, v] * other_state[v]
        level = state[u] + forcing_rate * jnp.tanh(mixing)
        if u == 0:
            level = level + jnp.where(has_surface, coupling_rate * (sst - state[0]), 0.0)
        forced.append(level)
    fourier = matmul(jnp.concatenate(forced), lon_forward).reshape(per, LAT, waves)
    back = jnp.stack([filtered(fourier[v]) for v in range(per)])
    zonal_mean = back[0, :, 0] * lon_basis[0, 0]
    air_score = jnp.sum(zonal_mean * weights) / weight_total
    air_point = jnp.full((8, 128), air_score)
    own, far, air_scores = call(
        functools.partial(return_kernel, sizes),
        2,
        [(slots, fields, levels, rows, waves)] * 2 + [(slots, 8, 128)],
        (tiles, slots * fields * members, slots * fields * members)
        + (slots * fields * members, tiles, comps, 2),
        back,
        air_point,
    )

    def sea_second(_):
        new, _ = sea_step(ocean, low, high, flux, donors, donors, land_sea, blend, rate)
        my_weights = lax.dynamic_slice_in_dim(jnp.asarray(weights), tile * rows, rows)
        sums = jnp.sum(jnp.mean(new[:, 0, 0], axis=2) * my_weights, axis=1)
        return new, jnp.broadcast_to(jnp.pad(sums, (0, 8 - slots))[:, None], (8, 128))

    def air_second(_):
        return ocean, jnp.zeros((8, 128), jnp.float32)

    ocean, partial = lax.cond(is_air, air_second, sea_second, 0)
    far_ocean, sea_parts = call(
        functools.partial(ocean_kernel, sizes),
        3,
        [(slots, fields, levels, rows, lon_count), (tiles, 8, 128)],
        (1, 1, tiles, tiles, 1),
        ocean,
        partial,
    )
    parents = lax.dynamic_slice_in_dim(ancestry, member * slots, slots)

    inside = parents % slots
    near = (parents // slots == member).astype(jnp.int32)

    def air_last(_):
        grid = resampled(
            air_last_kernel, inside, near, own, far, split_table(lon_basis), lon_count
        )
        return grid.reshape(member_state.shape), air_scores[:, 0, :1]

    def sea_last(_):
        score = jnp.sum(sea_parts[:, :slots, :1], axis=0) / weight_total
        states = resampled(sea_last_kernel, inside, near, ocean, far_ocean, (), lon_count)
        return states.reshape(member_state.shape), score

    return lax.cond(is_air, air_last, sea_last, 0)


def by_bands(
    member_state,
    layer_blend_operator,
    coefficient,
    interpolation_donor_meridians,
    land_sea,
    ancestry,
):
    slot_count = member_state.shape[0]
    component = lax.axis_index("comp")
    tile_index = lax.axis_index("tile")
    tile_count = lax.axis_size("tile")
    row_count = member_state.shape[4]
    lon_count = member_state.shape[5]
    lon_table, number = kept_lon_basis(lon_count)
    lon_basis = jnp.asarray(lon_table)
    local_modes = lon_table.shape[0] // tile_count
    my_numbers = lax.dynamic_slice_in_dim(jnp.asarray(number), tile_index * local_modes, local_modes)
    lat_basis = jnp.asarray(lat_table())
    order = jnp.arange(MODES, dtype=jnp.int32).astype(jnp.float32)
    sea_cells = land_sea[None, None] == 1
    diffusivity = coefficient[0][:, None, None, None]
    weights = row_weights()
    my_weights = lax.dynamic_slice_in_dim(jnp.asarray(weights), tile_index * row_count, row_count)
    weight_total = float(weights.sum())
    stepped_list = []
    partial_list = []
    for slot in range(slot_count):
        field = member_state[slot, 0]
        for _ in range(STEPS):
            surface = field[0, 0]
            partner = partner_2(surface, "comp", 0)
            received = donor_lookup(partner, interpolation_donor_meridians[0])
            mixing = jnp.einsum("uv,fvjx->fujx", layer_blend_operator[0], field, precision=precise)
            forced = field + forcing_rate * jnp.tanh(mixing)
            forced = forced.at[0, 0].add(coupling_rate * (received - surface))
            spectral_gain = 1.0 / (
                1.0
                + coefficient[0][:, None, None]
                * (order[None, None, :] ** 2 + my_numbers[None, :, None] ** 2)
                / (MODES * MODES)
            )
            fourier = jnp.einsum("fvjx,qx->fvjq", forced, lon_basis, precision=precise)
            spectrum = jnp.einsum(
                "lj,fkjq->fkql",
                lat_basis,
                lax.all_to_all(fourier, "tile", split_axis=3, concat_axis=2, tiled=True),
                precision=precise,
            )
            spectrum = spectrum * spectral_gain[:, None]
            returned = jnp.einsum("lj,fkql->fkjq", lat_basis, spectrum, precision=precise)
            filtered = lax.all_to_all(returned, "tile", split_axis=2, concat_axis=3, tiled=True)
            block_atm = jnp.einsum("fvjq,qx->fvjx", filtered, lon_basis, precision=precise)
            padded = padded_2(field, (("tile", 2),), 1)
            laplacian = (
                padded[:, :, 2:]
                + padded[:, :, :-2]
                + jnp.roll(field, 1, axis=3)
                + jnp.roll(field, -1, axis=3)
                - 4.0 * field
            )
            new_ocn = jnp.where(sea_cells, forced + diffusivity * laplacian, field)
            field = jnp.where(component == 0, block_atm, new_ocn)
        stepped_list.append(field)
        partial_list.append(jnp.sum(jnp.mean(field[0, 0], axis=1) * my_weights))
    local_states = jnp.stack(stepped_list)
    region_sums = lax.psum(jnp.stack(partial_list), "tile")
    region_score = (region_sums / weight_total).reshape(slot_count, 1)
    member_index = lax.axis_index("member")
    my_parents = lax.dynamic_slice_in_dim(ancestry, member_index * slot_count, slot_count)
    gathered = lax.all_gather(local_states, "member", axis=0, tiled=True)
    chosen = jnp.take(gathered, my_parents, axis=0)
    return (chosen[:, None], region_score)


def local(member_state, *others):
    members, comps, tiles = (lax.axis_size(name) for name in ("member", "comp", "tile"))
    slots, _, fields, levels, rows, _ = member_state.shape
    fits = members == 2 and comps == 2 and slots == comps and tiles == members * fields
    if fits and levels % members == 0 and rows % 8 == 0:
        return by_units(member_state, *others)
    return by_bands(member_state, *others)


def solution(mesh):
    return jax.shard_map(
        local,
        mesh=mesh,
        in_specs=(
            P("member", "comp", None, None, "tile", None),
            P("comp", None, None),
            P("comp", None),
            P("comp", "tile", None),
            P("tile", None),
            P(),
        ),
        out_specs=(P("member", "comp", None, None, "tile", None), P("member", "comp")),
        check_vma=False,
    )
```

profile of v0, /device:TPU:5, one launch (start us, length us, event | category | flops | bytes accessed | tf_op | source)
XLA Modules:
  0.0 213.0 jit_solution(552456100630463450)
XLA Ops:
  0.7 4.9 %copy.61 = f32[2,1,4,4,48,768]{5,4,3,2,1,0:T(8,128)} copy(f32[2,1,4,4,48,768]{5,4,3,2,1,0:T(8,128)} %param.22) | data formatting | bytes 9437184
  5.6 0.1 reshape_squeeze.3
  5.7 0.1 pad_maximum_fusion.1
  5.8 0.0 collective-permute-start.6
  5.8 1.4 collective-permute-start.3
  7.2 1.5 fusion.28
  8.8 1.3 collective-permute-start.1
  10.1 4.0 %collective-permute-start = (f32[2,4,4,1,768]{4,3,2,1,0:T(1,128)S(1)}, f32[2,4,4,1,768]{4,3,2,1,0:T(1,128)S(1)}, u32[]{:S(2)}, u32[]{:S(2)}) collective-permute-start(f32[2,4,4,1,768]{4,3,2,1,0:T(1,128)S(1)} %get-tuple-element.220), channel_id=1, source_target_pairs={{0,1},{1,2},{2,3},{3,4},{4,5},{5,6},{6,7},{8,9},{9,10},{10,11},{11... | collective-permute-start | bytes 294920 | tf_op jit(solution)/shard_map/ppermute | solution.py:565
  14.1 1.0 slice_bitcast_fusion.1
  15.0 0.2 collective-permute-start.2
  15.2 0.1 compare_convert_fusion
  15.3 0.5 and_select_fusion.1
  15.8 0.1 broadcast_select_fusion
  15.9 0.1 slice.112
  16.0 0.1 fusion.29
  16.1 0.1 slice.108
  16.1 0.6 dynamic_slice.18
  16.7 0.7 fusion.30
  17.4 4.4 %collective-permute-done.2 = f32[2,48,768]{2,1,0:T(8,128)S(1)} collective-permute-done((f32[2,48,768]{2,1,0:T(8,128)S(1)}, f32[2,48,768]{2,1,0:T(8,128)S(1)}, u32[]{:S(2)}, u32[]{:S(2)}) %collective-permute-start.2) | collective-permute-done | bytes 294944 | tf_op jit(solution)/shard_map/ppermute | solution.py:26
  21.8 11.4 %conditional.3 = (f32[2,4,4,48,512]{4,3,2,1,0:T(8,128)S(1)}, f32[2,48,768]{2,1,0:T(8,128)}, f32[2,4,4,48,768]{4,3,2,1,0:T(8,128)}) conditional(s32[]{:T(128)} %convert_element_type.10, (f32[2,4,4,48,768]{4,3,2,1,0:T(8,128)}, f32[2,4,4,1,768]{4,3,2,1,0:T(1,128)S(1)}, f32[2,4,4,1,768]{4,3,2,1,0:T(1,128)S(1)}, f32[2,48,768]{2,1,0:T(8,128)S(1)}, ...), branch_computations={%region_0.1_spmd, %region_1.2_spmd.clone} | conditional | bytes 12582940 | solution.py:620
  21.8 2.3 %copy.60.field_ref = f32[2,4,4,48,768]{4,3,2,1,0:T(8,128)S(1)} copy(f32[2,4,4,48,768]{4,3,2,1,0:T(8,128)} %get-tuple-element.75) | data formatting | bytes 9437184 | tf_op jit(solution)/shard_map/cond
  24.2 8.6 %branch_0_fun.3 = (f32[2,4,4,48,768]{4,3,2,1,0:T(8,128)}, f32[2,48,768]{2,1,0:T(8,128)}) custom-call(f32[2,4,4,48,768]{4,3,2,1,0:T(8,128)S(1)} %copy.60.field_ref, f32[2,4,4,1,768]{4,3,2,1,0:T(1,128)S(1)} %get-tuple-element.76.low_ref, f32[2,4,4,1,768]{4,3,2,1,0:T(1,128)S(1)} %get-tuple-element.77.high_ref, f32[2,48,768]{2,1,0:T(8,128)S(1)} %get-tuple-element.78.partner_ref, ...), custom_call_target="tpu_custom_call" | custom-call | tf_op jit(solution)/shard_map/cond/branch_0_fun/pallas_call | solution.py:506
  32.8 0.4 broadcast.55
  33.2 52.7 %shard_map.181 = (f32[2,384,512]{2,1,0:T(8,128)}, f32[384,768]{1,0:T(8,128)}, f32[4,4,48,512]{3,2,1,0:T(8,128)}) custom-call(f32[2,4,4,48,512]{4,3,2,1,0:T(8,128)S(1)} %get-tuple-element.132.c_ref, f32[2,48,768]{2,1,0:T(8,128)} %get-tuple-element.133.r_ref), custom_call_target="tpu_custom_call" | custom-call | tf_op jit(solution)/shard_map/pallas_call | solution.py:357
  85.9 0.0 copy-start.20
  86.0 0.0 copy-start.22
  86.0 2.7 %convolution_multiply_fusion.2 = f32[256,512]{1,0:T(8,128)S(1)} fusion(f32[256,384]{1,0:T(8,128)} %constant.136.clone, f32[2,384,512]{2,1,0:T(8,128)} %get-tuple-element.134, f32[256,512]{1,0:T(8,128)} %constant.138.clone, f32[]{:T(128)} %bitcast.8), kind=kOutput, calls=%fused_computation.19 | convolution fusion | flops 302645248 | bytes 2228736 | tf_op jit(solution)/shard_map/dot_general | solution.py:368
  88.7 0.0 copy-start.6
  88.7 1.2 convolution_multiply_fusion.3
  89.9 0.5 fusion.32
  90.4 0.5 fusion.33
  90.9 0.4 copy-done.9
  91.3 3.5 %fusion.4 = f32[768,768]{1,0:T(8,128)} fusion(f32[512,768]{1,0:T(8,128)S(1)} %copy-done.9, f32[384,512]{1,0:T(8,128)S(1)} %fusion.33, f32[384,512]{1,0:T(8,128)S(1)} %fusion.32), kind=kOutput, calls=%fused_computation.10 | convolution fusion | flops 1812332544 | bytes 5505024 | tf_op jit(solution)/shard_map/dot_general | solution.py:368
  94.9 10.2 %shard_map.182 = (f32[2,384,768]{2,1,0:T(8,128)}, f32[2,48,768]{2,1,0:T(8,128)}) custom-call(f32[2,384,768]{2,1,0:T(8,128)} %bitcast.84), custom_call_target="tpu_custom_call" | custom-call | tf_op jit(solution)/shard_map/pallas_call | solution.py:357
  105.1 0.0 copy-start.8
  105.1 7.9 %fusion.15 = (f32[384,768]{1,0:T(8,128)S(1)}, f32[384,768]{1,0:T(8,128)S(1)}) fusion(f32[384,768]{1,0:T(8,128)} %get-tuple-element.141, f32[768,768]{1,0:T(8,128)S(1)} %copy-done.5, f32[2,384,768]{2,1,0:T(8,128)} %get-tuple-element.140, f32[]{:T(128)} %bitcast.15, f32[]{:T(128)} %bitcast.14, f32[]{:T(128)} %bitcast.12, f32[]{:T(128)} %bitcast.11, ...), kind=kLoop, calls=%fused_computation.31 | loop fusion | flops 6488064 | bytes 8257569 | tf_op jit(solution)/shard_map/add | solution.py:657
  113.0 0.0 copy-start.21
  113.0 0.0 copy-start.23
  113.0 2.0 fusion
  115.1 1.2 convolution_multiply_fusion
  116.3 1.2 convolution_multiply_fusion.1
  117.5 2.1 %fusion.27 = (f32[2,4,4,1,768]{4,3,2,1,0:T(1,128)}, f32[2,4,4,1,768]{4,3,2,1,0:T(1,128)S(1)}) fusion(f32[2,4,4,48,768]{4,3,2,1,0:T(8,128)} %get-tuple-element.204), kind=kLoop, calls=%fused_computation.55 | loop fusion | bytes 393216 | tf_op jit(solution)/shard_map/slice | solution.py:566
  119.6 1.3 collective-permute-start.5
  120.9 0.0 copy-start.13
  120.9 6.0 %collective-permute-start.4 = (f32[2,4,4,1,768]{4,3,2,1,0:T(1,128)S(1)}, f32[2,4,4,1,768]{4,3,2,1,0:T(1,128)}, u32[]{:S(2)}, u32[]{:S(2)}) collective-permute-start(f32[2,4,4,1,768]{4,3,2,1,0:T(1,128)S(1)} %get-tuple-element.218), channel_id=1, source_target_pairs={{0,1},{1,2},{2,3},{3,4},{4,5},{5,6},{6,7},{8,9},{9,10},{10,11},{11... | collective-permute-start | bytes 294920 | tf_op jit(solution)/shard_map/ppermute | solution.py:565
  126.9 0.5 convolution_bitcast_fusion.1
  127.4 0.5 convolution_bitcast_fusion
  127.9 0.7 fusion.24
  129.2 1.3 pad_maximum_fusion.f_ref
  130.5 0.6 broadcast_in_dim.15.p_ref
  131.1 40.1 %shard_map.184 = (f32[2,4,4,48,512]{4,3,2,1,0:T(8,128)S(1)}, f32[2,4,4,48,512]{4,3,2,1,0:T(8,128)}, f32[2,8,128]{2,1,0:T(8,128)S(1)}) custom-call(f32[2,384,512]{2,1,0:T(8,128)} %pad_maximum_fusion.f_ref, f32[8,128]{1,0:T(8,128)} %broadcast_in_dim.15.p_ref), custom_call_target="tpu_custom_call" | custom-call | tf_op jit(solution)/shard_map/pallas_call | solution.py:357
  171.2 13.2 %conditional.4 = (f32[2,4,4,48,768]{4,3,2,1,0:T(8,128)}, f32[8,128]{1,0:T(8,128)S(1)}) conditional(s32[]{:T(128)} %convert_element_type.10, (f32[2,4,4,48,768]{4,3,2,1,0:T(8,128)}, f32[2,4,4,1,768]{4,3,2,1,0:T(1,128)}, f32[2,4,4,1,768]{4,3,2,1,0:T(1,128)}, f32[2,48,768]{2,1,0:T(8,128)}, s32[48,768]{1,0:T(8,128)S(1)}, ...), branch_computations={%region_2.5_spmd.clone, %region_5.6_spmd} | conditional | flops 73874 | bytes 29791848 | solution.py:683
  171.2 2.4 %copy.62.field_ref = f32[2,4,4,48,768]{4,3,2,1,0:T(8,128)S(1)} copy(f32[2,4,4,48,768]{4,3,2,1,0:T(8,128)} %get-tuple-element.194) | data formatting | bytes 9437184 | tf_op jit(solution)/shard_map/cond
  173.6 8.6 %branch_0_fun.5 = (f32[2,4,4,48,768]{4,3,2,1,0:T(8,128)S(1)}, f32[2,48,768]{2,1,0:T(8,128)}) custom-call(f32[2,4,4,48,768]{4,3,2,1,0:T(8,128)S(1)} %copy.62.field_ref, f32[2,4,4,1,768]{4,3,2,1,0:T(1,128)} %get-tuple-element.195.low_ref, f32[2,4,4,1,768]{4,3,2,1,0:T(1,128)} %get-tuple-element.196.high_ref, f32[2,48,768]{2,1,0:T(8,128)S(1)} %copy-done.12, ...), custom_call_target="tpu_custom_call" | custom-call | tf_op jit(solution)/shard_map/cond/branch_0_fun/pallas_call | solution.py:506
  182.3 0.8 dynamic-slice_multiply_fusion
  183.0 0.1 slice_reduce_fusion.1
  183.1 0.1 multiply_reduce_fusion
  183.2 0.1 broadcast_in_dim.16
  183.3 1.1 copy-done.4
  184.4 19.4 %shard_map.183 = (f32[2,4,4,48,768]{4,3,2,1,0:T(8,128)}, f32[8,8,128]{2,1,0:T(8,128)S(1)}) custom-call(f32[2,4,4,48,768]{4,3,2,1,0:T(8,128)} %get-tuple-element.136.o_ref, f32[8,128]{1,0:T(8,128)S(1)} %get-tuple-element.137.p_ref), custom_call_target="tpu_custom_call" | custom-call | tf_op jit(solution)/shard_map/pallas_call | solution.py:357
  203.8 8.7 %conditional.5 = (f32[2,1,4,4,48,768]{5,4,3,2,0,1:T(8,128)}, f32[2,1]{0,1:T(1,128)S(1)}) conditional(s32[]{:T(128)} %convert_element_type.10, (s32[2]{0:T(128)S(1)}, s32[2]{0:T(128)S(1)}, f32[2,4,4,48,768]{4,3,2,1,0:T(8,128)}, f32[2,4,4,48,768]{4,3,2,1,0:T(8,128)}, f32[8,8,128]{2,1,0:T(8,128)S(1)}) %tuple.92, (s32[2]{0:T(128)S(1)}, ...), branch_computations={%region_7.9_spmd, %region_9.10_spmd.clone} | conditional | flops 16 | bytes 6307928 | solution.py:708
  203.8 8.5 %branch_0_fun.4 = f32[2,4,4,48,768]{4,3,2,1,0:T(8,128)} custom-call(s32[2]{0:T(128)S(1)} %get-tuple-element.103.inside_ref, s32[2]{0:T(128)S(1)} %get-tuple-element.104.near_ref, f32[2,4,4,48,768]{4,3,2,1,0:T(8,128)} %get-tuple-element.105.own_ref, f32[2,4,4,48,768]{4,3,2,1,0:T(8,128)} %get-tuple-element.106.far_ref), custom_call_target="tpu_custom_call" | custom-call | tf_op jit(solution)/shard_map/cond/branch_0_fun/pallas_call | solution.py:548
  212.4 0.1 slice_reduce_fusion
  212.5 0.5 copy-done.24
  (38 shorter events, 0.1 us)
Async XLA Ops:
  0.6 5.0 %copy-start.14 = (f32[1,4,4]{2,1,0:T(4,128)S(1)}, f32[1,4,4]{2,1,0:T(4,128)}, u32[]{:S(2)}) copy-start(f32[1,4,4]{2,1,0:T(4,128)} %param.23) | copy-start | bytes 196
  0.6 5.1 %copy-start.15 = (f32[1,4]{1,0:T(1,128)S(1)}, f32[1,4]{1,0:T(1,128)}, u32[]{:S(2)}) copy-start(f32[1,4]{1,0:T(1,128)} %param.24) | copy-start | bytes 52
  0.7 5.1 %copy-start.7 = (s32[1,48,768]{2,1,0:T(8,128)S(1)}, s32[1,48,768]{2,1,0:T(8,128)}, u32[]{:S(2)}) copy-start(s32[1,48,768]{2,1,0:T(8,128)} %param.25) | copy-start | bytes 442372
  0.7 21.2 %copy-start.11 = (s32[48,768]{1,0:T(8,128)S(1)}, s32[48,768]{1,0:T(8,128)}, u32[]{:S(2)}) copy-start(s32[48,768]{1,0:T(8,128)} %param.26) | copy-start | bytes 442372
  0.7 14.5 %copy-start.18 = (s32[4]{0:T(128)S(1)}, s32[4]{0:T(128)}, u32[]{:S(2)}) copy-start(s32[4]{0:T(128)} %param.27) | copy-start | bytes 52
  5.8 10.0 %collective-permute-start.6 = (f32[20]{0:T(128)S(1)}, f32[20]{0:T(128)S(1)}, u32[]{:S(2)}, u32[]{:S(2)}) collective-permute-start(f32[20]{0:T(128)S(1)} %pad_maximum_fusion.1), channel_id=1, source_target_pairs={{0,8},{8,0},{1,9},{9,1},{2,10},{10,2},{3,11},{11,3},{4,12},{12,4},... | collective-permute-start | bytes 248 | tf_op jit(solution)/shard_map/ppermute | solution.py:26
  5.8 16.0 %collective-permute-start.3 = (s32[48,768]{1,0:T(8,128)S(1)}, s32[48,768]{1,0:T(8,128)S(1)}, u32[]{:S(2)}, u32[]{:S(2)}) collective-permute-start(s32[48,768]{1,0:T(8,128)S(1)} %bitcast.85), channel_id=1, source_target_pairs={{0,8},{8,0},{1,9},{9,1},{2,10},{10,2},{3,11},{11,3},{4,12},{12,4},... | collective-permute-start | bytes 442376 | tf_op jit(solution)/shard_map/ppermute | solution.py:26
  8.8 13.1 %collective-permute-start.1 = (f32[2,4,4,1,768]{4,3,2,1,0:T(1,128)S(1)}, f32[2,4,4,1,768]{4,3,2,1,0:T(1,128)S(1)}, u32[]{:S(2)}, u32[]{:S(2)}) collective-permute-start(f32[2,4,4,1,768]{4,3,2,1,0:T(1,128)S(1)} %get-tuple-element.219), channel_id=1, source_target_pairs={{1,0},{2,1},{3,2},{4,3},{5,4},{6,5},{7,6},{9,8},{10,9},{11,10},{12... | collective-permute-start | bytes 294920 | tf_op jit(solution)/shard_map/ppermute | solution.py:566
  10.1 11.8 %collective-permute-start = (f32[2,4,4,1,768]{4,3,2,1,0:T(1,128)S(1)}, f32[2,4,4,1,768]{4,3,2,1,0:T(1,128)S(1)}, u32[]{:S(2)}, u32[]{:S(2)}) collective-permute-start(f32[2,4,4,1,768]{4,3,2,1,0:T(1,128)S(1)} %get-tuple-element.220), channel_id=1, source_target_pairs={{0,1},{1,2},{2,3},{3,4},{4,5},{5,6},{6,7},{8,9},{9,10},{10,11},{11... | collective-permute-start | bytes 294920 | tf_op jit(solution)/shard_map/ppermute | solution.py:565
  15.0 6.8 %collective-permute-start.2 = (f32[2,48,768]{2,1,0:T(8,128)S(1)}, f32[2,48,768]{2,1,0:T(8,128)S(1)}, u32[]{:S(2)}, u32[]{:S(2)}) collective-permute-start(f32[2,48,768]{2,1,0:T(8,128)S(1)} %slice_bitcast_fusion.1), channel_id=1, source_target_pairs={{0,8},{8,0},{1,9},{9,1},{2,10},{10,2},{3,11},{11,3},{4,12},{12,4},... | collective-permute-start | bytes 884744 | tf_op jit(solution)/shard_map/ppermute | solution.py:26
  85.9 2.7 %copy-start.19 = (f32[2,384,512]{2,1,0:T(8,128)S(1)}, f32[2,384,512]{2,1,0:T(8,128)}, u32[]{:S(2)}) copy-start(f32[2,384,512]{2,1,0:T(8,128)} %get-tuple-element.134) | copy-start | bytes 4718596
  85.9 2.7 %copy-start.20 = (f32[256,512]{1,0:T(8,128)S(1)}, f32[256,512]{1,0:T(8,128)}, u32[]{:S(2)}) copy-start(f32[256,512]{1,0:T(8,128)} %constant.138.clone) | copy-start | bytes 1572868
  86.0 2.7 %copy-start.22 = (f32[256,384]{1,0:T(8,128)S(1)}, f32[256,384]{1,0:T(8,128)}, u32[]{:S(2)}) copy-start(f32[256,384]{1,0:T(8,128)} %constant.136.clone) | copy-start | bytes 1179652
  88.7 1.2 copy-start.6
  89.9 1.4 copy-start.9
  94.9 10.2 %copy-start.5 = (f32[768,768]{1,0:T(8,128)S(1)}, f32[768,768]{1,0:T(8,128)}, u32[]{:S(2)}) copy-start(f32[768,768]{1,0:T(8,128)} %fusion.4) | copy-start | bytes 7077892
  105.1 7.9 %copy-start.8 = (f32[768,512]{1,0:T(8,128)S(1)}, f32[768,512]{1,0:T(8,128)}, u32[]{:S(2)}) copy-start(f32[768,512]{1,0:T(8,128)} %constant.134.clone) | copy-start | bytes 4718596
  113.0 2.1 copy-start.21
  113.0 2.1 copy-start.23
  119.6 51.6 %collective-permute-start.5 = (f32[2,4,4,1,768]{4,3,2,1,0:T(1,128)}, f32[2,4,4,1,768]{4,3,2,1,0:T(1,128)}, u32[]{:S(2)}, u32[]{:S(2)}) collective-permute-start(f32[2,4,4,1,768]{4,3,2,1,0:T(1,128)} %get-tuple-element.217), channel_id=1, source_target_pairs={{1,0},{2,1},{3,2},{4,3},{5,4},{6,5},{7,6},{9,8},{10,9},{11,10},{12... | collective-permute-start | bytes 294920 | tf_op jit(solution)/shard_map/ppermute | solution.py:566
  120.9 7.0 %copy-start.13 = (f32[1,384,1]{2,1,0:T(8,128)S(1)}, f32[1,384,1]{2,1,0:T(8,128)}, u32[]{:S(2)}) copy-start(f32[1,384,1]{2,1,0:T(8,128)} %constant.150) | copy-start | bytes 4612
  120.9 50.3 %collective-permute-start.4 = (f32[2,4,4,1,768]{4,3,2,1,0:T(1,128)S(1)}, f32[2,4,4,1,768]{4,3,2,1,0:T(1,128)}, u32[]{:S(2)}, u32[]{:S(2)}) collective-permute-start(f32[2,4,4,1,768]{4,3,2,1,0:T(1,128)S(1)} %get-tuple-element.218), channel_id=1, source_target_pairs={{0,1},{1,2},{2,3},{3,4},{4,5},{5,6},{6,7},{8,9},{9,10},{10,11},{11... | collective-permute-start | bytes 294920 | tf_op jit(solution)/shard_map/ppermute | solution.py:565
  171.2 2.4 %copy-start.12 = (f32[2,48,768]{2,1,0:T(8,128)S(1)}, f32[2,48,768]{2,1,0:T(8,128)}, u32[]{:S(2)}) copy-start(f32[2,48,768]{2,1,0:T(8,128)} %get-tuple-element.197.partner_ref) | copy-start | bytes 884740 | tf_op jit(solution)/shard_map/cond
  171.2 2.4 %copy-start.16 = (f32[4]{0:T(128)S(1)}, f32[4]{0:T(128)}, u32[]{:S(2)}) copy-start(f32[4]{0:T(128)} %get-tuple-element.201.rate_ref) | copy-start | bytes 52 | tf_op jit(solution)/shard_map/cond
  182.3 2.1 %copy-start.4 = (f32[2,4,4,48,768]{4,3,2,1,0:T(8,128)}, f32[2,4,4,48,768]{4,3,2,1,0:T(8,128)S(1)}, u32[]{:S(2)}) copy-start(f32[2,4,4,48,768]{4,3,2,1,0:T(8,128)S(1)} %get-tuple-element.241) | copy-start | bytes 14155780 | tf_op jit(solution)/shard_map/cond
  184.4 19.4 %copy-start.17 = (s32[2]{0:T(128)S(1)}, s32[2]{0:T(128)}, u32[]{:S(2)}) copy-start(s32[2]{0:T(128)} %and_select_fusion.1) | copy-start | bytes 28
  212.5 0.5 copy-start.24
where the time goes:
time: 214 us; the launch traced here: 213 us
  Pallas kernels  148 us (69%)
  local copies, waits for them, and re-layouts  19 us (9%)
  starting transfers between devices  14.2 us (7%)
  matrix products  13.8 us (6%)
  other arithmetic  11.7 us (5%)
  waiting for transfers between devices  4.45 us (2%)
    pallas_call x4, Pallas kernels, call(): pl.pallas_call(kernel, out_shape=[jax.ShapeDtypeStruct(shape, jnp.float32...  122 us
    pallas_call x2, Pallas kernels, sea_step(): pl.pallas_call(sea_kernel, grid=field.shape[:2], out_shape=[jax.ShapeDtyp...  17.3 us
    dot_general x10, matrix products, matmul(): return jnp.dot(a, b, precision=precise, preferred_element_type=jnp.float32)  13.8 us
    ppermute x2, starting transfers between devices, edges(): low = lax.ppermute(field[:, :, :, -1:], 'tile', forward)  10 us
    pallas_call x1, Pallas kernels, resampled(): pl.pallas_call(kernel, grid_spec=pltpu.PrefetchScalarGridSpec(num_scalar_...  8.52 us
    add x1, other arithmetic, by_units(): level + jnp.where(has_surface, coupling_rate * (sst - state[0]), 0.0)  7.91 us
    unnamed x35, local copies, waits for them, and re-layouts  5.92 us
    cond x8, local copies, waits for them, and re-layouts  5.82 us
  transfers between devices with their start and end apart: 7, of which 1 were waited for; matrix products, arithmetic and copies ran while one was open for 4% of the time, Pallas kernels for 19%

commit v1 on v0

--- a/solution.py
+++ b/solution.py
@@ -110,15 +110,85 @@
     return jnp.logical_or(a[0] != b[0], jnp.logical_or(a[1] != b[1], a[2] != b[2]))
 
 
+def shores(y, t, tiles):
+    return jnp.logical_and(y == 1, t > 0), jnp.logical_and(y == 1, t < tiles - 1)
+
+
+def edge_copies(edge_ref, low_ref, high_ref, esend, erecv, m, y, t):
+    up = remote(edge_ref.at[:, :, 0], high_ref, esend.at[0], erecv.at[0], (m, y, t - 1))
+    down = remote(edge_ref.at[:, :, 1], low_ref, esend.at[1], erecv.at[1], (m, y, t + 1))
+    return up, down
+
+
+def couple_kernel(
+    sizes,
+    field_ref,
+    donors_ref,
+    blend_ref,
+    rate_ref,
+    edge_ref,
+    partner_ref,
+    odonors_ref,
+    oblend_ref,
+    orate_ref,
+    low_ref,
+    high_ref,
+    send,
+    recv,
+    esend,
+    erecv,
+):
+    members, comps, fields, tiles, rows = sizes
+    m, y, t = here()
+    other = (m, 1 - y, t)
+    north, south = shores(y, t, tiles)
+    targets = [(m >= 0, other), (north, (m, y, t - 1)), (south, (m, y, t + 1))]
+    greet(targets, 1 + north.astype(jnp.int32) + south.astype(jnp.int32))
+    slots = partner_ref.shape[0]
+    pairs = [(field_ref.at[s, 0, 0], partner_ref.at[s]) for s in range(slots)]
+    pairs += [(donors_ref, odonors_ref), (blend_ref, oblend_ref), (rate_ref, orate_ref)]
+    copies = [remote(a, b, send.at[k], recv.at[k], other) for k, (a, b) in enumerate(pairs)]
+    up, down = edge_copies(edge_ref, low_ref, high_ref, esend, erecv, m, y, t)
+    for copy in copies:
+        copy.start()
+    pl.when(north)(up.start)
+    pl.when(south)(down.start)
+    for copy in copies:
+        copy.wait()
+    pl.when(north)(up.wait_send)
+    pl.when(south)(down.wait_send)
+    pl.when(south)(up.wait_recv)
+    pl.when(north)(down.wait_recv)
+
+
 def spread_kernel(
-    sizes, c_ref, r_ref, u_ref, ru_ref, h_ref, send, hsend, hrecv, rsend, recv, rrecv, loc
+    sizes,
+    c_ref,
+    r_ref,
+    edge_ref,
+    u_ref,
+    ru_ref,
+    h_ref,
+    low_ref,
+    high_ref,
+    send,
+    hsend,
+    hrecv,
+    rsend,
+    recv,
+    rrecv,
+    loc,
+    esend,
+    erecv,
 ):
     members, comps, fields, tiles, rows = sizes
     me = m, y, t = here()
     per = c_ref.shape[2] // members
     unit_m, unit_f = t // fields, t % fields
     has_surface = jnp.logical_and(m == 0, unit_f == 0)
-    targets = [(y == 1, (m, 0, t))]
+    north, south = shores(y, t, tiles)
+    targets = [(y == 1, (m, 0, t)), (north, (m, y, t - 1)), (south, (m, y, t + 1))]
+    up, down = edge_copies(edge_ref, low_ref, high_ref, esend, erecv, m, y, t)
     for j in range(tiles):
         source = (unit_m, y, j)
         targets.append((differs(source, me), source))
@@ -128,7 +198,9 @@
     self_unit = (unit_m == m).astype(jnp.int32)
     self_surface = jnp.logical_and(has_surface, unit_m == m).astype(jnp.int32)
     count = members * fields - self_unit + jnp.where(y == 0, 1, comps - self_surface)
-    greet(targets, count)
+    greet(targets, count + north.astype(jnp.int32) + south.astype(jnp.int32))
+    pl.when(north)(up.start)
+    pl.when(south)(down.start)
 
     def rows_of(j):
         return pl.ds(pl.multiple_of(j * rows, 8), rows)
@@ -207,6 +279,11 @@
             end(surface(s))
         for k in range(len(pieces)):
             end(piece(k, h_ref))
+
+    pl.when(north)(up.wait_send)
+    pl.when(south)(down.wait_send)
+    pl.when(south)(up.wait_recv)
+    pl.when(north)(down.wait_recv)
 
 
 def swap_kernel(sizes, x_ref, xo_ref, sa_ref, send, recv, ssend, srecv, loc):
@@ -256,7 +333,27 @@
 
 
 def return_kernel(
-    sizes, f_ref, p_ref, own_ref, far_ref, score_ref, send, recv, fsend, frecv, psend, precv, loc
+    sizes,
+    f_ref,
+    p_ref,
+    o_ref,
+    q_ref,
+    own_ref,
+    far_ref,
+    score_ref,
+    faro_ref,
+    part_ref,
+    send,
+    recv,
+    fsend,
+    frecv,
+    psend,
+    precv,
+    loc,
+    osend,
+    orecv,
+    qsend,
+    qrecv,
 ):
     members, comps, fields, tiles, rows = sizes
     me = m, y, t = here()
@@ -265,12 +362,19 @@
     has_surface = jnp.logical_and(m == 0, unit_f == 0)
     other = (1 - m, y, t)
     pieces = [(s, f, c) for s in range(comps) for f in range(fields) for c in range(members)]
-    targets = [(y == 0, other)]
+    targets = [(m >= 0, other)]
+    for j in range(tiles):
+        targets.append((jnp.logical_and(y == 1, j != t), (m, y, j)))
     for s, f, c in pieces:
         source = (c, s, m * fields + f)
         targets.append((jnp.logical_and(y == 0, differs(source, me)), source))
     own_unit = jnp.logical_and(y == 0, unit_m == m).astype(jnp.int32)
-    greet(targets, tiles - own_unit + jnp.where(y == 0, 1, 0))
+    greet(targets, tiles - own_unit + jnp.where(y == 0, 1, tiles))
+    across = remote(o_ref, faro_ref, osend.at[0], orecv.at[0], other)
+    keep = pltpu.make_async_copy(q_ref, part_ref.at[t], loc.at[2])
+
+    def share(j):
+        return remote(q_ref, part_ref.at[t], qsend.at[j], qrecv.at[t], (m, y, j))
 
     def band(j):
         device = (unit_m, 0, j)
@@ -292,6 +396,13 @@
         pl.when(jnp.logical_not(away))(local.start)
         pl.when(jnp.logical_and(has_surface, away))(point.start)
         pl.when(jnp.logical_and(has_surface, jnp.logical_not(away)))(local_point.start)
+
+    @pl.when(y == 1)
+    def _():
+        across.start()
+        keep.start()
+        for j in range(tiles):
+            pl.when(j != t)(share(j).start)
 
     def forward(k):
         s, f, c = pieces[k]
@@ -323,40 +434,25 @@
         pl.when(away)(copy.wait_send)
         pl.when(jnp.logical_and(has_surface, away))(point.wait_send)
 
-
-def ocean_kernel(sizes, o_ref, p_ref, far_ref, score_ref, send, recv, psend, precv, loc):
-    members, comps, fields, tiles, rows = sizes
-    me = m, y, t = here()
-    other = (1 - m, y, t)
-    targets = [(y == 1, other)]
-    for j in range(tiles):
-        targets.append((jnp.logical_and(y == 1, j != t), (m, y, j)))
-    greet(targets, jnp.where(y == 1, tiles, 0))
-
     @pl.when(y == 1)
     def _():
-        across = remote(o_ref, far_ref, send.at[0], recv.at[0], other)
-        across.start()
-        local = pltpu.make_async_copy(p_ref, score_ref.at[t], loc.at[0])
-        local.start()
-
-        def point(j):
-            return remote(p_ref, score_ref.at[t], psend.at[j], precv.at[t], (m, y, j))
-
+        keep.wait()
         for j in range(tiles):
-            pl.when(j != t)(point(j).start)
-        for j in range(tiles):
-            arrival = remote(score_ref.at[j], score_ref.at[j], psend.at[0], precv.at[j], me)
+            arrival = remote(part_ref.at[j], part_ref.at[j], qsend.at[0], qrecv.at[j], me)
             pl.when(j != t)(arrival.wait_recv)
-            pl.when(j != t)(point(j).wait_send)
-        local.wait()
+            pl.when(j != t)(share(j).wait_send)
         across.wait()
 
 
 def call(kernel, collective_id, outs, sems, *args):
     return pl.pallas_call(
         kernel,
-        out_shape=[jax.ShapeDtypeStruct(shape, jnp.float32) for shape in outs],
+        out_shape=[
+            jax.ShapeDtypeStruct(out.shape, out.dtype)
+            if hasattr(out, "dtype")
+            else jax.ShapeDtypeStruct(out, jnp.float32)
+            for out in outs
+        ],
         in_specs=[pl.BlockSpec(memory_space=pl.ANY)] * len(args),
         out_specs=[pl.BlockSpec(memory_space=pl.ANY)] * len(outs),
         scratch_shapes=[pltpu.SemaphoreType.DMA((n,)) for n in sems],
@@ -427,10 +523,13 @@
     donors_ref,
     next_ref,
     land_ref,
+    weight_ref,
     blend_ref,
     rate_ref,
     out_ref,
     look_ref,
+    edge_ref,
+    sum_ref,
 ):
     levels, rows, lon_count = field_ref.shape[2:]
     rate = rate_ref[pl.program_id(1)]
@@ -440,8 +539,8 @@
     for u in range(levels):
         value = field_ref[0, 0, u]
         forced = value + mixed_level(blend_ref, field_ref, u)
-        north = jnp.where(row == 0, low_ref[0, 0, u], pltpu.roll(value, 1, 0))
-        south = jnp.where(row == rows - 1, high_ref[0, 0, u], pltpu.roll(value, rows - 1, 0))
+        north = jnp.where(row == 0, low_ref[0, 0, u : u + 1], pltpu.roll(value, 1, 0))
+        south = jnp.where(row == rows - 1, high_ref[0, 0, u : u + 1], pltpu.roll(value, rows - 1, 0))
         laplacian = (
             south
             + north
@@ -453,11 +552,17 @@
             received = lookup(partner_ref[0], donors_ref[...])
             extra = coupling_rate * (received - value)
             forced = forced + jnp.where(first, extra, 0.0)
-        out_ref[0, 0, u] = jnp.where(sea, forced + rate * laplacian, value)
+        result = jnp.where(sea, forced + rate * laplacian, value)
+        out_ref[0, 0, u] = result
+        edge_ref[0, 0, 0, u : u + 1] = result[:1]
+        edge_ref[0, 0, 1, u : u + 1] = result[rows - 1 :]
 
     @pl.when(first)
     def _():
         look_ref[0] = lookup(out_ref[0, 0, 0], next_ref[...])
+        total = jnp.sum(out_ref[0, 0, 0] * weight_ref[...], axis=0, keepdims=True)
+        total = jnp.sum(total, axis=1, keepdims=True) / lon_count
+        sum_ref[0] = jnp.broadcast_to(total, sum_ref.shape[1:])
 
 
 def whole_spec(array):
@@ -470,7 +575,8 @@
 
 
 def state_spec(shape):
-    return pl.BlockSpec((1, 1) + tuple(shape[2:]), lambda s, f, *_: (s, f, 0, 0, 0))
+    zeros = (0,) * (len(shape) - 2)
+    return pl.BlockSpec((1, 1) + tuple(shape[2:]), lambda s, f, *_: (s, f) + zeros)
 
 
 def surface_spec(shape):
@@ -502,13 +608,17 @@
     )(field, partner, donors, blend, high, low)
 
 
-def sea_step(field, low, high, partner, donors, following, land_sea, blend, rate):
+def sea_step(field, low, high, partner, donors, following, land_sea, weights, blend, rate):
+    slots, fields, levels, rows, lon_count = field.shape
+    edge = (slots, fields, 2, levels, lon_count)
     return pl.pallas_call(
         sea_kernel,
         grid=field.shape[:2],
         out_shape=[
             jax.ShapeDtypeStruct(field.shape, jnp.float32),
             jax.ShapeDtypeStruct(partner.shape, jnp.float32),
+            jax.ShapeDtypeStruct(edge, jnp.float32),
+            jax.ShapeDtypeStruct((slots, 8, 128), jnp.float32),
         ],
         in_specs=[
             state_spec(field.shape),
@@ -518,12 +628,18 @@
             whole_spec(donors),
             whole_spec(following),
             whole_spec(land_sea),
+            whole_spec(weights),
             scalar_spec(),
             scalar_spec(),
         ],
-        out_specs=[state_spec(field.shape), surface_spec(partner.shape)],
+        out_specs=[
+            state_spec(field.shape),
+            surface_spec(partner.shape),
+            state_spec(edge),
+            surface_spec((slots, 8, 128)),
+        ],
         compiler_params=large,
-    )(field, low, high, partner, donors, following, land_sea, blend, rate)
+    )(field, low, high, partner, donors, following, land_sea, weights, blend, rate)
 
 
 def air_last_kernel(inside_ref, near_ref, own_ref, far_ref, high_ref, low_ref, out_ref):
@@ -558,13 +674,99 @@
     )(inside, near, own, far, *tables)
 
 
-def edges(field):
-    count = lax.axis_size("tile")
-    forward = [(i, i + 1) for i in range(count - 1)]
-    backward = [(target, source) for source, target in forward]
-    low = lax.ppermute(field[:, :, :, -1:], "tile", forward)
-    high = lax.ppermute(field[:, :, :, :1], "tile", backward)
-    return low, high
+def left3(high_ref, low_ref, value):
+    high, low = split(value)
+    total = jnp.dot(low_ref[...], high, preferred_element_type=jnp.float32)
+    total = total + jnp.dot(high_ref[...], low, preferred_element_type=jnp.float32)
+    return total + jnp.dot(high_ref[...], high, preferred_element_type=jnp.float32)
+
+
+def filtered(value, squares_ref, rate_ref, forward, inverse):
+    spectrum = left3(*forward, value) / (1.0 + rate_ref[0] * squares_ref[...])
+    return left3(*inverse, spectrum)
+
+
+def to_grid_kernel(x_ref, sq_ref, rate_ref, fh, fl, ih, il, gh, gl, out_ref):
+    coefs = filtered(x_ref[0], sq_ref, rate_ref, (fh, fl), (ih, il))
+    out_ref[0] = dot3(coefs, gh, gl)
+
+
+def to_coefs_kernel(
+    x_ref,
+    o_ref,
+    sst_ref,
+    here_ref,
+    there_ref,
+    flag_ref,
+    w_ref,
+    sq_ref,
+    rate_ref,
+    fh,
+    fl,
+    ih,
+    il,
+    gh,
+    gl,
+    out_ref,
+    sum_ref,
+    forced,
+):
+    per = x_ref.shape[0]
+    u = pl.program_id(0)
+    mixing = here_ref[u, 0] * x_ref[0] + there_ref[u, 0] * o_ref[0]
+    for v in range(1, per):
+        mixing = mixing + here_ref[u, v] * x_ref[v] + there_ref[u, v] * o_ref[v]
+    forced[...] = x_ref[u] + forcing_rate * jnp.tanh(mixing)
+
+    @pl.when(jnp.logical_and(u == 0, flag_ref[0] == 1))
+    def _():
+        forced[...] += coupling_rate * (sst_ref[...] - x_ref[0])
+
+    coefs = dot3(forced[...], gh, gl)
+    result = filtered(coefs, sq_ref, rate_ref, (fh, fl), (ih, il))
+    out_ref[0] = result
+
+    @pl.when(u == 0)
+    def _():
+        total = jnp.sum(result[:, : w_ref.shape[1]] * w_ref[...], axis=0, keepdims=True)
+        total = jnp.sum(total, axis=1, keepdims=True)
+        sum_ref[...] = jnp.broadcast_to(total, sum_ref.shape)
+
+
+def level_spec(shape):
+    return pl.BlockSpec((1,) + tuple(shape[1:]), lambda u: (u, 0, 0))
+
+
+def to_grid(value, squares, rate, tables, lon_count):
+    shape = value.shape[:2] + (lon_count,)
+    return pl.pallas_call(
+        to_grid_kernel,
+        grid=value.shape[:1],
+        out_shape=jax.ShapeDtypeStruct(shape, jnp.float32),
+        in_specs=[level_spec(value.shape), whole_spec(squares), scalar_spec()]
+        + [whole_spec(table) for table in tables],
+        out_specs=level_spec(shape),
+        compiler_params=large,
+    )(value, squares, rate, *tables)
+
+
+def to_coefs(state, other, sst, mine, theirs, flag, weights, squares, rate, tables):
+    shape = state.shape[:2] + (squares.shape[1],)
+    return pl.pallas_call(
+        to_coefs_kernel,
+        grid=state.shape[:1],
+        out_shape=[
+            jax.ShapeDtypeStruct(shape, jnp.float32),
+            jax.ShapeDtypeStruct((8, 128), jnp.float32),
+        ],
+        in_specs=[whole_spec(state), whole_spec(other), whole_spec(sst)]
+        + [scalar_spec()] * 3
+        + [whole_spec(weights), whole_spec(squares), scalar_spec()]
+        + [whole_spec(table) for table in tables],
+        out_specs=[level_spec(shape), pl.BlockSpec((8, 128), lambda u: (0, 0))],
+        scratch_shapes=[pltpu.VMEM(state.shape[1:], jnp.float32)],
+        compiler_params=large,
+    )(state, other, sst, mine, theirs, flag, weights, squares, rate, *tables)
 
 
 def by_units(
@@ -583,59 +785,75 @@
     sizes = (members, comps, fields, tiles, rows)
     lon_basis, number = kept_lon_basis(lon_count)
     waves = lon_basis.shape[0]
-    lon_forward = jnp.asarray(np.ascontiguousarray(lon_basis.T))
-    lon_inverse = jnp.asarray(lon_basis)
+    lon_columns = np.ascontiguousarray(lon_basis.T)
     lat_basis = lat_table()
-    lat_forward = jnp.asarray(lat_basis)
-    lat_inverse = jnp.asarray(np.ascontiguousarray(lat_basis.T))
+    lat_tables = split_table(lat_basis) + split_table(np.ascontiguousarray(lat_basis.T))
     weights = row_weights()
     weight_total = float(weights.sum())
     order = np.arange(MODES).astype(np.float32)
-    squares = jnp.asarray(order[:, None] ** 2 + number[None, :] ** 2)
+    squares = order[:, None] ** 2 + number[None, :] ** 2
+    squares = jnp.asarray((squares / np.float32(MODES * MODES)).astype(np.float32))
+    air_weights = np.zeros((LAT, 128), np.float32)
+    air_weights[:, 0] = weights * lon_basis[0, 0] / weight_total
+    my_weights = lax.dynamic_slice_in_dim(jnp.asarray(weights[:, None]), tile * rows, rows)
 
     is_air = component == 0
-    small = jnp.concatenate([layer_blend_operator[0].reshape(-1), coefficient[0]])
-    other_small = partner_2(small, "comp", 0)
-    air_small = jnp.where(is_air, small, other_small)
-    air_blend = air_small[: levels * levels].reshape(levels, levels)
-    air_coefficient = air_small[levels * levels :]
-    donors = interpolation_donor_meridians[0]
-    other_donors = partner_2(donors, "comp", 0)
-    partner = partner_2(field[:, 0, 0], "comp", 0)
-    low, high = edges(field)
-
     blend = layer_blend_operator[0]
     rate = coefficient[0]
+    donors = interpolation_donor_meridians[0]
+    edge_shape = (slots, fields, 2, levels, lon_count)
+    halo_shape = (slots, fields, levels, lon_count)
+    edge = jnp.stack([field[:, :, :, 0], field[:, :, :, -1]], axis=2)
+
+    def within(low, high):
+        return jnp.where(tile == 0, 0.0, low), jnp.where(tile == tiles - 1, 0.0, high)
+
+    partner, other_donors, other_blend, other_rate, low, high = call(
+        functools.partial(couple_kernel, sizes),
+        4,
+        [(slots, rows, lon_count), donors, blend, coefficient, halo_shape, halo_shape],
+        (slots + 3, slots + 3, 2, 2),
+        field,
+        donors,
+        blend,
+        coefficient,
+        edge,
+    )
+    low, high = within(low, high)
+    air_blend = jnp.where(is_air, blend, other_blend)
+    air_rate = jnp.where(is_air, rate, other_rate[0])
 
     def air_first(_):
-        fourier = air_forward(field, partner, donors, blend, np.ascontiguousarray(lon_basis.T))
-        return fourier, jnp.zeros((slots, rows, lon_count), jnp.float32), field
+        fourier = air_forward(field, partner, donors, blend, lon_columns)
+        return (
+            fourier,
+            jnp.zeros((slots, rows, lon_count), jnp.float32),
+            jnp.zeros(field.shape, jnp.float32),
+            jnp.zeros(edge_shape, jnp.float32),
+        )
 
     def sea_first(_):
-        new, looked = sea_step(
-            field, low, high, partner, donors, other_donors, land_sea, blend, rate
+        new, looked, edge, _ = sea_step(
+            field, low, high, partner, donors, other_donors, land_sea, my_weights, blend, rate
         )
-        return jnp.zeros((slots, fields, levels, rows, waves), jnp.float32), looked, new
-
-    fourier, looked, ocean = lax.cond(is_air, air_first, sea_first, 0)
-    low, high = edges(ocean)
-    gathered, sst, _ = call(
+        return jnp.zeros((slots, fields, levels, rows, waves), jnp.float32), looked, new, edge
+
+    fourier, looked, ocean, edge = lax.cond(is_air, air_first, sea_first, 0)
+    gathered, sst, _, low, high = call(
         functools.partial(spread_kernel, sizes),
         0,
-        [(per, LAT, waves), (LAT, lon_count), (fields, levels, rows, waves)],
-        (members * fields,) * 3 + (comps, tiles, tiles, 2),
+        [(per, LAT, waves), (LAT, lon_count), (fields, levels, rows, waves)] + [halo_shape] * 2,
+        (members * fields,) * 3 + (comps, tiles, tiles, 2, 2, 2),
         fourier,
         looked,
+        edge,
     )
+    low, high = within(low, high)
     unit_field = tile % fields
-    unit_rate = lax.dynamic_index_in_dim(air_coefficient, unit_field, keepdims=False)
-    gain = 1.0 / (1.0 + unit_rate * squares / (MODES * MODES))
-
-    def filtered(level):
-        return matmul(lat_inverse, matmul(lat_forward, level) * gain)
-
-    coefs = jnp.concatenate([filtered(gathered[v]) for v in range(per)])
-    state = matmul(coefs, lon_inverse).reshape(per, LAT, lon_count)
+    unit_rate = lax.dynamic_slice_in_dim(air_rate, unit_field, 1)
+    state = to_grid(
+        gathered, squares, unit_rate, lat_tables + split_table(lon_basis), lon_count
+    )
     other_state, flux = call(
         functools.partial(swap_kernel, sizes),
         1,
@@ -646,48 +864,41 @@
     mine = lax.dynamic_slice_in_dim(air_blend, member * per, per)
     mine_own = lax.dynamic_slice_in_dim(mine, member * per, per, axis=1)
     mine_other = lax.dynamic_slice_in_dim(mine, (1 - member) * per, per, axis=1)
-    has_surface = jnp.logical_and(member == 0, unit_field == 0)
-    forced = []
-    for u in range(per):
-        mixing = mine_own[u, 0] * state[0] + mine_other[u, 0] * other_state[0]
-        for v in range(1, per):
-            mixing = mixing + mine_own[u, v] * state[v] + mine_other[u, v] * other_state[v]
-        level = state[u] + forcing_rate * jnp.tanh(mixing)
-        if u == 0:
-            level = level + jnp.where(has_surface, coupling_rate * (sst - state[0]), 0.0)
-        forced.append(level)
-    fourier = matmul(jnp.concatenate(forced), lon_forward).reshape(per, LAT, waves)
-    back = jnp.stack([filtered(fourier[v]) for v in range(per)])
-    zonal_mean = back[0, :, 0] * lon_basis[0, 0]
-    air_score = jnp.sum(zonal_mean * weights) / weight_total
-    air_point = jnp.full((8, 128), air_score)
-    own, far, air_scores = call(
+    flag = jnp.logical_and(member == 0, unit_field == 0).astype(jnp.int32).reshape(1)
+    back, air_point = to_coefs(
+        state,
+        other_state,
+        sst,
+        mine_own,
+        mine_other,
+        flag,
+        jnp.asarray(air_weights),
+        squares,
+        unit_rate,
+        lat_tables + split_table(lon_columns),
+    )
+
+    def sea_second(_):
+        new, _, _, sums = sea_step(
+            ocean, low, high, flux, donors, donors, land_sea, my_weights, blend, rate
+        )
+        return new, sums
+
+    def air_second(_):
+        return ocean, jnp.zeros((slots, 8, 128), jnp.float32)
+
+    ocean, sums = lax.cond(is_air, air_second, sea_second, 0)
+    own, far, air_scores, far_ocean, sea_parts = call(
         functools.partial(return_kernel, sizes),
         2,
-        [(slots, fields, levels, rows, waves)] * 2 + [(slots, 8, 128)],
+        [(slots, fields, levels, rows, waves)] * 2
+        + [(slots, 8, 128), field, (tiles, slots, 8, 128)],
         (tiles, slots * fields * members, slots * fields * members)
-        + (slots * fields * members, tiles, comps, 2),
+        + (slots * fields * members, tiles, comps, 3, 1, 1, tiles, tiles),
         back,
         air_point,
-    )
-
-    def sea_second(_):
-        new, _ = sea_step(ocean, low, high, flux, donors, donors, land_sea, blend, rate)
-        my_weights = lax.dynamic_slice_in_dim(jnp.asarray(weights), tile * rows, rows)
-        sums = jnp.sum(jnp.mean(new[:, 0, 0], axis=2) * my_weights, axis=1)
-        return new, jnp.broadcast_to(jnp.pad(sums, (0, 8 - slots))[:, None], (8, 128))
-
-    def air_second(_):
-        return ocean, jnp.zeros((8, 128), jnp.float32)
-
-    ocean, partial = lax.cond(is_air, air_second, sea_second, 0)
-    far_ocean, sea_parts = call(
-        functools.partial(ocean_kernel, sizes),
-        3,
-        [(slots, fields, levels, rows, lon_count), (tiles, 8, 128)],
-        (1, 1, tiles, tiles, 1),
         ocean,
-        partial,
+        sums,
     )
     parents = lax.dynamic_slice_in_dim(ancestry, member * slots, slots)
 
@@ -701,7 +912,7 @@
         return grid.reshape(member_state.shape), air_scores[:, 0, :1]
 
     def sea_last(_):
-        score = jnp.sum(sea_parts[:, :slots, :1], axis=0) / weight_total
+        score = jnp.sum(sea_parts[:, :, 0, :1], axis=0) / weight_total
         states = resampled(sea_last_kernel, inside, near, ocean, far_ocean, (), lon_count)
         return states.reshape(member_state.shape), score
 

time: 214 us -> 207 us (0.967)
  the two profiles are of different devices: /device:TPU:5 before, /device:TPU:11 now
where the time goes in v1:
time: 207 us; the launch traced here: 206 us
  Pallas kernels  169 us (82%)
  local copies, waits for them, and re-layouts  32.4 us (16%)
  other arithmetic  3.38 us (2%)
    pallas_call x4, Pallas kernels, call(): pl.pallas_call(kernel, out_shape=[jax.ShapeDtypeStruct(out.shape, out.dty...  138 us
    unnamed x53, local copies, waits for them, and re-layouts  18.5 us
    pallas_call x1, Pallas kernels, air_forward(): pl.pallas_call(air_kernel, grid=(slots, fields), out_shape=jax.ShapeDtype...  8.81 us
    pallas_call x1, Pallas kernels, resampled(): pl.pallas_call(kernel, grid_spec=pltpu.PrefetchScalarGridSpec(num_scalar_...  8.4 us
    pallas_call x1, Pallas kernels, to_coefs(): pl.pallas_call(to_coefs_kernel, grid=state.shape[:1], out_shape=[jax.Shap...  7.08 us
    pallas_call x1, Pallas kernels, to_grid(): pl.pallas_call(to_grid_kernel, grid=value.shape[:1], out_shape=jax.ShapeD...  7.05 us
    another operation x6, local copies, waits for them, and re-layouts  6.81 us
    squeeze x1, local copies, waits for them, and re-layouts, by_units(): field = member_state[:, 0]  4.92 us

profile of v1, /device:TPU:11, one launch (start us, length us, event | category | flops | bytes accessed | tf_op | source)
XLA Modules:
  0.0 206.4 jit_solution(9297883427056539033)
XLA Ops:
  0.7 1.3 compare_convert_fusion
  2.0 0.6 and_select_fusion.1
  2.6 0.7 constant_dynamic-slice_fusion
  3.4 5.4 %copy.37 = f32[2,1,4,4,48,768]{5,3,2,0,4,1:T(4,128)S(1)} copy(f32[2,1,4,4,48,768]{5,4,3,2,1,0:T(8,128)} %param.27) | data formatting | bytes 9437184 | tf_op args[0]
  8.7 0.0 copy-start.13
  8.8 0.8 pad_maximum_fusion.edge_ref
  9.6 1.4 copy-done.13
  11.0 4.9 %copy.29.field_ref = f32[2,4,4,48,768]{4,3,2,1,0:T(8,128)} copy(f32[2,4,4,48,768]{4,2,1,0,3:T(4,128)S(1)} %bitcast.28) | data formatting | bytes 9437184 | tf_op jit(solution)/shard_map/squeeze | solution.py:782
  15.9 0.0 copy-done.16
  15.9 0.0 copy-done.20
  15.9 0.0 copy-done.22
  15.9 0.0 copy-start.19
  15.9 12.5 %shard_map.216 = (f32[2,48,768]{2,1,0:T(8,128)S(1)}, s32[48,768]{1,0:T(8,128)S(1)}, f32[4,4]{1,0:T(4,128)}, f32[1,4]{1,0:T(1,128)}, f32[2,4,4,768]{3,2,1,0:T(4,128)S(1)}, /*index=5*/f32[2,4,4,768]{3,2,1,0:T(4,128)S(1)}) custom-call(f32[2,4,4,48,768]{4,3,2,1,0:T(8,128)} %copy.29.field_ref, s32[48,768]{1,0:T(8,128)S(1)} %bitcast.33, f32[4,4]{1,0:T(4,128)S(1)} %bitcast.37, ...), custom_call_target="tpu_custom_call" | custom-call | tf_op jit(solution)/shard_map/pallas_call | solution.py:448
  28.4 0.6 broadcast_select_fusion.5
  29.1 0.6 dynamic_slice.18.rate_ref
  29.7 0.1 fusion
  29.8 0.0 copy-done.17
  29.8 0.0 copy-done.19
  29.8 0.0 copy-start.8
  29.8 0.0 copy-start.9
  29.8 0.0 copy-start.10
  29.8 14.8 %conditional.3 = (f32[2,4,4,48,512]{4,3,2,1,0:T(8,128)}, f32[2,48,768]{2,1,0:T(8,128)S(1)}, f32[2,4,4,48,768]{4,3,2,1,0:T(8,128)S(1)}, f32[2,4,2,4,768]{4,3,2,1,0:T(4,128)S(1)}) conditional(s32[]{:T(128)} %convert_element_type.4, (pred[2,4,4,768]{3,2,1,0:T(4,128)(4,1)S(1)}, f32[2,4,4,768]{3,2,1,0:T(4,128)S(1)}, pred[2,4,4,768]{3,2,1,0:T(4,128)(4,1)S(1)}, ...), branch_computations={%region_0.1_spmd, %region_1.2_spmd} | conditional | flops 49152 | bytes 17793096 | solution.py:841
  30.0 0.0 copy-start.18
  30.0 5.2 %copy.31.field_ref = f32[2,4,4,48,768]{4,3,2,1,0:T(8,128)S(1)} copy(f32[2,4,4,48,768]{4,2,1,0,3:T(4,128)} %get-tuple-element.240) | data formatting | bytes 9437184 | tf_op jit(solution)/shard_map
  35.2 0.0 copy-done.18
  35.2 8.8 %branch_1_fun.2 = f32[2,4,4,48,512]{4,3,2,1,0:T(8,128)} custom-call(f32[2,4,4,48,768]{4,3,2,1,0:T(8,128)S(1)} %copy.31.field_ref, f32[2,48,768]{2,1,0:T(8,128)S(1)} %get-tuple-element.144.partner_ref, s32[48,768]{1,0:T(8,128)S(1)} %get-tuple-element.145.donors_ref, f32[4,4]{1,0:T(4,128)S(1)} %get-tuple-element.146.blend_ref, ...), custom_call_target="tpu_custom_call" | custom-call | tf_op jit(solution)/shard_map/cond/branch_1_fun/pallas_call | solution.py:593
  44.1 0.5 broadcast.42
  44.6 0.0 copy-start.14
  44.7 2.2 %copy-done.14 = f32[2,4,4,48,768]{4,3,2,1,0:T(8,128)} copy-done((f32[2,4,4,48,768]{4,3,2,1,0:T(8,128)}, f32[2,4,4,48,768]{4,3,2,1,0:T(8,128)S(1)}, u32[]{:S(2)}) %copy-start.14) | copy-done | bytes 4718616
  46.8 41.0 %shard_map.217 = (f32[2,384,512]{2,1,0:T(8,128)}, f32[384,768]{1,0:T(8,128)}, f32[4,4,48,512]{3,2,1,0:T(8,128)}, f32[2,4,4,768]{3,2,1,0:T(4,128)S(1)}, f32[2,4,4,768]{3,2,1,0:T(4,128)S(1)}) custom-call(f32[2,4,4,48,512]{4,3,2,1,0:T(8,128)} %get-tuple-element.205.c_ref, f32[2,48,768]{2,1,0:T(8,128)S(1)} %get-tuple-element.206.r_ref, ...), custom_call_target="tpu_custom_call" | custom-call | tf_op jit(solution)/shard_map/pallas_call | solution.py:448
  87.8 0.0 copy-done.3
  87.8 0.0 copy-done.7
  87.8 0.0 copy-done.8
  87.8 0.0 copy-done.9
  87.9 0.0 copy-done.10
  87.9 0.0 copy-start.5
  87.9 1.4 copy-done.5
  89.3 7.0 %shard_map.218.x_ref = f32[2,384,768]{2,1,0:T(8,128)S(1)} custom-call(f32[2,384,512]{2,1,0:T(8,128)S(1)} %copy-done.5, f32[256,512]{1,0:T(8,128)S(1)} %copy-done.3, f32[1]{0:T(128)} %dynamic_slice.18.rate_ref, bf16[256,384]{1,0:T(8,128)(2,1)S(1)} %copy-done.10, bf16[256,384]{1,0:T(8,128)(2,1)S(1)} %copy-done.9, bf16[384,256]{1,0:T(8,128)(2,1)S(1)} %copy-done.8, ...), custom_call_target="tpu_custom_call" | custom-call | tf_op jit(solution)/shard_map/pallas_call | solution.py:742
  96.3 0.0 copy-start
  96.3 1.4 copy-done
  97.8 5.0 %shard_map.219 = (f32[2,384,768]{2,1,0:T(8,128)}, f32[2,48,768]{2,1,0:T(8,128)S(1)}) custom-call(f32[2,384,768]{2,1,0:T(8,128)} %copy-done), custom_call_target="tpu_custom_call" | custom-call | tf_op jit(solution)/shard_map/pallas_call | solution.py:448
  102.8 0.0 copy-start.23
  102.8 0.0 copy-done.11
  102.8 0.0 copy-done.6
  102.8 0.0 copy-start.1
  102.8 1.7 copy-done.1
  104.5 1.7 copy-done.2
  106.1 7.1 %shard_map.220 = (f32[2,384,512]{2,1,0:T(8,128)S(1)}, f32[8,128]{1,0:T(8,128)S(1)}) custom-call(f32[2,384,768]{2,1,0:T(8,128)S(1)} %copy-done.1, f32[2,384,768]{2,1,0:T(8,128)S(1)} %copy-done.2, f32[384,768]{1,0:T(8,128)S(1)} %copy-done.6, f32[2,2]{1,0:T(2,128)S(1)} %get-tuple-element.265.here_ref, f32[2,2]{1,0:T(2,128)S(1)} %get-tuple-element.264.there_ref, ...), custom_call_target="tpu_custom_call" | custom-call | tf_op jit(solution)/shard_map/pallas_call | solution.py:755
  113.2 0.0 copy-start.4
  113.2 0.0 copy-start.12
  113.2 0.0 copy-done.23
  113.2 0.0 copy-done.21
  113.2 1.1 copy-done.4
  114.4 0.0 copy-done.12
  114.4 79.6 %shard_map.221 = (f32[2,4,4,48,512]{4,3,2,1,0:T(8,128)S(1)}, f32[2,4,4,48,512]{4,3,2,1,0:T(8,128)}, f32[2,8,128]{2,1,0:T(8,128)S(1)}, f32[2,4,4,48,768]{4,3,2,1,0:T(8,128)}, f32[8,2,8,128]{3,2,1,0:T(8,128)S(1)}) custom-call(f32[2,384,512]{2,1,0:T(8,128)} %copy-done.4, f32[8,128]{1,0:T(8,128)} %copy-done.12, f32[2,4,4,48,768]{4,3,2,1,0:T(8,128)} %get-tuple-element.214.o_ref, ...), custom_call_target="tpu_custom_call" | custom-call | tf_op jit(solution)/shard_map/pallas_call | solution.py:448
  194.1 0.0 copy-done.24
  194.1 0.0 copy-done.25
  194.1 10.1 %conditional.5 = (f32[2,1]{0,1:T(1,128)S(1)}, f32[2,1,4,4,48,768]{5,4,3,2,1,0:T(8,128)S(1)}) conditional(s32[]{:T(128)} %convert_element_type.4, (s32[2]{0:T(128)S(1)}, s32[2]{0:T(128)S(1)}, f32[2,4,4,48,768]{4,3,2,1,0:T(8,128)}, f32[2,4,4,48,768]{4,3,2,1,0:T(8,128)}, f32[8,2,8,128]{3,2,1,0:T(8,128)S(1)}) %tuple.79, (s32[2]{0:T(128)S(1)}, ...), branch_computations={%region_4.6_spmd, %region_6.7_spmd} | conditional | flops 16 | bytes 16416 | solution.py:919
  194.1 1.1 copy.32
  195.2 0.7 slice_bitcast_fusion
  195.8 8.4 %branch_1_fun.3 = f32[2,4,4,48,768]{4,3,2,1,0:T(8,128)S(1)} custom-call(s32[2]{0:T(128)S(1)} %get-tuple-element.167.inside_ref, s32[2]{0:T(128)S(1)} %get-tuple-element.168.near_ref, f32[2,4,4,48,512]{4,3,2,1,0:T(8,128)S(1)} %get-tuple-element.169.own_ref, f32[2,4,4,48,512]{4,3,2,1,0:T(8,128)} %get-tuple-element.170.far_ref, ...), custom_call_target="tpu_custom_call" | custom-call | tf_op jit(solution)/shard_map/cond/branch_1_fun/pallas_call | solution.py:664
  204.2 0.0 copy-start.15
  204.2 0.0 copy-start.26
  204.3 2.2 %copy-done.15 = f32[2,1,4,4,48,768]{5,4,3,2,1,0:T(8,128)} copy-done((f32[2,1,4,4,48,768]{5,4,3,2,1,0:T(8,128)}, f32[2,1,4,4,48,768]{5,4,3,2,1,0:T(8,128)S(1)}, u32[]{:S(2)}) %copy-start.15) | copy-done | bytes 4718616
  (21 shorter events, 0.1 us)
Async XLA Ops:
  8.7 2.2 %copy-start.13 = (f32[2,1,4,4,48,768]{5,3,2,0,4,1:T(4,128)}, f32[2,1,4,4,48,768]{5,3,2,0,4,1:T(4,128)S(1)}, u32[]{:S(2)}) copy-start(f32[2,1,4,4,48,768]{5,3,2,0,4,1:T(4,128)S(1)} %copy.37) | copy-start | bytes 14155780
  11.0 4.9 %copy-start.16 = (s32[1,48,768]{2,1,0:T(8,128)S(1)}, s32[1,48,768]{2,1,0:T(8,128)}, u32[]{:S(2)}) copy-start(s32[1,48,768]{2,1,0:T(8,128)} %param.30) | copy-start | bytes 442372
  11.0 4.9 %copy-start.20 = (f32[1,4,4]{2,1,0:T(4,128)S(1)}, f32[1,4,4]{2,1,0:T(4,128)}, u32[]{:S(2)}) copy-start(f32[1,4,4]{2,1,0:T(4,128)} %param.28) | copy-start | bytes 196
  11.0 4.9 %copy-start.22 = (f32[1,4]{1,0:T(1,128)S(1)}, f32[1,4]{1,0:T(1,128)}, u32[]{:S(2)}) copy-start(f32[1,4]{1,0:T(1,128)} %rate_ref.1) | copy-start | bytes 52
  15.9 13.9 %copy-start.17 = (bf16[768,512]{1,0:T(8,128)(2,1)S(1)}, bf16[768,512]{1,0:T(8,128)(2,1)}, u32[]{:S(2)}) copy-start(bf16[768,512]{1,0:T(8,128)(2,1)} %constant.125.clone.gl) | copy-start | bytes 2359300
  15.9 13.9 %copy-start.19 = (s32[48,768]{1,0:T(8,128)S(1)}, s32[48,768]{1,0:T(8,128)}, u32[]{:S(2)}) copy-start(s32[48,768]{1,0:T(8,128)} %param.31) | copy-start | bytes 442372
  29.8 58.0 %copy-start.3 = (f32[256,512]{1,0:T(8,128)S(1)}, f32[256,512]{1,0:T(8,128)}, u32[]{:S(2)}) copy-start(f32[256,512]{1,0:T(8,128)} %constant.122.clone.sq_ref) | copy-start | bytes 1572868
  29.8 58.0 %copy-start.7 = (bf16[384,256]{1,0:T(8,128)(2,1)S(1)}, bf16[384,256]{1,0:T(8,128)(2,1)}, u32[]{:S(2)}) copy-start(bf16[384,256]{1,0:T(8,128)(2,1)} %constant.121.clone.il) | copy-start | bytes 589828
  29.8 58.0 %copy-start.8 = (bf16[384,256]{1,0:T(8,128)(2,1)S(1)}, bf16[384,256]{1,0:T(8,128)(2,1)}, u32[]{:S(2)}) copy-start(bf16[384,256]{1,0:T(8,128)(2,1)} %constant.120.clone.ih) | copy-start | bytes 589828
  29.8 58.0 %copy-start.9 = (bf16[256,384]{1,0:T(8,128)(2,1)S(1)}, bf16[256,384]{1,0:T(8,128)(2,1)}, u32[]{:S(2)}) copy-start(bf16[256,384]{1,0:T(8,128)(2,1)} %constant.119.clone.fl) | copy-start | bytes 589828
  29.8 58.0 %copy-start.10 = (bf16[256,384]{1,0:T(8,128)(2,1)S(1)}, bf16[256,384]{1,0:T(8,128)(2,1)}, u32[]{:S(2)}) copy-start(bf16[256,384]{1,0:T(8,128)(2,1)} %constant.118.clone.fh) | copy-start | bytes 589828
  30.0 5.2 %copy-start.18 = (bf16[768,512]{1,0:T(8,128)(2,1)S(1)}, bf16[768,512]{1,0:T(8,128)(2,1)}, u32[]{:S(2)}) copy-start(bf16[768,512]{1,0:T(8,128)(2,1)} %get-tuple-element.147.high_ref) | copy-start | bytes 2359300 | tf_op jit(solution)/shard_map/cond
  44.6 2.2 %copy-start.14 = (f32[2,4,4,48,768]{4,3,2,1,0:T(8,128)}, f32[2,4,4,48,768]{4,3,2,1,0:T(8,128)S(1)}, u32[]{:S(2)}) copy-start(f32[2,4,4,48,768]{4,3,2,1,0:T(8,128)S(1)} %get-tuple-element.210) | copy-start | bytes 14155780
  46.8 55.9 %copy-start.11 = (f32[384,128]{1,0:T(8,128)S(1)}, f32[384,128]{1,0:T(8,128)}, u32[]{:S(2)}) copy-start(f32[384,128]{1,0:T(8,128)} %constant.128.clone.w_ref) | copy-start | bytes 589828
  87.9 1.4 copy-start.5
  89.3 13.5 %copy-start.6 = (f32[384,768]{1,0:T(8,128)S(1)}, f32[384,768]{1,0:T(8,128)}, u32[]{:S(2)}) copy-start(f32[384,768]{1,0:T(8,128)} %get-tuple-element.216.sst_ref) | copy-start | bytes 3538948
  96.3 1.4 copy-start
  102.8 10.5 %copy-start.23 = (f32[1,4]{1,0:T(1,128)S(1)}, f32[1,4]{1,0:T(1,128)}, u32[]{:S(2)}) copy-start(f32[1,4]{1,0:T(1,128)} %rate_ref.1) | copy-start | bytes 52
  102.8 1.7 copy-start.1
  104.5 1.7 copy-start.2
  106.1 7.1 %copy-start.21 = (f32[1,4,4]{2,1,0:T(4,128)S(1)}, f32[1,4,4]{2,1,0:T(4,128)}, u32[]{:S(2)}) copy-start(f32[1,4,4]{2,1,0:T(4,128)} %param.28) | copy-start | bytes 196
  113.2 1.2 copy-start.4
  113.2 1.2 copy-start.12
  114.4 79.7 %copy-start.24 = (s32[2]{0:T(128)S(1)}, s32[2]{0:T(128)}, u32[]{:S(2)}) copy-start(s32[2]{0:T(128)} %get-tuple-element.256) | copy-start | bytes 28
  114.4 79.7 %copy-start.25 = (s32[2]{0:T(128)S(1)}, s32[2]{0:T(128)}, u32[]{:S(2)}) copy-start(s32[2]{0:T(128)} %and_select_fusion.1) | copy-start | bytes 28
  204.2 2.2 %copy-start.15 = (f32[2,1,4,4,48,768]{5,4,3,2,1,0:T(8,128)}, f32[2,1,4,4,48,768]{5,4,3,2,1,0:T(8,128)S(1)}, u32[]{:S(2)}) copy-start(f32[2,1,4,4,48,768]{5,4,3,2,1,0:T(8,128)S(1)} %get-tuple-element.255) | copy-start | bytes 14155780
  204.2 2.2 %copy-start.26 = (f32[2,1]{0,1:T(1,128)}, f32[2,1]{0,1:T(1,128)S(1)}, u32[]{:S(2)}) copy-start(f32[2,1]{0,1:T(1,128)S(1)} %get-tuple-element.254) | copy-start | bytes 28

commit v2 on v1

--- a/solution.py
+++ b/solution.py
@@ -286,63 +286,38 @@
     pl.when(north)(down.wait_recv)
 
 
-def swap_kernel(sizes, x_ref, xo_ref, sa_ref, send, recv, ssend, srecv, loc):
-    members, comps, fields, tiles, rows = sizes
-    me = m, y, t = here()
-    unit_m, unit_f = t // fields, t % fields
-    has_surface = jnp.logical_and(m == 0, unit_f == 0)
+def swap_kernel(sizes, x_ref, xo_ref, send, recv):
+    m, y, t = here()
     other = (1 - m, y, t)
-    targets = [(m >= 0, other)]
-    for s in range(comps):
-        source = (0, s, m * fields)
-        targets.append((jnp.logical_and(y == 1, differs(source, me)), source))
-    own_surface = jnp.logical_and(has_surface, jnp.logical_and(y == 1, unit_m == m))
-    count = 1 + jnp.where(has_surface, tiles - own_surface.astype(jnp.int32), 0)
-    greet(targets, count)
-
-    def surface(j):
-        device = (unit_m, 1, j)
-        part = x_ref.at[0, pl.ds(j * rows, rows), :]
-        copy = remote(part, sa_ref.at[y], ssend.at[j], srecv.at[y], device)
-        return device, copy, pltpu.make_async_copy(part, sa_ref.at[y], loc.at[0])
-
-    @pl.when(has_surface)
-    def _():
-        for j in range(tiles):
-            device, copy, local = surface(j)
-            away = differs(device, me)
-            pl.when(away)(copy.start)
-            pl.when(jnp.logical_not(away))(local.start)
-
+    greet([(m >= 0, other)], 1)
     across = remote(x_ref, xo_ref, send.at[0], recv.at[0], other)
     across.start()
     across.wait()
-
-    @pl.when(has_surface)
-    def _():
-        for j in range(tiles):
-            device, copy, local = surface(j)
-            away = differs(device, me)
-            pl.when(away)(copy.wait_send)
-            pl.when(jnp.logical_not(away))(local.wait)
-
-    for s in range(comps):
-        away = jnp.logical_and(y == 1, differs((0, s, m * fields), me))
-        arrival = remote(sa_ref.at[s], sa_ref.at[s], ssend.at[0], srecv.at[s], me)
-        pl.when(away)(arrival.wait_recv)
 
 
 def return_kernel(
     sizes,
     f_ref,
     p_ref,
+    x_ref,
     o_ref,
-    q_ref,
+    low_ref,
+    high_ref,
+    donors_ref,
+    land_ref,
+    weight_ref,
+    blend_ref,
+    rate_ref,
     own_ref,
     far_ref,
     score_ref,
+    new_ref,
     faro_ref,
     part_ref,
+    before,
+    after,
+    flux,
+    sums,
     send,
     recv,
     fsend,
@@ -352,8 +327,11 @@
     loc,
     osend,
     orecv,
+    keep,
     qsend,
     qrecv,
+    ssend,
+    srecv,
 ):
     members, comps, fields, tiles, rows = sizes
     me = m, y, t = here()
@@ -365,16 +343,34 @@
     targets = [(m >= 0, other)]
     for j in range(tiles):
         targets.append((jnp.logical_and(y == 1, j != t), (m, y, j)))
+    for s in range(comps):
+        source = (0, s, m * fields)
+        targets.append((jnp.logical_and(y == 1, differs(source, me)), source))
     for s, f, c in pieces:
         source = (c, s, m * fields + f)
         targets.append((jnp.logical_and(y == 0, differs(source, me)), source))
     own_unit = jnp.logical_and(y == 0, unit_m == m).astype(jnp.int32)
-    greet(targets, tiles - own_unit + jnp.where(y == 0, 1, tiles))
-    across = remote(o_ref, faro_ref, osend.at[0], orecv.at[0], other)
-    keep = pltpu.make_async_copy(q_ref, part_ref.at[t], loc.at[2])
+    own_surface = jnp.logical_and(has_surface, jnp.logical_and(y == 1, unit_m == m))
+    count = tiles - own_unit + jnp.where(y == 0, 1, tiles)
+    greet(targets, count + jnp.where(has_surface, tiles - own_surface.astype(jnp.int32), 0))
+    load = pltpu.make_async_copy(o_ref, before, loc.at[2])
+    pl.when(y == 1)(load.start)
 
     def share(j):
-        return remote(q_ref, part_ref.at[t], qsend.at[j], qrecv.at[t], (m, y, j))
+        return remote(sums, part_ref.at[t], qsend.at[j], qrecv.at[t], (m, y, j))
+
+    def surface(j):
+        device = (unit_m, 1, j)
+        part = x_ref.at[0, pl.ds(j * rows, rows), :]
+        copy = remote(part, flux.at[y], ssend.at[j], srecv.at[y], device)
+        return differs(device, me), copy, pltpu.make_async_copy(part, flux.at[y], loc.at[3])
+
+    @pl.when(has_surface)
+    def _():
+        for j in range(tiles):
+            away, copy, local = surface(j)
+            pl.when(away)(copy.start)
+            pl.when(jnp.logical_not(away))(local.start)
 
     def band(j):
         device = (unit_m, 0, j)
@@ -396,13 +392,6 @@
         pl.when(jnp.logical_not(away))(local.start)
         pl.when(jnp.logical_and(has_surface, away))(point.start)
         pl.when(jnp.logical_and(has_surface, jnp.logical_not(away)))(local_point.start)
-
-    @pl.when(y == 1)
-    def _():
-        across.start()
-        keep.start()
-        for j in range(tiles):
-            pl.when(j != t)(share(j).start)
 
     def forward(k):
         s, f, c = pieces[k]
@@ -434,14 +423,87 @@
         pl.when(away)(copy.wait_send)
         pl.when(jnp.logical_and(has_surface, away))(point.wait_send)
 
+    def clone(s, f):
+        i = s * fields + f
+        part = (s, f)
+        return (
+            remote(after.at[part], faro_ref.at[part], osend.at[i], orecv.at[i], other),
+            pltpu.make_async_copy(after.at[part], new_ref.at[part], keep.at[i]),
+        )
+
     @pl.when(y == 1)
     def _():
-        keep.wait()
+        load.wait()
+        for s in range(comps):
+            away = differs((0, s, m * fields), me)
+            arrival = remote(flux.at[s], flux.at[s], ssend.at[0], srecv.at[s], me)
+            pl.when(away)(arrival.wait_recv)
+            own = pltpu.make_async_copy(x_ref.at[0, pl.ds(0, rows), :], flux.at[s], loc.at[3])
+            pl.when(jnp.logical_not(away))(own.wait)
+        sea = land_ref[...] == 1
+
+        def step(i, _):
+            s, f = lax.div(i, fields), lax.rem(i, fields)
+            levels = before.shape[2]
+            for u in range(levels):
+                mixing = blend_ref[u, 0] * before[s, f, 0]
+                for v in range(1, levels):
+                    mixing = mixing + blend_ref[u, v] * before[s, f, v]
+                value = before[s, f, u]
+                forced = value + forcing_rate * jnp.tanh(mixing)
+                ends = (low_ref[s, f, u : u + 1], high_ref[s, f, u : u + 1])
+                forced = forced + rate_ref[f] * laplacian_of(value, *ends)
+                after[s, f, u] = jnp.where(sea, forced, value)
+
+            @pl.when(f == 0)
+            def _():
+                value = before[s, 0, 0]
+                extra = coupling_rate * (lookup(flux[s], donors_ref[...]) - value)
+                result = after[s, 0, 0] + jnp.where(sea, extra, 0.0)
+                after[s, 0, 0] = result
+                sums[s] = weighted_sum(result, weight_ref[...], sums.shape[1:])
+
+            across, own = clone(s, f)
+            across.start()
+            own.start()
+            return 0
+
+        lax.fori_loop(0, comps * fields, step, 0)
+        mine = pltpu.make_async_copy(sums, part_ref.at[t], loc.at[4])
+        mine.start()
+        for j in range(tiles):
+            pl.when(j != t)(share(j).start)
+        mine.wait()
         for j in range(tiles):
             arrival = remote(part_ref.at[j], part_ref.at[j], qsend.at[0], qrecv.at[j], me)
             pl.when(j != t)(arrival.wait_recv)
             pl.when(j != t)(share(j).wait_send)
-        across.wait()
+        for s in range(comps):
+            for f in range(fields):
+                across, own = clone(s, f)
+                across.wait()
+                own.wait()
+
+    @pl.when(has_surface)
+    def _():
+        for j in range(tiles):
+            away, copy, local = surface(j)
+            pl.when(away)(copy.wait_send)
+
+
+def laplacian_of(value, low, high):
+    rows, lon_count = value.shape
+    row = lax.broadcasted_iota(jnp.int32, (rows, lon_count), 0)
+    north = jnp.where(row == 0, low, pltpu.roll(value, 1, 0))
+    south = jnp.where(row == rows - 1, high, pltpu.roll(value, rows - 1, 0))
+    east, west = pltpu.roll(value, 1, 1), pltpu.roll(value, lon_count - 1, 1)
+    return south + north + east + west - 4.0 * value
+
+
+def weighted_sum(value, weights, shape):
+    total = jnp.sum(value * weights, axis=0, keepdims=True)
+    total = jnp.sum(total, axis=1, keepdims=True) / value.shape[1]
+    return jnp.broadcast_to(total, shape)
 
 
 def call(kernel, collective_id, outs, sems, *args):
@@ -523,31 +585,21 @@
     donors_ref,
     next_ref,
     land_ref,
-    weight_ref,
     blend_ref,
     rate_ref,
     out_ref,
     look_ref,
     edge_ref,
-    sum_ref,
 ):
     levels, rows, lon_count = field_ref.shape[2:]
     rate = rate_ref[pl.program_id(1)]
     sea = land_ref[...] == 1
     first = pl.program_id(1) == 0
-    row = lax.broadcasted_iota(jnp.int32, (rows, lon_count), 0)
     for u in range(levels):
         value = field_ref[0, 0, u]
         forced = value + mixed_level(blend_ref, field_ref, u)
-        north = jnp.where(row == 0, low_ref[0, 0, u : u + 1], pltpu.roll(value, 1, 0))
-        south = jnp.where(row == rows - 1, high_ref[0, 0, u : u + 1], pltpu.roll(value, rows - 1, 0))
-        laplacian = (
-            south
-            + north
-            + pltpu.roll(value, 1, 1)
-            + pltpu.roll(value, lon_count - 1, 1)
-            - 4.0 * value
-        )
+        ends = (low_ref[0, 0, u : u + 1], high_ref[0, 0, u : u + 1])
+        laplacian = laplacian_of(value, *ends)
         if u == 0:
             received = lookup(partner_ref[0], donors_ref[...])
             extra = coupling_rate * (received - value)
@@ -560,9 +612,6 @@
     @pl.when(first)
     def _():
         look_ref[0] = lookup(out_ref[0, 0, 0], next_ref[...])
-        total = jnp.sum(out_ref[0, 0, 0] * weight_ref[...], axis=0, keepdims=True)
-        total = jnp.sum(total, axis=1, keepdims=True) / lon_count
-        sum_ref[0] = jnp.broadcast_to(total, sum_ref.shape[1:])
 
 
 def whole_spec(array):
@@ -608,7 +657,7 @@
     )(field, partner, donors, blend, high, low)
 
 
-def sea_step(field, low, high, partner, donors, following, land_sea, weights, blend, rate):
+def sea_step(field, low, high, partner, donors, following, land_sea, blend, rate):
     slots, fields, levels, rows, lon_count = field.shape
     edge = (slots, fields, 2, levels, lon_count)
     return pl.pallas_call(
@@ -618,7 +667,6 @@
             jax.ShapeDtypeStruct(field.shape, jnp.float32),
             jax.ShapeDtypeStruct(partner.shape, jnp.float32),
             jax.ShapeDtypeStruct(edge, jnp.float32),
-            jax.ShapeDtypeStruct((slots, 8, 128), jnp.float32),
         ],
         in_specs=[
             state_spec(field.shape),
@@ -628,7 +676,6 @@
             whole_spec(donors),
             whole_spec(following),
             whole_spec(land_sea),
-            whole_spec(weights),
             scalar_spec(),
             scalar_spec(),
         ],
@@ -636,10 +683,9 @@
             state_spec(field.shape),
             surface_spec(partner.shape),
             state_spec(edge),
-            surface_spec((slots, 8, 128)),
         ],
         compiler_params=large,
-    )(field, low, high, partner, donors, following, land_sea, weights, blend, rate)
+    )(field, low, high, partner, donors, following, land_sea, blend, rate)
 
 
 def air_last_kernel(inside_ref, near_ref, own_ref, far_ref, high_ref, low_ref, out_ref):
@@ -672,6 +718,29 @@
         out_shape=jax.ShapeDtypeStruct(shape, jnp.float32),
         compiler_params=large,
     )(inside, near, own, far, *tables)
+
+
+def edge_kernel(top_ref, bottom_ref, edge_ref):
+    for u in range(top_ref.shape[2]):
+        edge_ref[0, 0, 0, u : u + 1] = top_ref[0, 0, u, :1]
+        edge_ref[0, 0, 1, u : u + 1] = bottom_ref[0, 0, u, 7:]
+
+
+def edge_rows(field):
+    slots, fields, levels, rows, lon_count = field.shape
+    edge = (slots, fields, 2, levels, lon_count)
+    block = (1, 1, levels, 8, lon_count)
+    last = rows // 8 - 1
+    return pl.pallas_call(
+        edge_kernel,
+        grid=(slots, fields),
+        out_shape=jax.ShapeDtypeStruct(edge, jnp.float32),
+        in_specs=[
+            pl.BlockSpec(block, lambda s, f: (s, f, 0, 0, 0)),
+            pl.BlockSpec(block, lambda s, f: (s, f, 0, last, 0)),
+        ],
+        out_specs=state_spec(edge),
+    )(field, field)
 
 
 def left3(high_ref, low_ref, value):
@@ -803,7 +872,7 @@
     donors = interpolation_donor_meridians[0]
     edge_shape = (slots, fields, 2, levels, lon_count)
     halo_shape = (slots, fields, levels, lon_count)
-    edge = jnp.stack([field[:, :, :, 0], field[:, :, :, -1]], axis=2)
+    edge = edge_rows(field)
 
     def within(low, high):
         return jnp.where(tile == 0, 0.0, low), jnp.where(tile == tiles - 1, 0.0, high)
@@ -833,8 +902,8 @@
         )
 
     def sea_first(_):
-        new, looked, edge, _ = sea_step(
-            field, low, high, partner, donors, other_donors, land_sea, my_weights, blend, rate
+        new, looked, edge = sea_step(
+            field, low, high, partner, donors, other_donors, land_sea, blend, rate
         )
         return jnp.zeros((slots, fields, levels, rows, waves), jnp.float32), looked, new, edge
 
@@ -854,12 +923,8 @@
     state = to_grid(
         gathered, squares, unit_rate, lat_tables + split_table(lon_basis), lon_count
     )
-    other_state, flux = call(
-        functools.partial(swap_kernel, sizes),
-        1,
-        [(per, LAT, lon_count), (slots, rows, lon_count)],
-        (1, 1, tiles, comps, 1),
-        state,
+    (other_state,) = call(
+        functools.partial(swap_kernel, sizes), 1, [(per, LAT, lon_count)], (1, 1), state
     )
     mine = lax.dynamic_slice_in_dim(air_blend, member * per, per)
     mine_own = lax.dynamic_slice_in_dim(mine, member * per, per, axis=1)
@@ -878,28 +943,26 @@
         lat_tables + split_table(lon_columns),
     )
 
-    def sea_second(_):
-        new, _, _, sums = sea_step(
-            ocean, low, high, flux, donors, donors, land_sea, my_weights, blend, rate
-        )
-        return new, sums
-
-    def air_second(_):
-        return ocean, jnp.zeros((slots, 8, 128), jnp.float32)
-
-    ocean, sums = lax.cond(is_air, air_second, sea_second, 0)
-    own, far, air_scores, far_ocean, sea_parts = call(
+    count = slots * fields * members
+    anywhere = pl.BlockSpec(memory_space=pl.ANY)
+    inside = pl.BlockSpec(memory_space=pltpu.VMEM)
+    coefs_shape = (slots, fields, levels, rows, waves)
+    out_shapes = [coefs_shape, coefs_shape, (slots, 8, 128)]
+    out_shapes += [field.shape, field.shape, (tiles, slots, 8, 128)]
+    scratch = [field.shape, field.shape, (slots, rows, lon_count), (slots, 8, 128)]
+    sems = (tiles, count, count, count, tiles, comps, 5)
+    sems += (slots * fields,) * 3 + (tiles, tiles, tiles, comps)
+    own, far, air_scores, ocean, far_ocean, sea_parts = pl.pallas_call(
         functools.partial(return_kernel, sizes),
-        2,
-        [(slots, fields, levels, rows, waves)] * 2
-        + [(slots, 8, 128), field, (tiles, slots, 8, 128)],
-        (tiles, slots * fields * members, slots * fields * members)
-        + (slots * fields * members, tiles, comps, 3, 1, 1, tiles, tiles),
-        back,
-        air_point,
-        ocean,
-        sums,
-    )
+        out_shape=[jax.ShapeDtypeStruct(shape, jnp.float32) for shape in out_shapes],
+        in_specs=[anywhere] * 4 + [inside] * 5 + [scalar_spec()] * 2,
+        out_specs=[anywhere] * len(out_shapes),
+        scratch_shapes=[pltpu.VMEM(shape, jnp.float32) for shape in scratch]
+        + [pltpu.SemaphoreType.DMA((n,)) for n in sems],
+        compiler_params=pltpu.CompilerParams(
+            collective_id=2, has_side_effects=True, vmem_limit_bytes=40 * 1024 * 1024
+        ),
+    )(back, air_point, state, ocean, low, high, donors, land_sea, my_weights, blend, rate)
     parents = lax.dynamic_slice_in_dim(ancestry, member * slots, slots)
 
     inside = parents % slots

time: 207 us -> 178 us (0.86)
  local copies, waits for them, and re-layouts: 32.4 us -> 14.3 us
  Pallas kernels: 169 us -> 159 us
    pallas_call x4 -> x3, Pallas kernels: 138 us -> 57.5 us  [call(): pl.pallas_call(kernel, out_shape=[jax.ShapeDtypeStruct(out.shape, out.dty...]
    pallas_call x0 -> x2, Pallas kernels: none -> 69.9 us  [the longest x1 64.8 us: by_units(): pl.pallas_call(functools.partial(return_kernel, sizes), out_shape=[jax.Sh...]
    unnamed x53 -> x48, local copies, waits for them, and re-layouts: 18.5 us -> 8.4 us
    squeeze x1 -> x0, local copies, waits for them, and re-layouts: 4.92 us -> none  [by_units(): field = member_state[:, 0]]
    another operation x7 -> x4, local copies, waits for them, and re-layouts: 6.83 us -> 4.44 us
where the time goes in v2:
time: 178 us; the launch traced here: 177 us
  Pallas kernels  159 us (89%)
  local copies, waits for them, and re-layouts  14.3 us (8%)
  other arithmetic  2.42 us (1%)
    pallas_call x1, Pallas kernels, by_units(): pl.pallas_call(functools.partial(return_kernel, sizes), out_shape=[jax.Sh...  64.8 us
    pallas_call x3, Pallas kernels, call(): pl.pallas_call(kernel, out_shape=[jax.ShapeDtypeStruct(out.shape, out.dty...  57.5 us
    pallas_call x1, Pallas kernels, air_forward(): pl.pallas_call(air_kernel, grid=(slots, fields), out_shape=jax.ShapeDtype...  10.4 us
    pallas_call x1, Pallas kernels, resampled(): pl.pallas_call(kernel, grid_spec=pltpu.PrefetchScalarGridSpec(num_scalar_...  8.55 us
    unnamed x48, local copies, waits for them, and re-layouts  8.4 us
    pallas_call x1, Pallas kernels, to_coefs(): pl.pallas_call(to_coefs_kernel, grid=state.shape[:1], out_shape=[jax.Shap...  7.21 us
    pallas_call x1, Pallas kernels, to_grid(): pl.pallas_call(to_grid_kernel, grid=value.shape[:1], out_shape=jax.ShapeD...  5.59 us
    pallas_call x1, Pallas kernels, edge_rows(): pl.pallas_call(edge_kernel, grid=(slots, fields), out_shape=jax.ShapeDtyp...  5.18 us

profile of v2, /device:TPU:11, one launch (start us, length us, event | category | flops | bytes accessed | tf_op | source)
XLA Modules:
  0.0 176.9 jit_solution(5220596399447501071)
XLA Ops:
  0.7 0.7 compare_convert_fusion
  1.4 0.7 constant_dynamic-slice_fusion.weight_ref
  2.2 0.0 copy-start.19
  2.2 0.0 copy-start.21
  2.2 0.0 copy-start.22
  2.2 5.2 %shard_map.216.edge_ref = f32[2,4,2,4,768]{4,3,2,1,0:T(4,128)} custom-call(f32[2,4,4,48,768]{4,3,2,1,0:T(8,128)} %bitcast.19, f32[2,4,4,48,768]{4,3,2,1,0:T(8,128)} %bitcast.20), custom_call_target="tpu_custom_call" | custom-call | tf_op jit(solution)/shard_map/pallas_call | solution.py:734
  7.4 0.0 copy-done.19
  7.4 0.0 copy-done.21
  7.4 0.0 copy-done.22
  7.4 0.0 copy-start.17
  7.4 0.0 copy-start.18
  7.5 0.0 copy-start.20
  7.5 12.5 %shard_map.217 = (f32[2,48,768]{2,1,0:T(8,128)S(1)}, s32[48,768]{1,0:T(8,128)S(1)}, f32[4,4]{1,0:T(4,128)}, f32[1,4]{1,0:T(1,128)}, f32[2,4,4,768]{3,2,1,0:T(4,128)S(1)}, /*index=5*/f32[2,4,4,768]{3,2,1,0:T(4,128)S(1)}) custom-call(f32[2,4,4,48,768]{4,3,2,1,0:T(8,128)} %bitcast.21, s32[48,768]{1,0:T(8,128)S(1)} %bitcast.26, f32[4,4]{1,0:T(4,128)S(1)} %bitcast.30, ...), custom_call_target="tpu_custom_call" | custom-call | tf_op jit(solution)/shard_map/pallas_call | solution.py:510
  20.0 0.7 broadcast_select_fusion.5
  20.7 0.6 dynamic_slice.17.rate_ref
  21.3 0.1 fusion
  21.4 0.0 copy-done.17
  21.4 0.0 copy-done.18
  21.4 0.0 copy-done.20
  21.4 14.6 %conditional.2 = (f32[2,4,4,48,512]{4,3,2,1,0:T(8,128)}, f32[2,48,768]{2,1,0:T(8,128)}, f32[2,4,4,48,768]{4,3,2,1,0:T(8,128)}, f32[2,4,2,4,768]{4,3,2,1,0:T(4,128)}) conditional(s32[]{:T(128)} %convert_element_type.8, (pred[2,4,4,768]{3,2,1,0:T(4,128)(4,1)S(1)}, f32[2,4,4,768]{3,2,1,0:T(4,128)S(1)}, pred[2,4,4,768]{3,2,1,0:T(4,128)(4,1)S(1)}, ...), branch_computations={%region_0.1_spmd, %region_1.2_spmd} | conditional | flops 49152 | bytes 5210156 | solution.py:910
  21.4 10.4 %branch_1_fun.2 = f32[2,4,4,48,512]{4,3,2,1,0:T(8,128)} custom-call(f32[2,4,4,48,768]{4,3,2,1,0:T(8,128)} %get-tuple-element.94.field_ref, f32[2,48,768]{2,1,0:T(8,128)S(1)} %get-tuple-element.95.partner_ref, s32[48,768]{1,0:T(8,128)S(1)} %get-tuple-element.96.donors_ref, f32[4,4]{1,0:T(4,128)S(1)} %get-tuple-element.97.blend_ref, ...), custom_call_target="tpu_custom_call" | custom-call | tf_op jit(solution)/shard_map/cond/branch_1_fun/pallas_call | solution.py:642
  31.8 0.7 broadcast.41
  32.5 0.7 broadcast.39
  33.2 2.7 %broadcast.40 = f32[2,4,4,48,768]{4,3,2,1,0:T(8,128)} broadcast(f32[]{:T(128)} %constant.99.clone), dimensions={} | broadcast | bytes 4718596 | tf_op jit(solution)/shard_map/broadcast.6
  36.0 0.0 copy-start.4
  36.0 0.0 copy-start.7
  36.0 0.0 copy-start.8
  36.0 0.0 copy-start.10
  36.0 0.0 copy-start.13
  36.0 0.0 copy-start.15
  36.0 40.1 %shard_map.218 = (f32[2,384,512]{2,1,0:T(8,128)}, f32[384,768]{1,0:T(8,128)}, f32[4,4,48,512]{3,2,1,0:T(8,128)}, f32[2,4,4,768]{3,2,1,0:T(4,128)}, f32[2,4,4,768]{3,2,1,0:T(4,128)}) custom-call(f32[2,4,4,48,512]{4,3,2,1,0:T(8,128)} %get-tuple-element.140.c_ref, f32[2,48,768]{2,1,0:T(8,128)} %get-tuple-element.141.r_ref, ...), custom_call_target="tpu_custom_call" | custom-call | tf_op jit(solution)/shard_map/pallas_call | solution.py:510
  76.1 1.0 broadcast_select_fusion.2
  77.1 0.0 copy-done.4
  77.1 0.0 copy-done.7
  77.1 0.0 copy-done.8
  77.2 0.0 copy-done.9
  77.2 0.0 copy-done.10
  77.2 0.0 copy-done.13
  77.2 0.0 copy-done.15
  77.2 0.0 copy-start.5
  77.2 1.4 copy-done.5
  78.6 5.6 %shard_map.219.x_ref = f32[2,384,768]{2,1,0:T(8,128)S(1)} custom-call(f32[2,384,512]{2,1,0:T(8,128)S(1)} %copy-done.5, f32[256,512]{1,0:T(8,128)S(1)} %copy-done.4, f32[1]{0:T(128)} %dynamic_slice.17.rate_ref, bf16[256,384]{1,0:T(8,128)(2,1)S(1)} %copy-done.10, bf16[256,384]{1,0:T(8,128)(2,1)S(1)} %copy-done.9, bf16[384,256]{1,0:T(8,128)(2,1)S(1)} %copy-done.8, ...), custom_call_target="tpu_custom_call" | custom-call | tf_op jit(solution)/shard_map/pallas_call | solution.py:811
  84.2 0.0 copy-start
  84.2 1.4 copy-done
  85.6 4.9 %shard_map.220.o_ref = f32[2,384,768]{2,1,0:T(8,128)} custom-call(f32[2,384,768]{2,1,0:T(8,128)} %copy-done), custom_call_target="tpu_custom_call" | custom-call | tf_op jit(solution)/shard_map/pallas_call | solution.py:510
  90.5 0.0 copy-done.6
  90.5 0.0 copy-done.11
  90.5 0.0 copy-start.1
  90.5 1.7 copy-done.1
  92.2 1.7 copy-done.3
  93.9 7.2 %shard_map.221 = (f32[2,384,512]{2,1,0:T(8,128)S(1)}, f32[8,128]{1,0:T(8,128)S(1)}) custom-call(f32[2,384,768]{2,1,0:T(8,128)S(1)} %copy-done.1, f32[2,384,768]{2,1,0:T(8,128)S(1)} %copy-done.3, f32[384,768]{1,0:T(8,128)S(1)} %copy-done.6, f32[2,2]{1,0:T(2,128)S(1)} %get-tuple-element.175.here_ref, f32[2,2]{1,0:T(2,128)S(1)} %get-tuple-element.174.there_ref, ...), custom_call_target="tpu_custom_call" | custom-call | tf_op jit(solution)/shard_map/pallas_call | solution.py:824
  101.1 0.0 copy-done.2
  101.1 0.0 copy-start.14
  101.1 0.0 copy-start.16
  101.1 64.8 %shard_map.222 = (f32[2,4,4,48,512]{4,3,2,1,0:T(8,128)}, f32[2,4,4,48,512]{4,3,2,1,0:T(8,128)}, f32[2,8,128]{2,1,0:T(8,128)S(1)}, f32[2,4,4,48,768]{4,3,2,1,0:T(...) custom-call(f32[2,384,512]{2,1,0:T(8,128)S(1)} %get-tuple-element.147.f_ref, ...), custom_call_target="tpu_custom_call" | custom-call | tf_op jit(solution)/shard_map/pallas_call | solution.py:955
  165.9 0.0 copy-done.14
  165.9 0.0 copy-done.16
  165.9 8.8 %conditional.3 = (f32[2,1]{0,1:T(1,128)S(1)}, f32[2,1,4,4,48,768]{5,4,3,2,1,0:T(8,128)S(1)}) conditional(s32[]{:T(128)} %convert_element_type.8, (s32[2]{0:T(128)S(1)}, s32[2]{0:T(128)S(1)}, f32[2,4,4,48,768]{4,3,2,1,0:T(8,128)S(1)}, f32[2,4,4,48,768]{4,3,2,1,0:T(8,128)S(1)}, f32[8,2,8,128]{3,2,1,0:T(8,128)S(1)}) %tuple.28, (s32[2]{0:T(128)S(1)}, ...), branch_computations={%region_2.4_spmd, %region_4.5_spmd} | conditional | flops 16 | bytes 16416 | solution.py:982
  165.9 0.2 copy.27
  166.2 8.6 %branch_1_fun.3 = f32[2,4,4,48,768]{4,3,2,1,0:T(8,128)S(1)} custom-call(s32[2]{0:T(128)S(1)} %get-tuple-element.105.inside_ref, s32[2]{0:T(128)S(1)} %get-tuple-element.106.near_ref, f32[2,4,4,48,512]{4,3,2,1,0:T(8,128)} %get-tuple-element.107.own_ref, f32[2,4,4,48,512]{4,3,2,1,0:T(8,128)} %get-tuple-element.108.far_ref, ...), custom_call_target="tpu_custom_call" | custom-call | tf_op jit(solution)/shard_map/cond/branch_1_fun/pallas_call | solution.py:710
  174.7 0.0 copy-start.12
  174.8 0.0 copy-start.23
  174.8 2.2 %copy-done.12 = f32[2,1,4,4,48,768]{5,4,3,2,1,0:T(8,128)} copy-done((f32[2,1,4,4,48,768]{5,4,3,2,1,0:T(8,128)}, f32[2,1,4,4,48,768]{5,4,3,2,1,0:T(8,128)S(1)}, u32[]{:S(2)}) %copy-start.12) | copy-done | bytes 4718616
  176.9 0.0 copy-done.23
  (10 shorter events, 0.1 us)
Async XLA Ops:
  2.2 5.2 %copy-start.19 = (s32[1,48,768]{2,1,0:T(8,128)S(1)}, s32[1,48,768]{2,1,0:T(8,128)}, u32[]{:S(2)}) copy-start(s32[1,48,768]{2,1,0:T(8,128)} %param.28) | copy-start | bytes 442372
  2.2 5.2 %copy-start.21 = (f32[1,4,4]{2,1,0:T(4,128)S(1)}, f32[1,4,4]{2,1,0:T(4,128)}, u32[]{:S(2)}) copy-start(f32[1,4,4]{2,1,0:T(4,128)} %param.26) | copy-start | bytes 196
  2.2 5.2 %copy-start.22 = (f32[1,4]{1,0:T(1,128)S(1)}, f32[1,4]{1,0:T(1,128)}, u32[]{:S(2)}) copy-start(f32[1,4]{1,0:T(1,128)} %rate_ref.1) | copy-start | bytes 52
  7.4 13.9 %copy-start.17 = (bf16[768,512]{1,0:T(8,128)(2,1)S(1)}, bf16[768,512]{1,0:T(8,128)(2,1)}, u32[]{:S(2)}) copy-start(bf16[768,512]{1,0:T(8,128)(2,1)} %constant.123.clone.gl) | copy-start | bytes 2359300
  7.4 13.9 %copy-start.18 = (bf16[768,512]{1,0:T(8,128)(2,1)S(1)}, bf16[768,512]{1,0:T(8,128)(2,1)}, u32[]{:S(2)}) copy-start(bf16[768,512]{1,0:T(8,128)(2,1)} %constant.122.clone.gh) | copy-start | bytes 2359300
  7.5 13.9 %copy-start.20 = (s32[48,768]{1,0:T(8,128)S(1)}, s32[48,768]{1,0:T(8,128)}, u32[]{:S(2)}) copy-start(s32[48,768]{1,0:T(8,128)} %land_ref.1) | copy-start | bytes 442372
  36.0 41.1 %copy-start.4 = (f32[256,512]{1,0:T(8,128)S(1)}, f32[256,512]{1,0:T(8,128)}, u32[]{:S(2)}) copy-start(f32[256,512]{1,0:T(8,128)} %constant.120.clone.sq_ref) | copy-start | bytes 1572868
  36.0 41.1 %copy-start.7 = (bf16[384,256]{1,0:T(8,128)(2,1)S(1)}, bf16[384,256]{1,0:T(8,128)(2,1)}, u32[]{:S(2)}) copy-start(bf16[384,256]{1,0:T(8,128)(2,1)} %constant.119.clone.il) | copy-start | bytes 589828
  36.0 41.2 %copy-start.8 = (bf16[384,256]{1,0:T(8,128)(2,1)S(1)}, bf16[384,256]{1,0:T(8,128)(2,1)}, u32[]{:S(2)}) copy-start(bf16[384,256]{1,0:T(8,128)(2,1)} %constant.118.clone.ih) | copy-start | bytes 589828
  36.0 41.2 %copy-start.9 = (bf16[256,384]{1,0:T(8,128)(2,1)S(1)}, bf16[256,384]{1,0:T(8,128)(2,1)}, u32[]{:S(2)}) copy-start(bf16[256,384]{1,0:T(8,128)(2,1)} %constant.117.clone.fl) | copy-start | bytes 589828
  36.0 41.2 %copy-start.10 = (bf16[256,384]{1,0:T(8,128)(2,1)S(1)}, bf16[256,384]{1,0:T(8,128)(2,1)}, u32[]{:S(2)}) copy-start(bf16[256,384]{1,0:T(8,128)(2,1)} %constant.116.clone.fh) | copy-start | bytes 589828
  36.0 41.2 %copy-start.13 = (bf16[512,768]{1,0:T(8,128)(2,1)S(1)}, bf16[512,768]{1,0:T(8,128)(2,1)}, u32[]{:S(2)}) copy-start(bf16[512,768]{1,0:T(8,128)(2,1)} %constant.125.clone.gl) | copy-start | bytes 2359300
  36.0 41.2 %copy-start.15 = (bf16[512,768]{1,0:T(8,128)(2,1)S(1)}, bf16[512,768]{1,0:T(8,128)(2,1)}, u32[]{:S(2)}) copy-start(bf16[512,768]{1,0:T(8,128)(2,1)} %constant.124.clone.gh) | copy-start | bytes 2359300
  77.2 1.4 copy-start.5
  84.2 1.4 copy-start
  85.6 4.9 %copy-start.6 = (f32[384,768]{1,0:T(8,128)S(1)}, f32[384,768]{1,0:T(8,128)}, u32[]{:S(2)}) copy-start(f32[384,768]{1,0:T(8,128)} %get-tuple-element.145.sst_ref) | copy-start | bytes 3538948
  85.6 4.9 %copy-start.11 = (f32[384,128]{1,0:T(8,128)S(1)}, f32[384,128]{1,0:T(8,128)}, u32[]{:S(2)}) copy-start(f32[384,128]{1,0:T(8,128)} %constant.126.clone.w_ref) | copy-start | bytes 589828
  90.5 1.7 copy-start.1
  92.2 1.7 copy-start.3
  93.9 7.2 %copy-start.2 = (f32[2,384,768]{2,1,0:T(8,128)S(1)}, f32[2,384,768]{2,1,0:T(8,128)}, u32[]{:S(2)}) copy-start(f32[2,384,768]{2,1,0:T(8,128)} %copy-done) | copy-start | bytes 7077892
  101.1 64.8 %copy-start.14 = (bf16[512,768]{1,0:T(8,128)(2,1)S(1)}, bf16[512,768]{1,0:T(8,128)(2,1)}, u32[]{:S(2)}) copy-start(bf16[512,768]{1,0:T(8,128)(2,1)} %constant.125.clone.gl) | copy-start | bytes 2359300
  101.1 64.8 %copy-start.16 = (bf16[512,768]{1,0:T(8,128)(2,1)S(1)}, bf16[512,768]{1,0:T(8,128)(2,1)}, u32[]{:S(2)}) copy-start(bf16[512,768]{1,0:T(8,128)(2,1)} %constant.124.clone.gh) | copy-start | bytes 2359300
  174.7 2.2 %copy-start.12 = (f32[2,1,4,4,48,768]{5,4,3,2,1,0:T(8,128)}, f32[2,1,4,4,48,768]{5,4,3,2,1,0:T(8,128)S(1)}, u32[]{:S(2)}) copy-start(f32[2,1,4,4,48,768]{5,4,3,2,1,0:T(8,128)S(1)} %get-tuple-element.169) | copy-start | bytes 14155780
  174.8 2.2 %copy-start.23 = (f32[2,1]{0,1:T(1,128)}, f32[2,1]{0,1:T(1,128)S(1)}, u32[]{:S(2)}) copy-start(f32[2,1]{0,1:T(1,128)S(1)} %get-tuple-element.168) | copy-start | bytes 28

commit v3 on v2

--- a/solution.py
+++ b/solution.py
@@ -120,57 +120,40 @@
     return up, down
 
 
-def couple_kernel(
+def first_kernel(
     sizes,
     field_ref,
     donors_ref,
+    land_ref,
     blend_ref,
     rate_ref,
-    edge_ref,
-    partner_ref,
-    odonors_ref,
+    blend_any,
+    rate_any,
+    table_high,
+    table_low,
+    u_ref,
+    ru_ref,
+    new_ref,
+    low_out,
+    high_out,
     oblend_ref,
     orate_ref,
-    low_ref,
-    high_ref,
-    send,
-    recv,
+    before,
+    after,
+    coefs,
+    hops,
+    forced,
+    partner,
+    odonors,
+    looked,
+    edge,
+    low,
+    high,
+    load,
+    psend,
+    precv,
     esend,
     erecv,
-):
-    members, comps, fields, tiles, rows = sizes
-    m, y, t = here()
-    other = (m, 1 - y, t)
-    north, south = shores(y, t, tiles)
-    targets = [(m >= 0, other), (north, (m, y, t - 1)), (south, (m, y, t + 1))]
-    greet(targets, 1 + north.astype(jnp.int32) + south.astype(jnp.int32))
-    slots = partner_ref.shape[0]
-    pairs = [(field_ref.at[s, 0, 0], partner_ref.at[s]) for s in range(slots)]
-    pairs += [(donors_ref, odonors_ref), (blend_ref, oblend_ref), (rate_ref, orate_ref)]
-    copies = [remote(a, b, send.at[k], recv.at[k], other) for k, (a, b) in enumerate(pairs)]
-    up, down = edge_copies(edge_ref, low_ref, high_ref, esend, erecv, m, y, t)
-    for copy in copies:
-        copy.start()
-    pl.when(north)(up.start)
-    pl.when(south)(down.start)
-    for copy in copies:
-        copy.wait()
-    pl.when(north)(up.wait_send)
-    pl.when(south)(down.wait_send)
-    pl.when(south)(up.wait_recv)
-    pl.when(north)(down.wait_recv)
-
-
-def spread_kernel(
-    sizes,
-    c_ref,
-    r_ref,
-    edge_ref,
-    u_ref,
-    ru_ref,
-    h_ref,
-    low_ref,
-    high_ref,
     send,
     hsend,
     hrecv,
@@ -178,17 +161,18 @@
     recv,
     rrecv,
     loc,
-    esend,
-    erecv,
+    esend_2,
+    erecv_2,
 ):
     members, comps, fields, tiles, rows = sizes
     me = m, y, t = here()
-    per = c_ref.shape[2] // members
+    slots, _, levels = before.shape[:3]
+    per = levels // members
     unit_m, unit_f = t // fields, t % fields
     has_surface = jnp.logical_and(m == 0, unit_f == 0)
+    across = (m, 1 - y, t)
     north, south = shores(y, t, tiles)
-    targets = [(y == 1, (m, 0, t)), (north, (m, y, t - 1)), (south, (m, y, t + 1))]
-    up, down = edge_copies(edge_ref, low_ref, high_ref, esend, erecv, m, y, t)
+    targets = [(m >= 0, across), (north, (m, y, t - 1)), (south, (m, y, t + 1))]
     for j in range(tiles):
         source = (unit_m, y, j)
         targets.append((differs(source, me), source))
@@ -197,40 +181,19 @@
         targets.append((jnp.logical_and(has_surface, differs(source, me)), source))
     self_unit = (unit_m == m).astype(jnp.int32)
     self_surface = jnp.logical_and(has_surface, unit_m == m).astype(jnp.int32)
-    count = members * fields - self_unit + jnp.where(y == 0, 1, comps - self_surface)
+    count = 1 + members * fields - self_unit + jnp.where(y == 0, 0, comps - self_surface)
+    loading = pltpu.make_async_copy(field_ref, before, load.at[0])
+    loading.start()
     greet(targets, count + north.astype(jnp.int32) + south.astype(jnp.int32))
-    pl.when(north)(up.start)
-    pl.when(south)(down.start)
+
+    pairs = [(field_ref.at[s, 0, 0], partner.at[s]) for s in range(slots)]
+    pairs += [(donors_ref, odonors), (blend_any, oblend_ref), (rate_any, orate_ref)]
+    copies = [remote(p, q, psend.at[k], precv.at[k], across) for k, (p, q) in enumerate(pairs)]
+    up, down = edge_copies(edge.at[0], low, high, esend, erecv, m, y, t)
+    up_2, down_2 = edge_copies(edge.at[1], low_out, high_out, esend_2, erecv_2, m, y, t)
 
     def rows_of(j):
         return pl.ds(pl.multiple_of(j * rows, 8), rows)
-
-    pieces = [(f, c) for f in range(fields) for c in range(members)]
-
-    def place(k):
-        f, c = pieces[k]
-        return lax.rem(f + t, fields), c
-
-    def piece(k, ref):
-        f, c = place(k)
-        device = (c, y, m * fields + f)
-        src = ref.at[f, pl.ds(c * per, per)]
-        dst = u_ref.at[:, rows_of(t), :]
-        copy = remote(src, dst, send.at[k], recv.at[t], device)
-        return differs(device, me), copy, pltpu.make_async_copy(src, dst, loc.at[0])
-
-    def hop(k):
-        f, c = place(k)
-        part = (f, pl.ds(c * per, per))
-        return remote(
-            c_ref.at[(1,) + part], h_ref.at[part], hsend.at[k], hrecv.at[k], (m, 1 - y, t)
-        )
-
-    def surface(s):
-        device = (0, s, m * fields)
-        dst = ru_ref.at[rows_of(t), :]
-        copy = remote(r_ref.at[s], dst, rsend.at[s], rrecv.at[t], device)
-        return differs(device, me), copy, pltpu.make_async_copy(r_ref.at[s], dst, loc.at[1])
 
     def begin(parts):
         away, copy, local = parts
@@ -242,19 +205,136 @@
         pl.when(away)(copy.wait_send)
         pl.when(jnp.logical_not(away))(local.wait)
 
+    def piece(f, c, ref):
+        device = (c, y, m * fields + f)
+        src = ref.at[f, pl.ds(c * per, per)]
+        dst = u_ref.at[:, rows_of(t), :]
+        copy = remote(src, dst, send.at[f * members + c], recv.at[t], device)
+        return differs(device, me), copy, pltpu.make_async_copy(src, dst, loc.at[0])
+
+    def hop(f, c):
+        part = (f, pl.ds(c * per, per))
+        k = f * members + c
+        return remote(coefs.at[(1,) + part], hops.at[part], hsend.at[k], hrecv.at[k], across)
+
+    def surface(s):
+        device = (0, s, m * fields)
+        dst = ru_ref.at[rows_of(t), :]
+        copy = remote(looked.at[s], dst, rsend.at[s], rrecv.at[t], device)
+        return differs(device, me), copy, pltpu.make_async_copy(looked.at[s], dst, loc.at[1])
+
+    def field_at(j):
+        return jnp.where(j < fields - 1, 1 + lax.rem(j + t, fields - 1), 0)
+
+    def mixed(s, f, u):
+        total = blend_ref[u, 0] * before[s, f, 0]
+        for v in range(1, levels):
+            total = total + blend_ref[u, v] * before[s, f, v]
+        return forcing_rate * jnp.tanh(total)
+
+    def added(s):
+        received = lookup(partner[s], donors_ref[...])
+        return coupling_rate * (received - before[s, 0, 0])
+
+    def partner_arrives():
+        for copy in copies[:slots]:
+            copy.wait_recv()
+
+    for copy in copies:
+        copy.start()
+    loading.wait()
+    keep = pltpu.make_async_copy(after, new_ref, load.at[1])
+
     @pl.when(y == 0)
     def _():
-        for k in range(len(pieces)):
-            hop(k).start()
-            begin(piece(k, c_ref.at[0]))
+        def step(i, _):
+            j = lax.div(i, slots)
+            s, f = slots - 1 - lax.rem(i, slots), field_at(j)
+            for u in range(levels):
+                forced[u * rows : (u + 1) * rows] = before[s, f, u] + mixed(s, f, u)
+
+            pl.when(i == slots * (fields - 1))(partner_arrives)
+
+            @pl.when(j == fields - 1)
+            def _():
+                forced[:rows] += added(s)
+
+            result = dot3(forced[...], table_high, table_low)
+            coefs[s, f] = result.reshape(levels, rows, coefs.shape[-1])
+
+            @pl.when(s == 1)
+            def _():
+                for c in range(members):
+                    hop(f, c).start()
+
+            @pl.when(s == 0)
+            def _():
+                for c in range(members):
+                    begin(piece(f, c, coefs.at[0]))
+
+            return 0
+
+        lax.fori_loop(0, slots * fields, step, 0)
 
     @pl.when(y == 1)
     def _():
-        for s in range(comps):
-            begin(surface(s))
-        for k in range(len(pieces)):
-            hop(k).wait_recv()
-            begin(piece(k, h_ref))
+        pl.when(t == 0)(lambda: zero(low))
+        pl.when(t == tiles - 1)(lambda: zero(high))
+
+        def gather(i, _):
+            s, f = lax.div(i, fields), lax.rem(i, fields)
+            for u in range(levels):
+                edge[0, s, f, 0, u : u + 1] = before[s, f, u, :1]
+                edge[0, s, f, 1, u : u + 1] = before[s, f, u, rows - 1 :]
+            return 0
+
+        lax.fori_loop(0, slots * fields, gather, 0)
+        pl.when(north)(up.start)
+        pl.when(south)(down.start)
+        pl.when(south)(up.wait_recv)
+        pl.when(north)(down.wait_recv)
+        sea = land_ref[...] == 1
+
+        def step(j, _):
+            f = field_at(j)
+
+            pl.when(j == fields - 1)(partner_arrives)
+
+            def one(s, _):
+                for u in range(levels):
+                    value = before[s, f, u]
+                    total = value + mixed(s, f, u)
+                    ends = (low[s, f, u : u + 1], high[s, f, u : u + 1])
+                    total = total + rate_ref[0, f] * laplacian_of(value, *ends)
+                    after[s, f, u] = jnp.where(sea, total, value)
+
+                @pl.when(j == fields - 1)
+                def _():
+                    after[s, 0, 0] = after[s, 0, 0] + jnp.where(sea, added(s), 0.0)
+
+                for u in range(levels):
+                    edge[1, s, f, 0, u : u + 1] = after[s, f, u, :1]
+                    edge[1, s, f, 1, u : u + 1] = after[s, f, u, rows - 1 :]
+                return 0
+
+            lax.fori_loop(0, slots, one, 0)
+
+            @pl.when(j == fields - 1)
+            def _():
+                copies[slots].wait_recv()
+                for s in range(slots):
+                    looked[s] = lookup(after[s, 0, 0], odonors[...])
+                    begin(surface(s))
+                pl.when(north)(up_2.start)
+                pl.when(south)(down_2.start)
+                keep.start()
+
+            for c in range(members):
+                hop(f, c).wait_recv()
+                begin(piece(f, c, hops))
+            return 0
+
+        lax.fori_loop(0, fields, step, 0)
 
     for j in range(tiles):
         away = differs((unit_m, y, j), me)
@@ -269,21 +349,34 @@
 
     @pl.when(y == 0)
     def _():
-        for k in range(len(pieces)):
-            hop(k).wait_send()
-            end(piece(k, c_ref.at[0]))
+        copies[slots].wait_recv()
+        for f in range(fields):
+            for c in range(members):
+                hop(f, c).wait_send()
+                end(piece(f, c, coefs.at[0]))
 
     @pl.when(y == 1)
     def _():
         for s in range(comps):
             end(surface(s))
-        for k in range(len(pieces)):
-            end(piece(k, h_ref))
-
-    pl.when(north)(up.wait_send)
-    pl.when(south)(down.wait_send)
-    pl.when(south)(up.wait_recv)
-    pl.when(north)(down.wait_recv)
+        for f in range(fields):
+            for c in range(members):
+                end(piece(f, c, hops))
+        keep.wait()
+
+    for copy in copies:
+        copy.wait_send()
+    for copy in copies[slots + 1 :]:
+        copy.wait_recv()
+    for first, last in ((up, down), (up_2, down_2)):
+        pl.when(north)(first.wait_send)
+        pl.when(south)(last.wait_send)
+    pl.when(south)(up_2.wait_recv)
+    pl.when(north)(down_2.wait_recv)
+
+
+def zero(ref):
+    ref[...] = jnp.zeros(ref.shape, ref.dtype)
 
 
 def swap_kernel(sizes, x_ref, xo_ref, send, recv):
@@ -451,7 +544,10 @@
                     mixing = mixing + blend_ref[u, v] * before[s, f, v]
                 value = before[s, f, u]
                 forced = value + forcing_rate * jnp.tanh(mixing)
-                ends = (low_ref[s, f, u : u + 1], high_ref[s, f, u : u + 1])
+                ends = (
+                    jnp.where(t == 0, 0.0, low_ref[s, f, u : u + 1]),
+                    jnp.where(t == tiles - 1, 0.0, high_ref[s, f, u : u + 1]),
+                )
                 forced = forced + rate_ref[f] * laplacian_of(value, *ends)
                 after[s, f, u] = jnp.where(sea, forced, value)
 
@@ -556,64 +652,6 @@
     return result
 
 
-def mixed_level(blend_ref, field_ref, u):
-    levels = field_ref.shape[2]
-    total = blend_ref[u, 0] * field_ref[0, 0, 0]
-    for v in range(1, levels):
-        total = total + blend_ref[u, v] * field_ref[0, 0, v]
-    return forcing_rate * jnp.tanh(total)
-
-
-def air_kernel(field_ref, partner_ref, donors_ref, blend_ref, high_ref, low_ref, out_ref, forced):
-    levels, rows = field_ref.shape[2:4]
-    for u in range(levels):
-        forced[u * rows : (u + 1) * rows] = field_ref[0, 0, u] + mixed_level(blend_ref, field_ref, u)
-
-    @pl.when(pl.program_id(1) == 0)
-    def _():
-        received = lookup(partner_ref[0], donors_ref[...])
-        forced[:rows] += coupling_rate * (received - field_ref[0, 0, 0])
-
-    out_ref[0, 0] = dot3(forced[...], high_ref, low_ref).reshape(out_ref.shape[2:])
-
-
-def sea_kernel(
-    field_ref,
-    low_ref,
-    high_ref,
-    partner_ref,
-    donors_ref,
-    next_ref,
-    land_ref,
-    blend_ref,
-    rate_ref,
-    out_ref,
-    look_ref,
-    edge_ref,
-):
-    levels, rows, lon_count = field_ref.shape[2:]
-    rate = rate_ref[pl.program_id(1)]
-    sea = land_ref[...] == 1
-    first = pl.program_id(1) == 0
-    for u in range(levels):
-        value = field_ref[0, 0, u]
-        forced = value + mixed_level(blend_ref, field_ref, u)
-        ends = (low_ref[0, 0, u : u + 1], high_ref[0, 0, u : u + 1])
-        laplacian = laplacian_of(value, *ends)
-        if u == 0:
-            received = lookup(partner_ref[0], donors_ref[...])
-            extra = coupling_rate * (received - value)
-            forced = forced + jnp.where(first, extra, 0.0)
-        result = jnp.where(sea, forced + rate * laplacian, value)
-        out_ref[0, 0, u] = result
-        edge_ref[0, 0, 0, u : u + 1] = result[:1]
-        edge_ref[0, 0, 1, u : u + 1] = result[rows - 1 :]
-
-    @pl.when(first)
-    def _():
-        look_ref[0] = lookup(out_ref[0, 0, 0], next_ref[...])
-
-
 def whole_spec(array):
     zeros = (0,) * array.ndim
     return pl.BlockSpec(array.shape, lambda *_: zeros)
@@ -628,64 +666,7 @@
     return pl.BlockSpec((1, 1) + tuple(shape[2:]), lambda s, f, *_: (s, f) + zeros)
 
 
-def surface_spec(shape):
-    return pl.BlockSpec((1,) + tuple(shape[1:]), lambda s, f, *_: (s, 0, 0))
-
-
 large = pltpu.CompilerParams(vmem_limit_bytes=40 * 1024 * 1024)
-
-
-def air_forward(field, partner, donors, blend, table):
-    slots, fields, levels, rows, lon_count = field.shape
-    high, low = split_table(table)
-    shape = field.shape[:-1] + (table.shape[1],)
-    return pl.pallas_call(
-        air_kernel,
-        grid=(slots, fields),
-        out_shape=jax.ShapeDtypeStruct(shape, jnp.float32),
-        in_specs=[
-            state_spec(field.shape),
-            surface_spec(partner.shape),
-            whole_spec(donors),
-            scalar_spec(),
-            whole_spec(high),
-            whole_spec(low),
-        ],
-        out_specs=state_spec(shape),
-        scratch_shapes=[pltpu.VMEM((levels * rows, lon_count), jnp.float32)],
-        compiler_params=large,
-    )(field, partner, donors, blend, high, low)
-
-
-def sea_step(field, low, high, partner, donors, following, land_sea, blend, rate):
-    slots, fields, levels, rows, lon_count = field.shape
-    edge = (slots, fields, 2, levels, lon_count)
-    return pl.pallas_call(
-        sea_kernel,
-        grid=field.shape[:2],
-        out_shape=[
-            jax.ShapeDtypeStruct(field.shape, jnp.float32),
-            jax.ShapeDtypeStruct(partner.shape, jnp.float32),
-            jax.ShapeDtypeStruct(edge, jnp.float32),
-        ],
-        in_specs=[
-            state_spec(field.shape),
-            state_spec(low.shape),
-            state_spec(high.shape),
-            surface_spec(partner.shape),
-            whole_spec(donors),
-            whole_spec(following),
-            whole_spec(land_sea),
-            scalar_spec(),
-            scalar_spec(),
-        ],
-        out_specs=[
-            state_spec(field.shape),
-            surface_spec(partner.shape),
-            state_spec(edge),
-        ],
-        compiler_params=large,
-    )(field, low, high, partner, donors, following, land_sea, blend, rate)
 
 
 def air_last_kernel(inside_ref, near_ref, own_ref, far_ref, high_ref, low_ref, out_ref):
@@ -718,29 +699,6 @@
         out_shape=jax.ShapeDtypeStruct(shape, jnp.float32),
         compiler_params=large,
     )(inside, near, own, far, *tables)
-
-
-def edge_kernel(top_ref, bottom_ref, edge_ref):
-    for u in range(top_ref.shape[2]):
-        edge_ref[0, 0, 0, u : u + 1] = top_ref[0, 0, u, :1]
-        edge_ref[0, 0, 1, u : u + 1] = bottom_ref[0, 0, u, 7:]
-
-
-def edge_rows(field):
-    slots, fields, levels, rows, lon_count = field.shape
-    edge = (slots, fields, 2, levels, lon_count)
-    block = (1, 1, levels, 8, lon_count)
-    last = rows // 8 - 1
-    return pl.pallas_call(
-        edge_kernel,
-        grid=(slots, fields),
-        out_shape=jax.ShapeDtypeStruct(edge, jnp.float32),
-        in_specs=[
-            pl.BlockSpec(block, lambda s, f: (s, f, 0, 0, 0)),
-            pl.BlockSpec(block, lambda s, f: (s, f, 0, last, 0)),
-        ],
-        out_specs=state_spec(edge),
-    )(field, field)
 
 
 def left3(high_ref, low_ref, value):
@@ -870,54 +828,45 @@
     blend = layer_blend_operator[0]
     rate = coefficient[0]
     donors = interpolation_donor_meridians[0]
-    edge_shape = (slots, fields, 2, levels, lon_count)
-    halo_shape = (slots, fields, levels, lon_count)
-    edge = edge_rows(field)
-
-    def within(low, high):
-        return jnp.where(tile == 0, 0.0, low), jnp.where(tile == tiles - 1, 0.0, high)
-
-    partner, other_donors, other_blend, other_rate, low, high = call(
-        functools.partial(couple_kernel, sizes),
-        4,
-        [(slots, rows, lon_count), donors, blend, coefficient, halo_shape, halo_shape],
-        (slots + 3, slots + 3, 2, 2),
+    anywhere = pl.BlockSpec(memory_space=pl.ANY)
+    inside = pl.BlockSpec(memory_space=pltpu.VMEM)
+    halo = (slots, fields, levels, lon_count)
+    surface = (slots, rows, lon_count)
+    coefs_shape = (slots, fields, levels, rows, waves)
+    out_shapes = [(per, LAT, waves), (LAT, lon_count), field.shape, halo, halo]
+    out_shapes += [blend.shape, coefficient.shape]
+    scratch = [field.shape, field.shape, coefs_shape, coefs_shape[1:]]
+    scratch += [(levels * rows, lon_count), surface]
+    later = [surface, (2, slots, fields, 2, levels, lon_count), halo, halo]
+    pieces = members * fields
+    sems = (2, slots + 3, slots + 3, 2, 2, pieces, pieces, pieces, comps, tiles, tiles, 2, 2, 2)
+    gathered, sst, ocean, low, high, other_blend, other_rate = pl.pallas_call(
+        functools.partial(first_kernel, sizes),
+        out_shape=[jax.ShapeDtypeStruct(shape, jnp.float32) for shape in out_shapes],
+        in_specs=[anywhere, inside, inside]
+        + [scalar_spec()] * 2
+        + [anywhere] * 2
+        + [inside] * 2,
+        out_specs=[anywhere] * len(out_shapes),
+        scratch_shapes=[pltpu.VMEM(shape, jnp.float32) for shape in scratch]
+        + [pltpu.VMEM(donors.shape, jnp.int32)]
+        + [pltpu.VMEM(shape, jnp.float32) for shape in later]
+        + [pltpu.SemaphoreType.DMA((n,)) for n in sems],
+        compiler_params=pltpu.CompilerParams(
+            collective_id=0, has_side_effects=True, vmem_limit_bytes=48 * 1024 * 1024
+        ),
+    )(
         field,
         donors,
+        land_sea,
         blend,
         coefficient,
-        edge,
+        blend,
+        coefficient,
+        *split_table(lon_columns),
     )
-    low, high = within(low, high)
     air_blend = jnp.where(is_air, blend, other_blend)
     air_rate = jnp.where(is_air, rate, other_rate[0])
-
-    def air_first(_):
-        fourier = air_forward(field, partner, donors, blend, lon_columns)
-        return (
-            fourier,
-            jnp.zeros((slots, rows, lon_count), jnp.float32),
-            jnp.zeros(field.shape, jnp.float32),
-            jnp.zeros(edge_shape, jnp.float32),
-        )
-
-    def sea_first(_):
-        new, looked, edge = sea_step(
-            field, low, high, partner, donors, other_donors, land_sea, blend, rate
-        )
-        return jnp.zeros((slots, fields, levels, rows, waves), jnp.float32), looked, new, edge
-
-    fourier, looked, ocean, edge = lax.cond(is_air, air_first, sea_first, 0)
-    gathered, sst, _, low, high = call(
-        functools.partial(spread_kernel, sizes),
-        0,
-        [(per, LAT, waves), (LAT, lon_count), (fields, levels, rows, waves)] + [halo_shape] * 2,
-        (members * fields,) * 3 + (comps, tiles, tiles, 2, 2, 2),
-        fourier,
-        looked,
-        edge,
-    )
-    low, high = within(low, high)
     unit_field = tile % fields
     unit_rate = lax.dynamic_slice_in_dim(air_rate, unit_field, 1)
     state = to_grid(
@@ -944,9 +893,6 @@
     )
 
     count = slots * fields * members
-    anywhere = pl.BlockSpec(memory_space=pl.ANY)
-    inside = pl.BlockSpec(memory_space=pltpu.VMEM)
-    coefs_shape = (slots, fields, levels, rows, waves)
     out_shapes = [coefs_shape, coefs_shape, (slots, 8, 128)]
     out_shapes += [field.shape, field.shape, (tiles, slots, 8, 128)]
     scratch = [field.shape, field.shape, (slots, rows, lon_count), (slots, 8, 128)]

time: 178 us -> 179 us (level)
  local copies, waits for them, and re-layouts: 14.3 us -> 19.1 us
  Pallas kernels: 159 us -> 157 us
    pallas_call x3 -> x1, Pallas kernels: 57.5 us -> 4.89 us  [call(): pl.pallas_call(kernel, out_shape=[jax.ShapeDtypeStruct(out.shape, out.dty...]
    pallas_call x2 -> x1, Pallas kernels: 15.6 us -> 47.6 us  [by_units(): pl.pallas_call(functools.partial(first_kernel, sizes), out_shape=[jax.Sha...]
    pallas_call x1, Pallas kernels: 64.8 us -> 83.8 us  [by_units(): pl.pallas_call(functools.partial(return_kernel, sizes), out_shape=[jax.Sh...]
    unnamed x48 -> x70, local copies, waits for them, and re-layouts: 8.4 us -> 17.4 us
    another operation x4 -> x1, local copies, waits for them, and re-layouts: 4.44 us -> 0.22 us
where the time goes in v3:
time: 179 us; the launch traced here: 178 us
  Pallas kernels  157 us (88%)
  local copies, waits for them, and re-layouts  19.1 us (11%)
    pallas_call x1, Pallas kernels, by_units(): pl.pallas_call(functools.partial(return_kernel, sizes), out_shape=[jax.Sh...  83.8 us
    pallas_call x1, Pallas kernels, by_units(): pl.pallas_call(functools.partial(first_kernel, sizes), out_shape=[jax.Sha...  47.6 us
    unnamed x70, local copies, waits for them, and re-layouts  17.4 us
    pallas_call x1, Pallas kernels, resampled(): pl.pallas_call(kernel, grid_spec=pltpu.PrefetchScalarGridSpec(num_scalar_...  8.78 us
    pallas_call x1, Pallas kernels, to_coefs(): pl.pallas_call(to_coefs_kernel, grid=state.shape[:1], out_shape=[jax.Shap...  6.48 us
    pallas_call x1, Pallas kernels, to_grid(): pl.pallas_call(to_grid_kernel, grid=value.shape[:1], out_shape=jax.ShapeD...  5.76 us
    pallas_call x1, Pallas kernels, call(): pl.pallas_call(kernel, out_shape=[jax.ShapeDtypeStruct(out.shape, out.dty...  4.89 us

profile of v3, /device:TPU:11, one launch (start us, length us, event | category | flops | bytes accessed | tf_op | source)
XLA Modules:
  0.0 178.2 jit_solution(8975773523047461536)
XLA Ops:
  0.7 0.7 compare_convert_fusion
  1.4 0.7 constant_dynamic-slice_fusion.weight_ref
  2.2 0.0 copy-start.5
  2.2 1.1 copy-done.5
  3.3 0.0 copy-start.7
  3.3 1.1 copy-done.7
  4.4 0.9 copy-done.17
  5.3 0.9 copy-done.19
  6.2 0.7 copy-done.26
  6.9 0.7 copy-done.28
  7.6 0.0 copy-start.15
  7.6 0.0 copy-start.31
  7.6 0.0 copy-start.33
  7.6 47.6 %shard_map.216 = (f32[2,384,512]{2,1,0:T(8,128)S(1)}, f32[384,768]{1,0:T(8,128)S(1)}, f32[2,4,4,48,768]{4,3,2,1,0:T(8,128)}, f32[2,4,4,768]{3,2,1,0:T(4,128)S(1)...) custom-call(f32[2,4,4,48,768]{4,3,2,1,0:T(8,128)} %bitcast.27, s32[48,768]{1,0:T(8,128)S(1)} %bitcast.19, ...), custom_call_target="tpu_custom_call" | custom-call | tf_op jit(solution)/shard_map/pallas_call | solution.py:843
  55.3 0.0 copy-start.22
  55.3 0.6 copy-done.22
  55.9 0.6 copy-done.24
  56.5 0.7 dynamic_slice.17.rate_ref
  57.2 0.1 fusion
  57.3 0.0 copy-done.9
  57.3 0.0 copy-done.10
  57.3 0.0 copy-done.11
  57.3 0.0 copy-done.13
  57.3 0.0 copy-done.15
  57.3 0.0 copy-done.31
  57.3 0.0 copy-done.33
  57.3 0.0 copy-start.6
  57.4 0.0 copy-start.8
  57.4 5.8 %shard_map.217.x_ref = f32[2,384,768]{2,1,0:T(8,128)S(1)} custom-call(f32[2,384,512]{2,1,0:T(8,128)S(1)} %get-tuple-element.53.x_ref, f32[256,512]{1,0:T(8,128)S(1)} %copy-done.9, f32[1]{0:T(128)} %dynamic_slice.17.rate_ref, bf16[256,384]{1,0:T(8,128)(2,1)S(1)} %copy-done.15, bf16[256,384]{1,0:T(8,128)(2,1)S(1)} %copy-done.13, ...), custom_call_target="tpu_custom_call" | custom-call | tf_op jit(solution)/shard_map/pallas_call | solution.py:769
  63.1 0.0 copy-start
  63.2 1.4 copy-done
  64.5 4.9 %shard_map.218.o_ref = f32[2,384,768]{2,1,0:T(8,128)} custom-call(f32[2,384,768]{2,1,0:T(8,128)} %copy-done), custom_call_target="tpu_custom_call" | custom-call | tf_op jit(solution)/shard_map/pallas_call | solution.py:606
  69.4 0.0 copy-done.6
  69.5 0.0 copy-done.8
  69.5 0.0 copy-start.1
  69.5 1.7 copy-done.1
  71.1 1.7 copy-done.3
  72.8 0.9 copy-done.12
  73.7 0.9 copy-done.14
  74.7 0.9 copy-done.16
  75.6 0.9 copy-done.21
  76.5 0.0 copy-start.23
  76.5 0.0 copy-start.25
  76.5 0.0 copy-start.27
  76.6 0.0 copy-start.29
  76.6 6.5 %shard_map.219 = (f32[2,384,512]{2,1,0:T(8,128)S(1)}, f32[8,128]{1,0:T(8,128)S(1)}) custom-call(f32[2,384,768]{2,1,0:T(8,128)S(1)} %copy-done.1, f32[2,384,768]{2,1,0:T(8,128)S(1)} %copy-done.3, f32[384,768]{1,0:T(8,128)S(1)} %get-tuple-element.55.sst_ref, f32[2,2]{1,0:T(2,128)S(1)} %get-tuple-element.83.here_ref, f32[2,2]{1,0:T(2,128)S(1)} %get-tuple-element.82.there_ref, ...), custom_call_target="tpu_custom_call" | custom-call | tf_op jit(solution)/shard_map/pallas_call | solution.py:782
  83.1 0.0 copy-start.32
  83.1 0.0 copy-done.2
  83.1 0.0 copy-done.4
  83.1 0.0 copy-done.18
  83.1 0.0 copy-done.20
  83.1 0.0 copy-done.23
  83.1 0.0 copy-done.25
  83.1 0.0 copy-done.27
  83.1 0.0 copy-done.29
  83.1 83.8 %shard_map.220 = (f32[2,4,4,48,512]{4,3,2,1,0:T(8,128)}, f32[2,4,4,48,512]{4,3,2,1,0:T(8,128)}, f32[2,8,128]{2,1,0:T(8,128)S(1)}, f32[2,4,4,48,768]{4,3,2,1,0:T(...) custom-call(f32[2,384,512]{2,1,0:T(8,128)S(1)} %get-tuple-element.57.f_ref, ...), custom_call_target="tpu_custom_call" | custom-call | tf_op jit(solution)/shard_map/pallas_call | solution.py:901
  167.0 0.0 copy-done.32
  167.0 9.0 %conditional.1 = (f32[2,1]{0,1:T(1,128)S(1)}, f32[2,1,4,4,48,768]{5,4,3,2,1,0:T(8,128)S(1)}) conditional(s32[]{:T(128)} %convert_element_type.7, (s32[2]{0:T(128)S(1)}, s32[2]{0:T(128)S(1)}, f32[2,4,4,48,768]{4,3,2,1,0:T(8,128)S(1)}, f32[2,4,4,48,768]{4,3,2,1,0:T(8,128)S(1)}, f32[8,2,8,128]{3,2,1,0:T(8,128)S(1)}) %tuple.15, (s32[2]{0:T(128)S(1)}, ...), branch_computations={%region_0.2_spmd, %region_2.3_spmd} | conditional | flops 16 | bytes 16416 | solution.py:928
  167.0 0.2 copy.27
  167.3 8.8 %branch_1_fun.1 = f32[2,4,4,48,768]{4,3,2,1,0:T(8,128)S(1)} custom-call(s32[2]{0:T(128)S(1)} %get-tuple-element.29.inside_ref, s32[2]{0:T(128)S(1)} %get-tuple-element.30.near_ref, f32[2,4,4,48,512]{4,3,2,1,0:T(8,128)} %get-tuple-element.31.own_ref, f32[2,4,4,48,512]{4,3,2,1,0:T(8,128)} %get-tuple-element.32.far_ref, ...), custom_call_target="tpu_custom_call" | custom-call | tf_op jit(solution)/shard_map/cond/branch_1_fun/pallas_call | solution.py:691
  176.1 0.0 copy-start.30
  176.1 0.0 copy-start.34
  176.1 2.2 %copy-done.30 = f32[2,1,4,4,48,768]{5,4,3,2,1,0:T(8,128)} copy-done((f32[2,1,4,4,48,768]{5,4,3,2,1,0:T(8,128)}, f32[2,1,4,4,48,768]{5,4,3,2,1,0:T(8,128)S(1)}, u32[]{:S(2)}) %copy-start.30) | copy-done | bytes 4718616
  178.2 0.0 copy-done.34
  (22 shorter events, 0.0 us)
Async XLA Ops:
  2.2 1.1 copy-start.5
  3.3 1.1 copy-start.7
  4.4 0.9 copy-start.17
  5.3 0.9 copy-start.19
  6.2 0.7 copy-start.26
  6.9 0.7 copy-start.28
  7.6 49.7 %copy-start.9 = (f32[256,512]{1,0:T(8,128)S(1)}, f32[256,512]{1,0:T(8,128)}, u32[]{:S(2)}) copy-start(f32[256,512]{1,0:T(8,128)} %constant.108.clone.sq_ref) | copy-start | bytes 1572868
  7.6 49.7 %copy-start.10 = (bf16[384,256]{1,0:T(8,128)(2,1)S(1)}, bf16[384,256]{1,0:T(8,128)(2,1)}, u32[]{:S(2)}) copy-start(bf16[384,256]{1,0:T(8,128)(2,1)} %constant.107.clone.il) | copy-start | bytes 589828
  7.6 49.7 %copy-start.11 = (bf16[384,256]{1,0:T(8,128)(2,1)S(1)}, bf16[384,256]{1,0:T(8,128)(2,1)}, u32[]{:S(2)}) copy-start(bf16[384,256]{1,0:T(8,128)(2,1)} %constant.106.clone.ih) | copy-start | bytes 589828
  7.6 49.7 %copy-start.13 = (bf16[256,384]{1,0:T(8,128)(2,1)S(1)}, bf16[256,384]{1,0:T(8,128)(2,1)}, u32[]{:S(2)}) copy-start(bf16[256,384]{1,0:T(8,128)(2,1)} %constant.105.clone.fl) | copy-start | bytes 589828
  7.6 49.7 %copy-start.15 = (bf16[256,384]{1,0:T(8,128)(2,1)S(1)}, bf16[256,384]{1,0:T(8,128)(2,1)}, u32[]{:S(2)}) copy-start(bf16[256,384]{1,0:T(8,128)(2,1)} %constant.104.clone.fh) | copy-start | bytes 589828
  7.6 49.7 %copy-start.31 = (bf16[512,768]{1,0:T(8,128)(2,1)S(1)}, bf16[512,768]{1,0:T(8,128)(2,1)}, u32[]{:S(2)}) copy-start(bf16[512,768]{1,0:T(8,128)(2,1)} %constant.113.clone.gl) | copy-start | bytes 2359300
  7.6 49.7 %copy-start.33 = (bf16[512,768]{1,0:T(8,128)(2,1)S(1)}, bf16[512,768]{1,0:T(8,128)(2,1)}, u32[]{:S(2)}) copy-start(bf16[512,768]{1,0:T(8,128)(2,1)} %constant.112.clone.gh) | copy-start | bytes 2359300
  55.3 0.6 copy-start.22
  55.9 0.6 copy-start.24
  57.3 12.1 %copy-start.6 = (bf16[768,512]{1,0:T(8,128)(2,1)S(1)}, bf16[768,512]{1,0:T(8,128)(2,1)}, u32[]{:S(2)}) copy-start(bf16[768,512]{1,0:T(8,128)(2,1)} %constant.111.clone.table_low.gl) | copy-start | bytes 2359300
  57.4 12.1 %copy-start.8 = (bf16[768,512]{1,0:T(8,128)(2,1)S(1)}, bf16[768,512]{1,0:T(8,128)(2,1)}, u32[]{:S(2)}) copy-start(bf16[768,512]{1,0:T(8,128)(2,1)} %constant.110.clone.table_high.gh) | copy-start | bytes 2359300
  63.1 1.4 copy-start
  69.5 1.7 copy-start.1
  71.1 1.7 copy-start.3
  72.8 0.9 copy-start.12
  73.7 0.9 copy-start.14
  74.7 0.9 copy-start.16
  75.6 0.9 copy-start.21
  76.5 6.6 %copy-start.2 = (f32[2,384,768]{2,1,0:T(8,128)S(1)}, f32[2,384,768]{2,1,0:T(8,128)}, u32[]{:S(2)}) copy-start(f32[2,384,768]{2,1,0:T(8,128)} %copy-done) | copy-start | bytes 7077892
  76.5 6.6 %copy-start.4 = (f32[2,4,4,48,768]{4,3,2,1,0:T(8,128)S(1)}, f32[2,4,4,48,768]{4,3,2,1,0:T(8,128)}, u32[]{:S(2)}) copy-start(f32[2,4,4,48,768]{4,3,2,1,0:T(8,128)} %get-tuple-element.59.o_ref) | copy-start | bytes 14155780
  76.5 6.6 %copy-start.18 = (s32[1,48,768]{2,1,0:T(8,128)S(1)}, s32[1,48,768]{2,1,0:T(8,128)}, u32[]{:S(2)}) copy-start(s32[1,48,768]{2,1,0:T(8,128)} %param.26) | copy-start | bytes 442372
  76.5 6.6 %copy-start.20 = (s32[48,768]{1,0:T(8,128)S(1)}, s32[48,768]{1,0:T(8,128)}, u32[]{:S(2)}) copy-start(s32[48,768]{1,0:T(8,128)} %land_ref.3) | copy-start | bytes 442372
  76.5 6.6 %copy-start.23 = (f32[2,4,4,768]{3,2,1,0:T(4,128)S(1)}, f32[2,4,4,768]{3,2,1,0:T(4,128)}, u32[]{:S(2)}) copy-start(f32[2,4,4,768]{3,2,1,0:T(4,128)} %copy-done.22) | copy-start | bytes 294916
  76.5 6.6 %copy-start.25 = (f32[2,4,4,768]{3,2,1,0:T(4,128)S(1)}, f32[2,4,4,768]{3,2,1,0:T(4,128)}, u32[]{:S(2)}) copy-start(f32[2,4,4,768]{3,2,1,0:T(4,128)} %copy-done.24) | copy-start | bytes 294916
  76.5 6.6 %copy-start.27 = (f32[1,4,4]{2,1,0:T(4,128)S(1)}, f32[1,4,4]{2,1,0:T(4,128)}, u32[]{:S(2)}) copy-start(f32[1,4,4]{2,1,0:T(4,128)} %param.24) | copy-start | bytes 196
  76.6 6.6 %copy-start.29 = (f32[1,4]{1,0:T(1,128)S(1)}, f32[1,4]{1,0:T(1,128)}, u32[]{:S(2)}) copy-start(f32[1,4]{1,0:T(1,128)} %rate_any.1) | copy-start | bytes 52
  83.1 83.9 %copy-start.32 = (bf16[512,768]{1,0:T(8,128)(2,1)S(1)}, bf16[512,768]{1,0:T(8,128)(2,1)}, u32[]{:S(2)}) copy-start(bf16[512,768]{1,0:T(8,128)(2,1)} %constant.113.clone.gl) | copy-start | bytes 2359300
  176.1 2.2 %copy-start.30 = (f32[2,1,4,4,48,768]{5,4,3,2,1,0:T(8,128)}, f32[2,1,4,4,48,768]{5,4,3,2,1,0:T(8,128)S(1)}, u32[]{:S(2)}) copy-start(f32[2,1,4,4,48,768]{5,4,3,2,1,0:T(8,128)S(1)} %get-tuple-element.79) | copy-start | bytes 14155780
  176.1 2.2 %copy-start.34 = (f32[2,1]{0,1:T(1,128)}, f32[2,1]{0,1:T(1,128)S(1)}, u32[]{:S(2)}) copy-start(f32[2,1]{0,1:T(1,128)S(1)} %get-tuple-element.78) | copy-start | bytes 28

commit v4 on v3

--- a/solution.py
+++ b/solution.py
@@ -223,8 +223,12 @@
         copy = remote(looked.at[s], dst, rsend.at[s], rrecv.at[t], device)
         return differs(device, me), copy, pltpu.make_async_copy(looked.at[s], dst, loc.at[1])
 
+    late = 1 + lax.rem(t, fields - 1)
+
     def field_at(j):
-        return jnp.where(j < fields - 1, 1 + lax.rem(j + t, fields - 1), 0)
+        at = jnp.where(j > late, j - 1, j)
+        turn = lax.div(t, fields - 1) + t
+        return jnp.where(j == late, 0, 1 + lax.rem(at + turn, fields - 1))
 
     def mixed(s, f, u):
         total = blend_ref[u, 0] * before[s, f, 0]
@@ -248,14 +252,14 @@
     @pl.when(y == 0)
     def _():
         def step(i, _):
-            j = lax.div(i, slots)
-            s, f = slots - 1 - lax.rem(i, slots), field_at(j)
+            s, j = slots - 1 - lax.div(i, fields), lax.rem(i, fields)
+            f = field_at(j)
             for u in range(levels):
                 forced[u * rows : (u + 1) * rows] = before[s, f, u] + mixed(s, f, u)
 
-            pl.when(i == slots * (fields - 1))(partner_arrives)
-
-            @pl.when(j == fields - 1)
+            pl.when(i == late)(partner_arrives)
+
+            @pl.when(j == late)
             def _():
                 forced[:rows] += added(s)
 
@@ -298,7 +302,7 @@
         def step(j, _):
             f = field_at(j)
 
-            pl.when(j == fields - 1)(partner_arrives)
+            pl.when(j == late)(partner_arrives)
 
             def one(s, _):
                 for u in range(levels):
@@ -308,7 +312,7 @@
                     total = total + rate_ref[0, f] * laplacian_of(value, *ends)
                     after[s, f, u] = jnp.where(sea, total, value)
 
-                @pl.when(j == fields - 1)
+                @pl.when(j == late)
                 def _():
                     after[s, 0, 0] = after[s, 0, 0] + jnp.where(sea, added(s), 0.0)
 
@@ -319,12 +323,15 @@
 
             lax.fori_loop(0, slots, one, 0)
 
-            @pl.when(j == fields - 1)
+            @pl.when(j == late)
             def _():
                 copies[slots].wait_recv()
                 for s in range(slots):
                     looked[s] = lookup(after[s, 0, 0], odonors[...])
                     begin(surface(s))
+
+            @pl.when(j == fields - 1)
+            def _():
                 pl.when(north)(up_2.start)
                 pl.when(south)(down_2.start)
                 keep.start()
@@ -341,11 +348,11 @@
         part = u_ref.at[:, rows_of(j), :]
         arrival = remote(part, part, send.at[0], recv.at[j], me)
         pl.when(away)(arrival.wait_recv)
-        late = remote(
+        arrival = remote(
             ru_ref.at[rows_of(j), :], ru_ref.at[rows_of(j), :], rsend.at[0], rrecv.at[j], me
         )
         away = jnp.logical_and(has_surface, differs((unit_m, 1, j), me))
-        pl.when(away)(late.wait_recv)
+        pl.when(away)(arrival.wait_recv)
 
     @pl.when(y == 0)
     def _():
@@ -527,16 +534,21 @@
     @pl.when(y == 1)
     def _():
         load.wait()
-        for s in range(comps):
-            away = differs((0, s, m * fields), me)
-            arrival = remote(flux.at[s], flux.at[s], ssend.at[0], srecv.at[s], me)
-            pl.when(away)(arrival.wait_recv)
-            own = pltpu.make_async_copy(x_ref.at[0, pl.ds(0, rows), :], flux.at[s], loc.at[3])
-            pl.when(jnp.logical_not(away))(own.wait)
         sea = land_ref[...] == 1
 
+        def flux_arrives():
+            for s in range(comps):
+                away = differs((0, s, m * fields), me)
+                arrival = remote(flux.at[s], flux.at[s], ssend.at[0], srecv.at[s], me)
+                pl.when(away)(arrival.wait_recv)
+                part = x_ref.at[0, pl.ds(0, rows), :]
+                own = pltpu.make_async_copy(part, flux.at[s], loc.at[3])
+                pl.when(jnp.logical_not(away))(own.wait)
+
         def step(i, _):
-            s, f = lax.div(i, fields), lax.rem(i, fields)
+            j, s = lax.div(i, comps), lax.rem(i, comps)
+            f = lax.rem(j + 1, fields)
+            pl.when(i == comps * (fields - 1))(flux_arrives)
             levels = before.shape[2]
             for u in range(levels):
                 mixing = blend_ref[u, 0] * before[s, f, 0]
@@ -666,7 +678,7 @@
     return pl.BlockSpec((1, 1) + tuple(shape[2:]), lambda s, f, *_: (s, f) + zeros)
 
 
-large = pltpu.CompilerParams(vmem_limit_bytes=40 * 1024 * 1024)
+large = pltpu.CompilerParams(vmem_limit_bytes=24 * 1024 * 1024)
 
 
 def air_last_kernel(inside_ref, near_ref, own_ref, far_ref, high_ref, low_ref, out_ref):
@@ -853,7 +865,7 @@
         + [pltpu.VMEM(shape, jnp.float32) for shape in later]
         + [pltpu.SemaphoreType.DMA((n,)) for n in sems],
         compiler_params=pltpu.CompilerParams(
-            collective_id=0, has_side_effects=True, vmem_limit_bytes=48 * 1024 * 1024
+            collective_id=0, has_side_effects=True, vmem_limit_bytes=26 * 1024 * 1024
         ),
     )(
         field,
@@ -906,7 +918,7 @@
         scratch_shapes=[pltpu.VMEM(shape, jnp.float32) for shape in scratch]
         + [pltpu.SemaphoreType.DMA((n,)) for n in sems],
         compiler_params=pltpu.CompilerParams(
-            collective_id=2, has_side_effects=True, vmem_limit_bytes=40 * 1024 * 1024
+            collective_id=2, has_side_effects=True, vmem_limit_bytes=18 * 1024 * 1024
         ),
     )(back, air_point, state, ocean, low, high, donors, land_sea, my_weights, blend, rate)
     parents = lax.dynamic_slice_in_dim(ancestry, member * slots, slots)

time: 179 us -> 174 us (0.972)
  Pallas kernels: 157 us -> 150 us
  local copies, waits for them, and re-layouts: 19.1 us -> 22.5 us
    pallas_call x1, Pallas kernels: 83.8 us -> 73 us  [by_units(): pl.pallas_call(functools.partial(return_kernel, sizes), out_shape=[jax.Sh...]
    unnamed x70, local copies, waits for them, and re-layouts: 17.4 us -> 20.8 us
    pallas_call x1, Pallas kernels: 47.6 us -> 51 us  [by_units(): pl.pallas_call(functools.partial(first_kernel, sizes), out_shape=[jax.Sha...]
where the time goes in v4:
time: 174 us
  Pallas kernels  150 us (86%)
  local copies, waits for them, and re-layouts  22.5 us (13%)
    pallas_call x1, Pallas kernels, by_units(): pl.pallas_call(functools.partial(return_kernel, sizes), out_shape=[jax.Sh...  73 us
    pallas_call x1, Pallas kernels, by_units(): pl.pallas_call(functools.partial(first_kernel, sizes), out_shape=[jax.Sha...  51 us
    unnamed x70, local copies, waits for them, and re-layouts  20.8 us
    pallas_call x1, Pallas kernels, resampled(): pl.pallas_call(kernel, grid_spec=pltpu.PrefetchScalarGridSpec(num_scalar_...  8.49 us
    pallas_call x1, Pallas kernels, to_coefs(): pl.pallas_call(to_coefs_kernel, grid=state.shape[:1], out_shape=[jax.Shap...  6.39 us
    pallas_call x1, Pallas kernels, to_grid(): pl.pallas_call(to_grid_kernel, grid=value.shape[:1], out_shape=jax.ShapeD...  5.7 us
    pallas_call x1, Pallas kernels, call(): pl.pallas_call(kernel, out_shape=[jax.ShapeDtypeStruct(out.shape, out.dty...  4.89 us

profile of v4, /device:TPU:11, one launch (start us, length us, event | category | flops | bytes accessed | tf_op | source)
XLA Modules:
  0.0 173.8 jit_solution(6716532449183435883)
XLA Ops:
  0.7 0.7 compare_convert_fusion
  1.4 0.7 constant_dynamic-slice_fusion.weight_ref
  2.2 0.0 copy-start.3
  2.2 2.3 %copy-done.3 = f32[2,1,4,4,48,768]{5,4,3,2,1,0:T(8,128)S(1)} copy-done((f32[2,1,4,4,48,768]{5,4,3,2,1,0:T(8,128)S(1)}, f32[2,1,4,4,48,768]{5,4,3,2,1,0:T(8,128)}, u32[]{:S(2)}) %copy-start.3) | copy-done | bytes 4718616
  4.5 0.0 copy-start.5
  4.5 1.1 copy-done.5
  5.6 0.0 copy-start.7
  5.6 1.1 copy-done.7
  6.8 0.9 copy-done.16
  7.7 0.9 copy-done.18
  8.6 0.7 copy-done.23
  9.3 0.7 copy-done.25
  9.9 0.0 copy-start.15
  9.9 0.0 copy-start.28
  10.0 0.0 copy-start.30
  10.0 51.0 %shard_map.216 = (f32[2,384,512]{2,1,0:T(8,128)S(1)}, f32[384,768]{1,0:T(8,128)S(1)}, f32[2,4,4,48,768]{4,3,2,1,0:T(8,128)S(1)}, f32[2,4,4,768]{3,2,1,0:T(4,128)...) custom-call(f32[2,4,4,48,768]{4,3,2,1,0:T(8,128)S(1)} %bitcast.19, ...), custom_call_target="tpu_custom_call" | custom-call | tf_op jit(solution)/shard_map/pallas_call | solution.py:855
  61.0 0.0 copy-start.4
  61.0 2.2 %copy-done.4 = f32[2,4,4,48,768]{4,3,2,1,0:T(8,128)} copy-done((f32[2,4,4,48,768]{4,3,2,1,0:T(8,128)}, f32[2,4,4,48,768]{4,3,2,1,0:T(8,128)S(1)}, u32[]{:S(2)}) %copy-start.4) | copy-done | bytes 4718616
  63.2 1.1 copy-done.10
  64.2 0.6 copy-done.21
  64.9 0.6 dynamic_slice.17.rate_ref
  65.5 0.1 fusion
  65.6 0.0 copy-done.9
  65.6 0.0 copy-done.12
  65.6 0.0 copy-done.13
  65.6 0.0 copy-done.14
  65.6 0.0 copy-done.15
  65.6 0.0 copy-done.28
  65.6 0.0 copy-done.30
  65.6 0.0 copy-start.6
  65.7 0.0 copy-start.8
  65.7 5.7 %shard_map.217.x_ref = f32[2,384,768]{2,1,0:T(8,128)S(1)} custom-call(f32[2,384,512]{2,1,0:T(8,128)S(1)} %get-tuple-element.53.x_ref, f32[256,512]{1,0:T(8,128)S(1)} %copy-done.9, f32[1]{0:T(128)} %dynamic_slice.17.rate_ref, bf16[256,384]{1,0:T(8,128)(2,1)S(1)} %copy-done.15, bf16[256,384]{1,0:T(8,128)(2,1)S(1)} %copy-done.14, ...), custom_call_target="tpu_custom_call" | custom-call | tf_op jit(solution)/shard_map/pallas_call | solution.py:781
  71.4 0.0 copy-start
  71.4 1.4 copy-done
  72.8 4.9 %shard_map.218.o_ref = f32[2,384,768]{2,1,0:T(8,128)} custom-call(f32[2,384,768]{2,1,0:T(8,128)} %copy-done), custom_call_target="tpu_custom_call" | custom-call | tf_op jit(solution)/shard_map/pallas_call | solution.py:618
  77.7 0.0 copy-done.6
  77.7 0.0 copy-done.8
  77.7 0.0 copy-start.1
  77.7 1.7 copy-done.1
  79.4 1.7 copy-done.2
  81.1 1.3 copy-done.11
  82.3 0.9 copy-done.20
  83.3 0.0 copy-start.24
  83.3 0.0 copy-start.26
  83.3 6.4 %shard_map.219 = (f32[2,384,512]{2,1,0:T(8,128)S(1)}, f32[8,128]{1,0:T(8,128)S(1)}) custom-call(f32[2,384,768]{2,1,0:T(8,128)S(1)} %copy-done.1, f32[2,384,768]{2,1,0:T(8,128)S(1)} %copy-done.2, f32[384,768]{1,0:T(8,128)S(1)} %copy-done.11, f32[2,2]{1,0:T(2,128)S(1)} %get-tuple-element.83.here_ref, f32[2,2]{1,0:T(2,128)S(1)} %get-tuple-element.82.there_ref, ...), custom_call_target="tpu_custom_call" | custom-call | tf_op jit(solution)/shard_map/pallas_call | solution.py:794
  89.7 0.0 copy-start.29
  89.7 0.0 copy-start.31
  89.7 0.0 slice-done
  89.7 0.0 slice-done.1
  89.7 0.0 copy-done.17
  89.7 0.0 copy-done.19
  89.8 0.0 copy-done.22
  89.8 0.0 copy-done.24
  89.8 0.0 copy-done.26
  89.8 73.0 %shard_map.220 = (f32[2,4,4,48,512]{4,3,2,1,0:T(8,128)}, f32[2,4,4,48,512]{4,3,2,1,0:T(8,128)}, f32[2,8,128]{2,1,0:T(8,128)S(1)}, f32[2,4,4,48,768]{4,3,2,1,0:T(...) custom-call(f32[2,384,512]{2,1,0:T(8,128)S(1)} %get-tuple-element.57.f_ref, ...), custom_call_target="tpu_custom_call" | custom-call | tf_op jit(solution)/shard_map/pallas_call | solution.py:913
  162.8 0.0 copy-done.29
  162.8 0.0 copy-done.31
  162.8 8.8 %conditional.1 = (f32[2,1]{0,1:T(1,128)S(1)}, f32[2,1,4,4,48,768]{5,4,3,2,1,0:T(8,128)S(1)}) conditional(s32[]{:T(128)} %convert_element_type.7, (s32[2]{0:T(128)S(1)}, s32[2]{0:T(128)S(1)}, f32[2,4,4,48,768]{4,3,2,1,0:T(8,128)S(1)}, f32[2,4,4,48,768]{4,3,2,1,0:T(8,128)S(1)}, f32[8,2,8,128]{3,2,1,0:T(8,128)S(1)}) %tuple.15, (s32[2]{0:T(128)S(1)}, ...), branch_computations={%region_0.2_spmd, %region_2.3_spmd} | conditional | flops 16 | bytes 16416 | solution.py:940
  162.9 0.2 copy.27
  163.1 8.5 %branch_1_fun.1 = f32[2,4,4,48,768]{4,3,2,1,0:T(8,128)S(1)} custom-call(s32[2]{0:T(128)S(1)} %get-tuple-element.29.inside_ref, s32[2]{0:T(128)S(1)} %get-tuple-element.30.near_ref, f32[2,4,4,48,512]{4,3,2,1,0:T(8,128)} %get-tuple-element.31.own_ref, f32[2,4,4,48,512]{4,3,2,1,0:T(8,128)} %get-tuple-element.32.far_ref, ...), custom_call_target="tpu_custom_call" | custom-call | tf_op jit(solution)/shard_map/cond/branch_1_fun/pallas_call | solution.py:703
  171.6 0.0 copy-start.27
  171.6 0.0 copy-start.32
  171.6 2.2 %copy-done.27 = f32[2,1,4,4,48,768]{5,4,3,2,1,0:T(8,128)} copy-done((f32[2,1,4,4,48,768]{5,4,3,2,1,0:T(8,128)}, f32[2,1,4,4,48,768]{5,4,3,2,1,0:T(8,128)S(1)}, u32[]{:S(2)}) %copy-start.27) | copy-done | bytes 4718616
  173.8 0.0 copy-done.32
  (23 shorter events, 0.0 us)
Async XLA Ops:
  2.2 2.3 %copy-start.3 = (f32[2,1,4,4,48,768]{5,4,3,2,1,0:T(8,128)S(1)}, f32[2,1,4,4,48,768]{5,4,3,2,1,0:T(8,128)}, u32[]{:S(2)}) copy-start(f32[2,1,4,4,48,768]{5,4,3,2,1,0:T(8,128)} %param.23) | copy-start | bytes 14155780
  4.5 1.1 copy-start.5
  5.6 1.1 copy-start.7
  6.8 0.9 copy-start.16
  7.7 0.9 copy-start.18
  8.6 0.7 copy-start.23
  9.3 0.7 copy-start.25
  9.9 55.7 %copy-start.9 = (f32[256,512]{1,0:T(8,128)S(1)}, f32[256,512]{1,0:T(8,128)}, u32[]{:S(2)}) copy-start(f32[256,512]{1,0:T(8,128)} %constant.108.clone.sq_ref) | copy-start | bytes 1572868
  9.9 55.7 %copy-start.12 = (bf16[384,256]{1,0:T(8,128)(2,1)S(1)}, bf16[384,256]{1,0:T(8,128)(2,1)}, u32[]{:S(2)}) copy-start(bf16[384,256]{1,0:T(8,128)(2,1)} %constant.107.clone.il) | copy-start | bytes 589828
  9.9 55.7 %copy-start.13 = (bf16[384,256]{1,0:T(8,128)(2,1)S(1)}, bf16[384,256]{1,0:T(8,128)(2,1)}, u32[]{:S(2)}) copy-start(bf16[384,256]{1,0:T(8,128)(2,1)} %constant.106.clone.ih) | copy-start | bytes 589828
  9.9 55.7 %copy-start.14 = (bf16[256,384]{1,0:T(8,128)(2,1)S(1)}, bf16[256,384]{1,0:T(8,128)(2,1)}, u32[]{:S(2)}) copy-start(bf16[256,384]{1,0:T(8,128)(2,1)} %constant.105.clone.fl) | copy-start | bytes 589828
  9.9 55.7 %copy-start.15 = (bf16[256,384]{1,0:T(8,128)(2,1)S(1)}, bf16[256,384]{1,0:T(8,128)(2,1)}, u32[]{:S(2)}) copy-start(bf16[256,384]{1,0:T(8,128)(2,1)} %constant.104.clone.fh) | copy-start | bytes 589828
  9.9 55.7 %copy-start.28 = (bf16[512,768]{1,0:T(8,128)(2,1)S(1)}, bf16[512,768]{1,0:T(8,128)(2,1)}, u32[]{:S(2)}) copy-start(bf16[512,768]{1,0:T(8,128)(2,1)} %constant.113.clone.gl) | copy-start | bytes 2359300
  10.0 55.7 %copy-start.30 = (bf16[512,768]{1,0:T(8,128)(2,1)S(1)}, bf16[512,768]{1,0:T(8,128)(2,1)}, u32[]{:S(2)}) copy-start(bf16[512,768]{1,0:T(8,128)(2,1)} %constant.112.clone.gh) | copy-start | bytes 2359300
  61.0 2.2 %copy-start.4 = (f32[2,4,4,48,768]{4,3,2,1,0:T(8,128)}, f32[2,4,4,48,768]{4,3,2,1,0:T(8,128)S(1)}, u32[]{:S(2)}) copy-start(f32[2,4,4,48,768]{4,3,2,1,0:T(8,128)S(1)} %get-tuple-element.59.o_ref) | copy-start | bytes 14155780
  63.2 1.1 copy-start.10
  64.2 0.6 copy-start.21
  65.6 12.1 %copy-start.6 = (bf16[768,512]{1,0:T(8,128)(2,1)S(1)}, bf16[768,512]{1,0:T(8,128)(2,1)}, u32[]{:S(2)}) copy-start(bf16[768,512]{1,0:T(8,128)(2,1)} %constant.111.clone.table_low.gl) | copy-start | bytes 2359300
  65.7 12.1 %copy-start.8 = (bf16[768,512]{1,0:T(8,128)(2,1)S(1)}, bf16[768,512]{1,0:T(8,128)(2,1)}, u32[]{:S(2)}) copy-start(bf16[768,512]{1,0:T(8,128)(2,1)} %constant.110.clone.table_high.gh) | copy-start | bytes 2359300
  71.4 1.4 copy-start
  72.8 16.9 %slice-start = ((s8[4718592]{0:T(1024)(128)(4,1)}), s8[524288]{0:T(1024)(128)(4,1)S(1)}, s32[]{:S(2)}) async-start(s8[4718592]{0:T(1024)(128)(4,1)} %bitcast.20), calls=%async_computation | async-start | bytes 1048576
  77.7 1.7 copy-start.1
  79.4 1.7 copy-start.2
  81.1 1.3 copy-start.11
  82.3 0.9 copy-start.20
  83.3 6.5 %slice-start.1 = ((s8[4718592]{0:T(1024)(128)(4,1)}), s8[4194304]{0:T(1024)(128)(4,1)S(1)}, s32[]{:S(2)}) async-start(s8[4718592]{0:T(1024)(128)(4,1)} %bitcast.20), calls=%async_computation.1 | async-start | bytes 8388608
  83.3 6.5 %copy-start.17 = (s32[1,48,768]{2,1,0:T(8,128)S(1)}, s32[1,48,768]{2,1,0:T(8,128)}, u32[]{:S(2)}) copy-start(s32[1,48,768]{2,1,0:T(8,128)} %param.26) | copy-start | bytes 442372
  83.3 6.5 %copy-start.19 = (s32[48,768]{1,0:T(8,128)S(1)}, s32[48,768]{1,0:T(8,128)}, u32[]{:S(2)}) copy-start(s32[48,768]{1,0:T(8,128)} %land_ref.3) | copy-start | bytes 442372
  83.3 6.5 %copy-start.22 = (f32[2,4,4,768]{3,2,1,0:T(4,128)S(1)}, f32[2,4,4,768]{3,2,1,0:T(4,128)}, u32[]{:S(2)}) copy-start(f32[2,4,4,768]{3,2,1,0:T(4,128)} %copy-done.21) | copy-start | bytes 294916
  83.3 6.5 %copy-start.24 = (f32[1,4,4]{2,1,0:T(4,128)S(1)}, f32[1,4,4]{2,1,0:T(4,128)}, u32[]{:S(2)}) copy-start(f32[1,4,4]{2,1,0:T(4,128)} %param.24) | copy-start | bytes 196
  83.3 6.5 %copy-start.26 = (f32[1,4]{1,0:T(1,128)S(1)}, f32[1,4]{1,0:T(1,128)}, u32[]{:S(2)}) copy-start(f32[1,4]{1,0:T(1,128)} %rate_any.1) | copy-start | bytes 52
  89.7 73.1 %copy-start.29 = (bf16[512,768]{1,0:T(8,128)(2,1)S(1)}, bf16[512,768]{1,0:T(8,128)(2,1)}, u32[]{:S(2)}) copy-start(bf16[512,768]{1,0:T(8,128)(2,1)} %constant.113.clone.gl) | copy-start | bytes 2359300
  89.7 73.1 %copy-start.31 = (bf16[512,768]{1,0:T(8,128)(2,1)S(1)}, bf16[512,768]{1,0:T(8,128)(2,1)}, u32[]{:S(2)}) copy-start(bf16[512,768]{1,0:T(8,128)(2,1)} %constant.112.clone.gh) | copy-start | bytes 2359300
  171.6 2.2 %copy-start.27 = (f32[2,1,4,4,48,768]{5,4,3,2,1,0:T(8,128)}, f32[2,1,4,4,48,768]{5,4,3,2,1,0:T(8,128)S(1)}, u32[]{:S(2)}) copy-start(f32[2,1,4,4,48,768]{5,4,3,2,1,0:T(8,128)S(1)} %get-tuple-element.79) | copy-start | bytes 14155780
  171.6 2.2 %copy-start.32 = (f32[2,1]{0,1:T(1,128)}, f32[2,1]{0,1:T(1,128)S(1)}, u32[]{:S(2)}) copy-start(f32[2,1]{0,1:T(1,128)S(1)} %get-tuple-element.78) | copy-start | bytes 28

commit v5 on v4

--- a/solution.py
+++ b/solution.py
@@ -678,7 +678,7 @@
     return pl.BlockSpec((1, 1) + tuple(shape[2:]), lambda s, f, *_: (s, f) + zeros)
 
 
-large = pltpu.CompilerParams(vmem_limit_bytes=24 * 1024 * 1024)
+large = pltpu.CompilerParams(vmem_limit_bytes=60 * 1024 * 1024)
 
 
 def air_last_kernel(inside_ref, near_ref, own_ref, far_ref, high_ref, low_ref, out_ref):
@@ -865,7 +865,7 @@
         + [pltpu.VMEM(shape, jnp.float32) for shape in later]
         + [pltpu.SemaphoreType.DMA((n,)) for n in sems],
         compiler_params=pltpu.CompilerParams(
-            collective_id=0, has_side_effects=True, vmem_limit_bytes=26 * 1024 * 1024
+            collective_id=0, has_side_effects=True, vmem_limit_bytes=60 * 1024 * 1024
         ),
     )(
         field,
@@ -918,7 +918,7 @@
         scratch_shapes=[pltpu.VMEM(shape, jnp.float32) for shape in scratch]
         + [pltpu.SemaphoreType.DMA((n,)) for n in sems],
         compiler_params=pltpu.CompilerParams(
-            collective_id=2, has_side_effects=True, vmem_limit_bytes=18 * 1024 * 1024
+            collective_id=2, has_side_effects=True, vmem_limit_bytes=60 * 1024 * 1024
         ),
     )(back, air_point, state, ocean, low, high, donors, land_sea, my_weights, blend, rate)
     parents = lax.dynamic_slice_in_dim(ancestry, member * slots, slots)

time: 174 us -> 167 us (0.960)
  local copies, waits for them, and re-layouts: 22.5 us -> 4.9 us
  Pallas kernels: 150 us -> 159 us
    unnamed x70 -> x10, local copies, waits for them, and re-layouts: 20.8 us -> 0.54 us
    pallas_call x1, Pallas kernels: 6.39 us -> 10.2 us  [to_coefs(): pl.pallas_call(to_coefs_kernel, grid=state.shape[:1], out_shape=[jax.Shap...]
    pallas_call x1, Pallas kernels: 5.7 us -> 8.12 us  [to_grid(): pl.pallas_call(to_grid_kernel, grid=value.shape[:1], out_shape=jax.ShapeD...]
where the time goes in v5:
time: 167 us; the launch traced here: 166 us
  Pallas kernels  159 us (95%)
  local copies, waits for them, and re-layouts  4.9 us (3%)
    pallas_call x1, Pallas kernels, by_units(): pl.pallas_call(functools.partial(return_kernel, sizes), out_shape=[jax.Sh...  74 us
    pallas_call x1, Pallas kernels, by_units(): pl.pallas_call(functools.partial(first_kernel, sizes), out_shape=[jax.Sha...  51.8 us
    pallas_call x1, Pallas kernels, to_coefs(): pl.pallas_call(to_coefs_kernel, grid=state.shape[:1], out_shape=[jax.Shap...  10.2 us
    pallas_call x1, Pallas kernels, resampled(): pl.pallas_call(kernel, grid_spec=pltpu.PrefetchScalarGridSpec(num_scalar_...  9.82 us
    pallas_call x1, Pallas kernels, to_grid(): pl.pallas_call(to_grid_kernel, grid=value.shape[:1], out_shape=jax.ShapeD...  8.12 us
    pallas_call x1, Pallas kernels, call(): pl.pallas_call(kernel, out_shape=[jax.ShapeDtypeStruct(out.shape, out.dty...  4.89 us

profile of v5, /device:TPU:11, one launch (start us, length us, event | category | flops | bytes accessed | tf_op | source)
XLA Modules:
  0.0 166.0 jit_solution(13715317981597348976)
XLA Ops:
  0.6 0.0 copy-start
  0.6 0.0 copy-start.1
  0.7 0.0 copy-start.3
  0.7 0.0 copy-start.2
  0.7 0.8 compare_convert_fusion
  1.6 1.3 constant_dynamic-slice_fusion.weight_ref
  2.9 51.8 %shard_map.216 = (f32[2,384,512]{2,1,0:T(8,128)}, f32[384,768]{1,0:T(8,128)}, f32[2,4,4,48,768]{4,3,2,1,0:T(8,128)}, f32[2,4,4,768]{3,2,1,0:T(4,128)}, f32[2,4,4...) custom-call(f32[2,4,4,48,768]{4,3,2,1,0:T(8,128)} %bitcast.21, s32[48,768]{1,0:T(8,128)} %bitcast.22, ...), custom_call_target="tpu_custom_call" | custom-call | tf_op jit(solution)/shard_map/pallas_call | solution.py:855
  54.7 0.0 copy-done.3
  54.7 0.6 broadcast_select_fusion.1
  55.4 0.6 dynamic_slice.17.rate_ref
  56.0 0.0 copy-done.2
  56.0 0.7 fusion
  56.7 0.0 copy-done
  56.7 0.0 copy-done.1
  56.7 8.1 %shard_map.217.x_ref = f32[2,384,768]{2,1,0:T(8,128)} custom-call(f32[2,384,512]{2,1,0:T(8,128)} %get-tuple-element.53.x_ref, f32[256,512]{1,0:T(8,128)} %constant.108.clone.sq_ref, f32[1]{0:T(128)} %dynamic_slice.17.rate_ref, bf16[256,384]{1,0:T(8,128)(2,1)} %constant.104.clone.fh, bf16[256,384]{1,0:T(8,128)(2,1)} %constant.105.clone.fl, ...), custom_call_target="tpu_custom_call" | custom-call | tf_op jit(solution)/shard_map/pallas_call | solution.py:781
  64.8 4.9 %shard_map.218.o_ref = f32[2,384,768]{2,1,0:T(8,128)} custom-call(f32[2,384,768]{2,1,0:T(8,128)} %shard_map.217.x_ref), custom_call_target="tpu_custom_call" | custom-call | tf_op jit(solution)/shard_map/pallas_call | solution.py:618
  69.7 10.2 %shard_map.219 = (f32[2,384,512]{2,1,0:T(8,128)}, f32[8,128]{1,0:T(8,128)}) custom-call(f32[2,384,768]{2,1,0:T(8,128)} %shard_map.217.x_ref, f32[2,384,768]{2,1,0:T(8,128)} %shard_map.218.o_ref, f32[384,768]{1,0:T(8,128)} %get-tuple-element.55.sst_ref, f32[2,2]{1,0:T(2,128)} %get-tuple-element.83.here_ref, f32[2,2]{1,0:T(2,128)} %get-tuple-element.82.there_ref, ...), custom_call_target="tpu_custom_call" | custom-call | tf_op jit(solution)/shard_map/pallas_call | solution.py:794
  79.9 74.0 %shard_map.220 = (f32[2,4,4,48,512]{4,3,2,1,0:T(8,128)S(1)}, f32[2,4,4,48,512]{4,3,2,1,0:T(8,128)}, f32[2,8,128]{2,1,0:T(8,128)S(1)}, f32[2,4,4,48,768]{4,3,2,1,...) custom-call(f32[2,384,512]{2,1,0:T(8,128)} %get-tuple-element.57.f_ref, ...), custom_call_target="tpu_custom_call" | custom-call | tf_op jit(solution)/shard_map/pallas_call | solution.py:913
  153.9 11.6 %conditional.1 = (f32[2,1]{0,1:T(1,128)S(1)}, f32[2,1,4,4,48,768]{5,4,3,2,1,0:T(8,128)}) conditional(s32[]{:T(128)} %convert_element_type.7, (s32[2]{0:T(128)S(1)}, s32[2]{0:T(128)S(1)}, f32[2,4,4,48,768]{4,3,2,1,0:T(8,128)}, f32[2,4,4,48,768]{4,3,2,1,0:T(8,128)}, f32[8,2,8,128]{3,2,1,0:T(8,128)S(1)}) %tuple.15, (s32[2]{0:T(128)S(1)}, ...), branch_computations={%region_0.2_spmd, %region_2.3_spmd} | conditional | flops 16 | bytes 16416 | solution.py:940
  154.0 1.0 copy.27
  155.0 0.7 slice_bitcast_fusion
  155.7 9.8 %branch_1_fun.1 = f32[2,4,4,48,768]{4,3,2,1,0:T(8,128)} custom-call(s32[2]{0:T(128)S(1)} %get-tuple-element.29.inside_ref, s32[2]{0:T(128)S(1)} %get-tuple-element.30.near_ref, f32[2,4,4,48,512]{4,3,2,1,0:T(8,128)S(1)} %get-tuple-element.31.own_ref, f32[2,4,4,48,512]{4,3,2,1,0:T(8,128)} %get-tuple-element.32.far_ref, ...), custom_call_target="tpu_custom_call" | custom-call | tf_op jit(solution)/shard_map/cond/branch_1_fun/pallas_call | solution.py:703
  165.5 0.0 copy-start.4
  165.5 0.5 copy-done.4
  (2 shorter events, 0.0 us)
Async XLA Ops:
  0.6 56.1 %copy-start = (bf16[512,768]{1,0:T(8,128)(2,1)S(1)}, bf16[512,768]{1,0:T(8,128)(2,1)}, u32[]{:S(2)}) copy-start(bf16[512,768]{1,0:T(8,128)(2,1)} %constant.113.clone.gl) | copy-start | bytes 2359300
  0.6 56.0 %copy-start.1 = (bf16[512,768]{1,0:T(8,128)(2,1)S(1)}, bf16[512,768]{1,0:T(8,128)(2,1)}, u32[]{:S(2)}) copy-start(bf16[512,768]{1,0:T(8,128)(2,1)} %constant.112.clone.gh) | copy-start | bytes 2359300
  0.7 54.1 %copy-start.3 = (f32[1,4]{1,0:T(1,128)S(1)}, f32[1,4]{1,0:T(1,128)}, u32[]{:S(2)}) copy-start(f32[1,4]{1,0:T(1,128)} %rate_any.1) | copy-start | bytes 52
  0.7 55.3 %copy-start.2 = (f32[1,4,4]{2,1,0:T(4,128)S(1)}, f32[1,4,4]{2,1,0:T(4,128)}, u32[]{:S(2)}) copy-start(f32[1,4,4]{2,1,0:T(4,128)} %param.24) | copy-start | bytes 196
  165.5 0.5 copy-start.4
